TPU v7x, 32 devices: a whole 2x2x4 slice. The times are simulated.
32 devices in a mesh: dp: 4 (over y, core), seq: 8 (over z, x).
Axes of the slice: x: 2, y: 2, z: 4, core: 2. Of those that a mesh axis runs over, the one named last changes fastest.
Arguments:
- tokens: bfloat16 [4, 2048, 1024], P('dp', 'seq'), may hold values from -6 to 6
- w_qkv: bfloat16 [1024, 3072], P('seq'), may hold values from -0.25 to 0.25
- w_out: bfloat16 [1024, 1024], P('seq'), may hold values from -3 to 3
- w_up: bfloat16 [1024, 4096], P('seq'), may hold values from -0.1875 to 0.1875
- w_down: bfloat16 [4096, 1024], P('seq'), may hold values from -0.09375 to 0.09375
- g_attn: bfloat16 [1024], P('seq'), may hold values from 0.5 to 1.5
- g_mlp: bfloat16 [1024], P('seq'), may hold values from 0.5 to 1.5
- ssm_rate: bfloat16 [1024, 16], P('seq'), may hold values from 2.4318695e-05 to 0.049804688
- ssm_in: bfloat16 [1024, 16], P('seq'), may hold values from -0.29882812 to 0.29882812
- ssm_out: bfloat16 [1024, 16], P('seq'), may hold values from -1.5 to 1.5
- h_init: float32 [4, 1024, 16], P('dp'), may hold values from -4 to 4
- cotangent: bfloat16 [4, 2048, 1024], P('dp', 'seq'), may hold values from -6 to 6
- d_h_ends: float32 [4, 8, 1024, 16], P('dp', 'seq'), may hold values from -6 to 6
Outputs:
- result: bfloat16 [4, 2048, 1024], P('dp', 'seq')
- d_tokens: bfloat16 [4, 2048, 1024], P('dp', 'seq')
- d_w_qkv: float32 [1024, 3072], P('seq')
- d_w_out: float32 [1024, 1024], P('seq')
- d_w_up: float32 [1024, 4096], P('seq')
- d_w_down: float32 [4096, 1024], P('seq')
- d_g_attn: float32 [1024], P('seq')
- d_g_mlp: float32 [1024], P('seq')
- d_ssm_rate: float32 [1024, 16], P('seq')
- d_ssm_in: float32 [1024, 16], P('seq')
- d_ssm_out: float32 [1024, 16], P('seq')
- d_h_init: float32 [4, 1024, 16], P('dp', 'seq')
- h_ends: float32 [4, 8, 1024, 16], P('dp', 'seq')
All inputs are finite; a program needn't handle non-finite values.
Results may differ from a plain program's by a relative error of at most 0.019.
Values may be sent and summed in bfloat16 or wider, within the bound.
No kernel may reach another device: no remote copies, remote signals or barrier semaphores. Data moves between devices by JAX's collectives and lax.ppermute only.
A program may use at most 256 MiB of HBM per device.

v0:
```python
import functools
import math

import jax
import jax.numpy as jnp
from jax import lax
from jax.experimental import pallas as pl
from jax.experimental.pallas import tpu as pltpu
from jax.sharding import PartitionSpec as P

HEADS = 8
HD = 128
CTX = 128
NST = 16
LANES = 128
GROUP = 4
TEAM = 4

epsilon = 1e-05
far_below = -1e30
bf16 = jnp.bfloat16
f32 = jnp.float32


def swap(a, axis, bit):
    return lax.ppermute(a, axis, [(k, k ^ bit) for k in range(lax.axis_size(axis))])


def swap_team(a, r):
    if r == 1:
        return swap(a, "dp", 1)
    if r == 2:
        return swap(a, "seq", 1)
    nd, ns = lax.axis_size("dp"), lax.axis_size("seq")
    pairs = [(d * ns + k, (d ^ 1) * ns + (k ^ 1)) for d in range(nd) for k in range(ns)]
    return lax.ppermute(a, ("dp", "seq"), pairs)


def gather_team(a):
    far = swap_team(a, 2)
    return [a, swap_team(a, 1), far, swap_team(far, 1)]


def far_kernel(mine, came, out):
    out[...] = (mine[...] + came[...].astype(f32)).astype(bf16)


def sum_team(parts, middle=None, end=None):
    one, three = swap_team(parts[1], 1), swap_team(parts[3], 1)
    if middle is not None:
        three = after(three, middle)
    shape = jax.ShapeDtypeStruct(three.shape, bf16)
    near = call(far_kernel, "far_sum", shape, (parts[2], three), 0)
    far = swap_team(near, 2)
    if end is not None:
        one, far = after((one, far), end)
    return parts[0], one, far, near


def trade_team(parts):
    return [parts[0]] + [swap_team(parts[r], r) for r in (1, 2, 3)]


def high_bits(axis):
    size = lax.axis_size(axis)
    return [1 << k for k in reversed(range(1, size.bit_length() - 1))]


def pick(a, index, axis=0):
    return lax.dynamic_index_in_dim(a, index, axis, False)


def ordered(blocks, index):
    bit = len(blocks) // 2
    while bit:
        flip = (index & bit) != 0
        blocks = [jnp.where(flip, blocks[r ^ bit], blocks[r]) for r in range(len(blocks))]
        bit //= 2
    return blocks


def after(x, *others):
    return lax.optimization_barrier((x, others))[0]


def whole_spec():
    return pl.BlockSpec(memory_space=pltpu.VMEM)


def scalar_spec():
    return pl.BlockSpec(memory_space=pltpu.SMEM)


def any_spec():
    return pl.BlockSpec(memory_space=pl.ANY)


BIG = pltpu.CompilerParams(vmem_limit_bytes=32 * 2**20)
MIDDLE = pltpu.CompilerParams(vmem_limit_bytes=24 * 2**20)
SMALL = pltpu.CompilerParams(vmem_limit_bytes=20 * 2**20)


def block_of(shape):
    return pl.BlockSpec(shape, lambda *k: (0,) * len(shape), pipeline_mode=pl.Buffered(1))


def call(kernel, name, out_shape, args, scalars=1, **more):
    specs = [scalar_spec()] * scalars + [block_of(a.shape) for a in args[scalars:]]
    return pl.pallas_call(
        kernel,
        grid=(1,),
        out_shape=out_shape,
        in_specs=specs,
        out_specs=jax.tree.map(lambda o: block_of(o.shape), out_shape),
        compiler_params=MIDDLE,
        name=name,
        **more,
    )(*args)


def share_kernel(spots, copies, idx, *refs):
    ins, outs, sem = refs[:spots], refs[spots:-1], refs[-1]
    flying = []
    for n, (src, dst, rows_at, cols_at, size, to) in enumerate(copies):
        row = pl.multiple_of(rows_at(idx), 16)
        col = pl.multiple_of(cols_at(idx), LANES)
        flying.append(
            pltpu.make_async_copy(
                ins[src].at[pl.ds(row, size[0]), pl.ds(col, size[1])],
                outs[dst].at[:, pl.ds(to, size[1])],
                sem.at[n],
            )
        )
    for one in flying:
        one.start()
    for one in flying:
        one.wait()


def shares(idx, w_qkv, w_out, w_up, w_down, ny, ns):
    shard, dim = w_out.shape
    quarter = dim // TEAM
    rows, fb = shard // ny, w_down.shape[0] // TEAM
    copies = []
    for away in (0, 1):
        def who(i, away=away):
            return i[0] ^ (2 * away)

        for part in range(3):
            copies.append((0, away, lambda i: i[1] * rows,
                           lambda i, w=who, p=part: p * dim + w(i) * quarter, (rows, quarter), part * quarter))
        copies.append((1, away, lambda i: i[1] * rows,
                       lambda i, w=who: w(i) * quarter, (rows, quarter), 3 * quarter))
        if fb % LANES == 0:
            for k in range(ns):
                copies.append((2, 2 + away, lambda i: i[1] * rows,
                               lambda i, w=who, k=k: (k * TEAM + w(i)) * fb, (rows, fb), k * fb))
        for h in (0, 1):
            copies.append((3, 4 + 2 * h + away, lambda i, w=who, h=h: w(i) * fb + h * (fb // 2),
                           lambda i: 0, (fb // 2, dim), 0))
    sizes = [(rows, dim)] * 2 + [(rows, ns * fb)] * 2 + [(fb // 2, dim)] * 4
    out = pl.pallas_call(
        functools.partial(share_kernel, 4, copies),
        out_shape=[jax.ShapeDtypeStruct(s, bf16) for s in sizes],
        in_specs=[scalar_spec()] + [any_spec()] * 4,
        out_specs=[whole_spec()] * 8,
        scratch_shapes=[pltpu.SemaphoreType.DMA((len(copies),))],
        name="shares",
    )(idx, w_qkv, w_out, w_up, w_down)
    out = [list(out[k : k + 2]) for k in (0, 2, 4, 6)]
    if fb % LANES:
        mine = lax.dynamic_slice_in_dim(w_up, idx[1] * rows, rows, 0).reshape(rows, ns, TEAM, fb)
        out[1] = [pick(mine, idx[0] ^ r, 2).reshape(rows, ns * fb) for r in (0, 2)]
    return out


def place_kernel(maps, cuts, idx, places, *refs):
    ins, outs = refs[: len(maps)], refs[len(maps) :]
    for ref, (which, order, step, offset) in zip(ins, maps):
        rows = ref.shape[1]
        for k, r in enumerate(order):
            at = pl.multiple_of(((places[which] ^ r) * step + offset) * rows, 16)
            if cuts:
                width = outs[0].shape[1]
                outs[0][pl.ds(at, rows), :] = ref[k, :, :width]
                outs[-1][pl.ds(at, rows), :] = ref[k, :, width:]
            else:
                outs[0][pl.ds(at, rows), :] = ref[k]
    for r in range(cuts):
        rows = outs[1].shape[0]
        at = pl.multiple_of((idx[0] ^ r) * rows, 16)
        outs[1 + r][...] = outs[-1][pl.ds(at, rows), :]


def append_kernel(a_ref, b_ref, out):
    count = a_ref.shape[0]
    out[:count] = a_ref[...]
    out[count:] = b_ref[...]


def append(a, b):
    shape = jax.ShapeDtypeStruct((a.shape[0] + b.shape[0],) + a.shape[1:], bf16)
    return call(append_kernel, "append", shape, (a, b), 0)


class Gathering:
    def __init__(self, own, away, parted):
        ny = lax.axis_size("dp") // 2 if parted else 1
        self.seq_steps = [(1, ny)] + [(bit, bit * ny) for bit in high_bits("seq")]
        self.a, self.away, self.order, self.n = own[None], away[None], [0], 0

    def step(self, wait=None):
        bit, weight = self.seq_steps[self.n]
        if self.n:
            self.a = append(self.a, self.came)
            self.order = self.order + [r | self.seq_steps[self.n - 1][1] for r in self.order]
        sent = self.a if self.n else self.away
        self.came = swap(sent if wait is None else after(sent, wait), "seq", bit)
        self.n += 1
        if self.n == len(self.seq_steps):
            last = [r | weight for r in self.order]
            self.pieces = [(self.a, self.order), (self.came, last)]
        return self.came

    def rest(self, wait=None):
        while self.n < len(self.seq_steps) - 1:
            self.step(wait)
            wait = None
        return self.came

    def across(self, k, wait=None):
        new = [self.pieces[k]]
        for bit in high_bits("dp"):
            for a, order in list(new):
                a = a if wait is None else after(a, wait)
                new.append((swap(a, "dp", bit), [r | (bit // 2) for r in order]))
        self.pieces += new[1:]
        return new[1][0]


def place_weight(idx, places, groups, width=None):
    arrays = [a for pieces, *_ in groups for a, _ in pieces]
    maps = [(which, order, step, at) for pieces, which, step, at in groups for _, order in pieces]
    rows, cols = sum(a.shape[0] * a.shape[1] for a in arrays), arrays[0].shape[2]
    shapes = [(rows, cols)]
    scratch = []
    if width:
        shapes = [(rows, width)] + [(rows // TEAM, cols - width)] * TEAM
        scratch = [pltpu.VMEM((rows, cols - width), bf16)]
    return call(
        functools.partial(place_kernel, maps, TEAM if width else 0),
        "place_weight",
        [jax.ShapeDtypeStruct(s, bf16) for s in shapes],
        (idx, places, *arrays),
        2,
        scratch_shapes=scratch,
    )


def attn_grad_kernel(idx, x_ref, dq_ref, ctx_ref, dctx_ref, *refs):
    parts, out = refs[:TEAM], refs[TEAM]
    k = pl.program_id(0)
    width = dq_ref.shape[1] // 3
    grad = dot_tn(x_ref[...], dq_ref[...])
    far = dot_tn(ctx_ref[...], dctx_ref[...])
    out[:, :width] = grad[:, :width].astype(bf16)
    out[:, width : 3 * width] = (grad[:, width:] + far).astype(bf16)
    per = parts[0].shape[0] // out.shape[0]
    member = (k // per) ^ idx[0]
    at = pl.multiple_of((k % per) * out.shape[0], 16)
    for r in range(TEAM):
        @pl.when(member == r)
        def _(r=r):
            out[:, 3 * width :] = parts[r][pl.ds(at, out.shape[0]), :]


def attn_grad(idx, inputs, d_qkv, context, d_ctx_kv, parts):
    dim, step = inputs.shape[1], LANES
    return pl.pallas_call(
        attn_grad_kernel,
        grid=(dim // step,),
        out_shape=jax.ShapeDtypeStruct((dim, d_qkv.shape[1] + parts[0].shape[1]), bf16),
        in_specs=[
            scalar_spec(),
            pl.BlockSpec((inputs.shape[0], step), lambda k: (0, k)),
            block_of(d_qkv.shape),
            pl.BlockSpec((context.shape[0], step), lambda k: (0, k)),
            block_of(d_ctx_kv.shape),
        ]
        + [block_of(p.shape) for p in parts],
        out_specs=pl.BlockSpec((step, d_qkv.shape[1] + parts[0].shape[1]), lambda k: (k, 0)),
        compiler_params=SMALL,
        name="attn_grad",
    )(idx, inputs, d_qkv, context, d_ctx_kv, *parts)


def insert_bit(k, at, bit):
    return ((k >> at) << (at + 1)) | (bit << at) | (k & ((1 << at) - 1))


def split_kernel(before, side, at, place, x_ref, *refs):
    here = (place[0] >> side) & 1
    if before is None:
        (away_ref,) = refs
        for k in range(away_ref.shape[0]):
            away_ref[k] = x_ref[insert_bit(k, at, 1 - here)]
        return
    recv_ref, keep_ref, away_ref = refs

    def total(k):
        j = k if before is True else insert_bit(k, before[1], (place[0] >> before[0]) & 1)
        return (x_ref[j].astype(f32) + recv_ref[k].astype(f32)).astype(bf16)

    for k in range(away_ref.shape[0]):
        away_ref[k] = total(insert_bit(k, at, 1 - here))
        keep_ref[k] = total(insert_bit(k, at, here))


class Reduction:
    def __init__(self, x, place):
        ny = lax.axis_size("dp") // 2
        ns = lax.axis_size("seq")
        y_bits = ny.bit_length() - 1
        steps = [("dp", bit, (bit // 2).bit_length() - 1, 0) for bit in reversed(high_bits("dp"))]
        steps += [("seq", b, (b * ny).bit_length() - 1, 1) for b in reversed(high_bits("seq"))]
        self.steps = steps + [("seq", 1, y_bits, 0)]
        self.place, self.n, self.came = place, 0, None
        self.kept = x.reshape(ns * ny, -1, x.shape[1])

    def step(self, wait=None):
        n, x, recv = self.n, self.kept, self.came
        axis, bit, side, at = self.steps[n]
        if n == 0 and wait is not None:
            x = after(x, wait)
        elif wait is not None:
            recv = after(recv, wait)
        before = None if n == 0 else (self.steps[0][2:] if n == 1 else True)
        count = x.shape[0] // 2 if n == 0 else recv.shape[0] // 2
        half = jax.ShapeDtypeStruct((count,) + x.shape[1:], bf16)
        out = call(
            functools.partial(split_kernel, before, side, at),
            "split_sum",
            [half] if n == 0 else [half, half],
            (self.place, x) if n == 0 else (self.place, x, recv),
        )
        if n:
            self.kept = out[0]
        self.sent = out[-1]
        self.came = swap(self.sent, axis, bit)
        self.n += 1
        return self.sent

    def last(self, wait=None):
        while self.n < len(self.steps):
            self.step(wait)
            wait = None
        return self.kept, self.came


def halves_kernel(place, x_ref, out_ref, in_ref):
    y, z = place[0] & 1, (place[0] >> 2) & 1
    for k in range(out_ref.shape[0]):
        low = ((k >> 1) << 3) | ((k & 1) << 1) | (1 - y)
        out_ref[k] = x_ref[low | ((1 - z) << 2)]
        in_ref[k] = x_ref[low | (z << 2)]


def leave_kernel(place, x_ref, came_ref, out_ref):
    y, z = place[0] & 1, (place[0] >> 2) & 1
    for k in range(out_ref.shape[0]):
        mine = x_ref[((k >> 1) << 3) | ((1 - z) << 2) | ((k & 1) << 1) | y]
        out_ref[k] = (mine.astype(f32) + came_ref[k].astype(f32)).astype(bf16)


def stay_kernel(place, x_ref, came_ref, near_ref, keep_ref, out_ref):
    y, z, far = place[0] & 1, (place[0] >> 2) & 1, (place[0] >> 3) & 1

    def total(k):
        mine = x_ref[((k >> 1) << 3) | (z << 2) | ((k & 1) << 1) | y]
        return (mine.astype(f32) + came_ref[k].astype(f32) + near_ref[k].astype(f32)).astype(bf16)

    for k in (0, 1):
        keep_ref[k] = total((far << 1) | k)
        out_ref[k] = total(((1 - far) << 1) | k)


class HalvedReduction(Reduction):
    def step(self, wait=None):
        n = self.n
        if n > 2:
            self.steps = [None, None, None, ("seq", 1, 1, 0)]
            return super().step(wait)
        x = self.kept
        four = jax.ShapeDtypeStruct((x.shape[0] // 4,) + x.shape[1:], bf16)
        two = jax.ShapeDtypeStruct((2,) + x.shape[1:], bf16)
        if n == 0:
            x = x if wait is None else after(x, wait)
            out, stay = call(halves_kernel, "halves", (four, four), (self.place, x))
            self.sent = out
            self.out, self.stay = swap(out, "dp", 2), swap(stay, "dp", 2)
        elif n == 1:
            came = self.out if wait is None else after(self.out, wait)
            self.sent = call(leave_kernel, "leave_sum", four, (self.place, x, came))
            self.near = swap(self.sent, "seq", 2)
        else:
            came = self.near if wait is None else after(self.near, wait)
            args = (self.place, x, self.stay, came)
            self.kept, self.sent = call(stay_kernel, "stay_sum", (two, two), args)
            self.came = swap(self.sent, "seq", 4)
        self.n += 1
        return self.sent


def final_kernel(kind, fb, idx, mine_ref, other_ref, *outs):
    count, rows, width = mine_ref.shape
    for k in range(count):
        row = pl.multiple_of((idx[1] ^ (k // 2)) * rows, 16)
        for core, ref in enumerate((mine_ref, other_ref)):
            member = idx[0] ^ (2 * (k % 2) + core)
            if kind == "down":
                at = pl.multiple_of(member * (rows * count // 2) + row, 16)
                outs[0][pl.ds(at, rows), :] = ref[k].astype(f32)
            elif kind == "up":
                for n in range(width // fb):
                    col = pl.multiple_of((n * TEAM + member) * fb, LANES)
                    block = ref[k, :, n * fb : (n + 1) * fb]
                    outs[0][pl.ds(row, rows), pl.ds(col, fb)] = block.astype(f32)
            else:
                dim = outs[1].shape[1]
                quarter = dim // TEAM
                for part in range(4):
                    to = outs[0] if part < 3 else outs[1]
                    col = pl.multiple_of((part % 3) * dim * (part < 3) + member * quarter, LANES)
                    block = ref[k, :, part * quarter : (part + 1) * quarter]
                    to[pl.ds(row, rows), pl.ds(col, quarter)] = block.astype(f32)


def spread(own, near):
    blocks = {0: append(own, near)}
    for bit in high_bits("dp"):
        for m in list(blocks):
            blocks[m | (bit // 2)] = swap(blocks[m], "dp", bit)
    blocks = [blocks[m] for m in range(len(blocks))]
    while len(blocks) > 1:
        blocks = [append(a, b) for a, b in zip(blocks[0::2], blocks[1::2])]
    return blocks[0], swap(blocks[0], "dp", 1)


def spread_weight(kind, pair, idx, shapes, fb=LANES):
    return call(
        functools.partial(final_kernel, kind, fb),
        "final_" + kind,
        [jax.ShapeDtypeStruct(s, f32) for s in shapes],
        (idx, *spread(*pair)),
    )


def spread_narrow(pair, idx, shape, fb):
    mine, other = spread(*pair)
    teams = [mine[0::2], other[0::2], mine[1::2], other[1::2]]
    teams = jnp.stack(ordered(teams, idx[0]))
    rows = jnp.stack(ordered([teams[:, m] for m in range(teams.shape[1])], idx[1]), axis=1)
    rows = rows.reshape(TEAM, shape[0], shape[1] // (TEAM * fb), fb).transpose(1, 2, 0, 3)
    return rows.reshape(shape).astype(f32)


def ends_kernel(mid, u_ref, a_ref, mid_ref, end_ref):
    rows = u_ref.shape[0]
    a = [a_ref[n] for n in range(NST)]

    def eight(k, s):
        for t in range(8):
            u = u_ref[k * 8 + t]
            s = tuple(a[n] * s[n] + u for n in range(NST))
        return s

    zero = tuple(jnp.zeros_like(a[0]) for _ in range(NST))
    s = lax.fori_loop(0, mid // 8, eight, zero)
    for n in range(NST):
        mid_ref[n] = s[n]
    s = lax.fori_loop(mid // 8, rows // 8, eight, s)
    for n in range(NST):
        end_ref[n] = s[n]


def local_ends(u, a):
    shape = jax.ShapeDtypeStruct(a.shape, f32)
    kernel = functools.partial(ends_kernel, u.shape[0] - CTX)
    return call(kernel, "ssm_ends", (shape, shape), (u, a), 0)


def context_kernel(mid, late, u_ref, a_ref, gin_ref, gout_ref, h_ref, first_ref, second_ref, y_ref):
    half = NST // 2
    for base in (0, half):
        ns = range(base, base + half)
        a = [a_ref[n] for n in ns]
        gin = [gin_ref[n] for n in ns]
        gout = [gout_ref[n] for n in ns]

        def step(k, h):
            for t in range(4):
                p = k * 4 + t
                u = u_ref[mid + p]
                h = tuple(a[n] * h[n] + gin[n] * u for n in range(half))
                y = functools.reduce(jnp.add, [gout[n] * h[n] for n in range(half)])
                y_ref[p] = y if base == 0 else y_ref[p] + y
            return h

        lax.fori_loop(0, CTX // 4, step, tuple(h_ref[n] for n in ns))
    per = y_ref.shape[1] // TEAM
    for w in range(2):
        for c in range(per):
            own, other = y_ref[:, w * per + c, :], y_ref[:, (2 + w) * per + c, :]
            at = (slice(w * CTX, (w + 1) * CTX), slice(c * LANES, (c + 1) * LANES))
            first_ref[at] = jnp.where(late[0] == 1, other, own).astype(bf16)
            second_ref[at] = jnp.where(late[0] == 1, own, other).astype(bf16)


def contexts(half, u, a, gin, gout, h_mid):
    shape = jax.ShapeDtypeStruct((2 * CTX, u.shape[1] * LANES // TEAM), bf16)
    return call(
        functools.partial(context_kernel, u.shape[0] - CTX),
        "ssm_context",
        (shape, shape),
        (half, u, a, gin, gout, h_mid),
        scratch_shapes=[pltpu.VMEM((CTX,) + u.shape[1:], f32)],
    )


def tail_kernel(dy_ref, a_ref, gout_ref, lam_ref):
    half = dy_ref.shape[1]
    a = [a_ref[n, :half] for n in range(NST)]
    gout = [gout_ref[n, :half] for n in range(NST)]

    def eight(k, lam):
        for t in range(8):
            dy = dy_ref[CTX - 1 - (k * 8 + t)]
            lam = tuple(a[n] * lam[n] + gout[n] * dy for n in range(NST))
        return lam

    lam = lax.fori_loop(0, CTX // 8, eight, tuple(jnp.zeros_like(a[0]) for _ in range(NST)))
    for n in range(NST):
        lam_ref[n] = lam[n]


def tail_adjoint(dy, a, gout):
    shape = jax.ShapeDtypeStruct((NST,) + dy.shape[1:], f32)
    return call(tail_kernel, "ssm_tail", shape, (dy, a, gout), 0)


def first_context_kernel(dy0_ref, a_ref, gout_ref, init_ref, da_ref, dgout_ref, g0_ref, hs):
    ns = range(GROUP)
    a = [a_ref[n] for n in ns]
    gout = [gout_ref[n] for n in ns]
    zero = tuple(jnp.zeros_like(a[0]) for _ in ns)

    def ahead(k, h):
        for t in range(8):
            h = tuple(a[n] * h[n] for n in ns)
            for n in ns:
                hs[k * 8 + t + 1, n] = h[n]
        return h

    h = tuple(init_ref[n] for n in ns)
    for n in ns:
        hs[0, n] = h[n]
    lax.fori_loop(0, CTX // 8, ahead, h)

    def back(k, carry):
        mu, da, dgout = carry
        for t in range(4):
            q = CTX - 1 - (k * 4 + t)
            dy = dy0_ref[q]
            mu = tuple(mu[n] + gout[n] * dy for n in ns)
            dgout = tuple(dgout[n] + dy * hs[q + 1, n] for n in ns)
            da = tuple(da[n] + mu[n] * hs[q, n] for n in ns)
            mu = tuple(a[n] * mu[n] for n in ns)
        return mu, da, dgout

    mu, da, dgout = lax.fori_loop(0, CTX // 4, back, (zero, zero, zero))
    for n in ns:
        g0_ref[n] = mu[n]
        da_ref[n] = da[n]
        dgout_ref[n] = dgout[n]


def first_context_back(dy0, a, gout, h_init):
    tile = dy0.shape[1:]
    states = pl.BlockSpec((GROUP,) + tile, lambda g: (g, 0, 0))
    return pl.pallas_call(
        first_context_kernel,
        grid=(NST // GROUP,),
        out_shape=(jax.ShapeDtypeStruct(a.shape, f32),) * 3,
        in_specs=[pl.BlockSpec(dy0.shape, lambda g: (0, 0, 0))] + [states] * 3,
        out_specs=(states,) * 3,
        scratch_shapes=[pltpu.VMEM((CTX + 1, GROUP) + tile, f32)],
        name="first_context",
    )(dy0, a, gout, h_init)


def back_kernel(
    u_ref, dy_ref, a_ref, gin_ref, gout_ref, h_ref, lam_ref, da0_ref, dgout0_ref,
    du_ref, dgin_ref, da_ref, dgout_ref, g_ref, hs,
):
    first = pl.program_id(0) == 0
    rows = u_ref.shape[0]
    mid = rows - CTX
    ns = range(GROUP)
    a = [a_ref[n] for n in ns]
    gin = [gin_ref[n] for n in ns]
    gout = [gout_ref[n] for n in ns]
    zero = tuple(jnp.zeros_like(a[0]) for _ in ns)

    def ahead(k, h):
        for t in range(8):
            p = k * 8 + t
            u = u_ref[p]
            h = tuple(a[n] * h[n] + gin[n] * u for n in ns)
            for n in ns:
                hs[p + 1, n] = h[n]
        return h

    h = tuple(h_ref[n] for n in ns)
    for n in ns:
        hs[0, n] = h[n]
    lax.fori_loop(0, rows // 8, ahead, h)

    def tail(k, carry):
        lam, dgin, da, dgout = carry
        for t in range(4):
            q = CTX - 1 - (k * 4 + t)
            p = mid + q
            dy, u = dy_ref[q], u_ref[p]
            lam = tuple(lam[n] + gout[n] * dy for n in ns)
            dgout = tuple(dgout[n] + dy * hs[p + 1, n] for n in ns)
            dgin = tuple(dgin[n] + lam[n] * u for n in ns)
            da = tuple(da[n] + lam[n] * hs[p, n] for n in ns)
            du = functools.reduce(jnp.add, [gin[n] * lam[n] for n in ns])
            du_ref[p] = jnp.where(first, du, du_ref[p] + du)
            lam = tuple(a[n] * lam[n] for n in ns)
        return lam, dgin, da, dgout

    def head(k, carry):
        lam, dgin, da = carry
        for t in range(4):
            p = mid - 1 - (k * 4 + t)
            u = u_ref[p]
            dgin = tuple(dgin[n] + lam[n] * u for n in ns)
            da = tuple(da[n] + lam[n] * hs[p, n] for n in ns)
            du = functools.reduce(jnp.add, [gin[n] * lam[n] for n in ns])
            du_ref[p] = jnp.where(first, du, du_ref[p] + du)
            lam = tuple(a[n] * lam[n] for n in ns)
        return lam, dgin, da

    lam = tuple(lam_ref[n] for n in ns)
    da0, dgout0 = tuple(da0_ref[n] for n in ns), tuple(dgout0_ref[n] for n in ns)
    lam, dgin, da, dgout = lax.fori_loop(0, CTX // 4, tail, (lam, zero, da0, dgout0))
    lam, dgin, da = lax.fori_loop(0, mid // 4, head, (lam, dgin, da))
    for n in ns:
        g_ref[n] = lam[n]
        dgin_ref[n] = dgin[n]
        da_ref[n] = da[n]
        dgout_ref[n] = dgout[n]


def ssm_back(u, dy, a, gin, gout, state_in, lam_end, da0, dgout0):
    tile = u.shape[1:]
    states = pl.BlockSpec((GROUP,) + tile, lambda g: (g, 0, 0))
    rows = pl.BlockSpec(u.shape, lambda g: (0, 0, 0))
    tail = pl.BlockSpec(dy.shape, lambda g: (0, 0, 0))
    out = jax.ShapeDtypeStruct(a.shape, f32)
    return pl.pallas_call(
        back_kernel,
        grid=(NST // GROUP,),
        out_shape=(jax.ShapeDtypeStruct(u.shape, f32),) + (out,) * 4,
        in_specs=[rows, tail] + [states] * 7,
        out_specs=(rows,) + (states,) * 4,
        scratch_shapes=[pltpu.VMEM((u.shape[0] + 1, GROUP) + tile, f32)],
        compiler_params=SMALL,
        name="ssm_back",
    )(u, dy, a, gin, gout, state_in, lam_end, da0, dgout0)


def dot_nt(x, y):
    return lax.dot_general(x, y, (((1,), (1,)), ((), ())), preferred_element_type=f32)


def dot_nn(x, y):
    return jnp.dot(x, y, preferred_element_type=f32)


def dot_tn(x, y):
    return lax.dot_general(x, y, (((0,), (0,)), ((), ())), preferred_element_type=f32)


def softmax_parts(q, keys):
    rows = q.shape[0]
    scores = [dot_nt(q, k) * (1.0 / math.sqrt(HD)) for k in keys]
    at = lax.broadcasted_iota(jnp.int32, (rows, rows), 0)
    to = lax.broadcasted_iota(jnp.int32, (rows, rows), 1)
    scores[-1] = jnp.where(to <= at, scores[-1], far_below)
    top = functools.reduce(jnp.maximum, [jnp.max(s, axis=-1, keepdims=True) for s in scores])
    es = [jnp.exp(s - top) for s in scores]
    total = functools.reduce(jnp.add, [jnp.sum(e, axis=-1, keepdims=True) for e in es])
    return [e / total for e in es]


def attend_kernel(half_ref, q0, q1, k0, k1, v0, v1, kc, vc, out_ref):
    w, h = pl.program_id(0), pl.program_id(1)
    rows = q0.shape[0]
    for half, q, keys, values in ((0, q0, (kc, k0), (vc, v0)), (1, q1, (kc, k0, k1), (vc, v0, v1))):
        probs = softmax_parts(q[...], [k[...] for k in keys])
        out = [dot_nn(p.astype(bf16), v[...]) for p, v in zip(probs, values)]
        at = pl.multiple_of(((half ^ half_ref[0]) * 2 + w) * rows, 16)
        col = pl.multiple_of(h * HD, LANES)
        out_ref[pl.ds(at, rows), pl.ds(col, HD)] = functools.reduce(jnp.add, out).astype(bf16)


def attend_back_kernel(
    half_ref, q0, q1, k0, k1, v0, v1, kc, vc, do0, do1, dqkv_ref, dctx_ref
):
    w, h = pl.program_id(0), pl.program_id(1)
    rows, heads = q0.shape[0], pl.num_programs(1)
    scale = 1.0 / math.sqrt(HD)
    dk, dv = [0.0, 0.0, 0.0], [0.0, 0.0, 0.0]

    def row_of(half):
        return pl.multiple_of(((half ^ half_ref[0]) * 2 + w) * rows, 16)

    def col_of(part):
        return pl.multiple_of((part * heads + h) * HD, LANES)

    cases = ((0, q0, do0, (kc, k0), (vc, v0)), (1, q1, do1, (kc, k0, k1), (vc, v0, v1)))
    for half, q, do, keys, values in cases:
        query, d_out = q[...], do[...]
        probs = softmax_parts(query, [k[...] for k in keys])
        d_probs = [dot_nt(d_out, v[...]) for v in values]
        sums = [jnp.sum(p * d, axis=-1, keepdims=True) for p, d in zip(probs, d_probs)]
        delta = functools.reduce(jnp.add, sums)
        d_scores = [(p * (d - delta)).astype(bf16) for p, d in zip(probs, d_probs)]
        dq = functools.reduce(jnp.add, [dot_nn(d, k[...]) for d, k in zip(d_scores, keys)])
        dqkv_ref[pl.ds(row_of(half), rows), pl.ds(col_of(0), HD)] = (dq * scale).astype(bf16)
        for n, (d, p) in enumerate(zip(d_scores, probs)):
            dk[n] = dk[n] + dot_tn(d, query)
            dv[n] = dv[n] + dot_tn(p.astype(bf16), d_out)
    ctx_row = pl.multiple_of(w * CTX, 16)
    dctx_ref[pl.ds(ctx_row, CTX), pl.ds(col_of(0), HD)] = (dk[0] * scale).astype(bf16)
    dctx_ref[pl.ds(ctx_row, CTX), pl.ds(col_of(1), HD)] = dv[0].astype(bf16)
    for half in (0, 1):
        dqkv_ref[pl.ds(row_of(half), rows), pl.ds(col_of(1), HD)] = (dk[1 + half] * scale).astype(bf16)
        dqkv_ref[pl.ds(row_of(half), rows), pl.ds(col_of(2), HD)] = dv[1 + half].astype(bf16)


def attention_specs(rows, heads):
    def at(half, part):
        return pl.BlockSpec((rows, HD), lambda w, h, s: ((half ^ s[0]) * 2 + w, part * heads + h))

    def ctx(part):
        return pl.BlockSpec((CTX, HD), lambda w, h, s: (w, part * heads + h))

    return [at(half, part) for part in range(3) for half in (0, 1)] + [ctx(0), ctx(1)]


def whole_block(shape):
    return pl.BlockSpec(shape, lambda w, h, s: (0, 0))


def attend(half, qkv, ctx_kv):
    rows, heads = qkv.shape[0] // TEAM, qkv.shape[1] // (3 * HD)
    out = (qkv.shape[0], heads * HD)
    return pl.pallas_call(
        attend_kernel,
        grid_spec=pltpu.PrefetchScalarGridSpec(
            num_scalar_prefetch=1,
            grid=(2, heads),
            in_specs=attention_specs(rows, heads),
            out_specs=whole_block(out),
        ),
        out_shape=jax.ShapeDtypeStruct(out, bf16),
        compiler_params=SMALL,
        name="attend",
    )(half, *[qkv] * 6, ctx_kv, ctx_kv)


def attend_back(half, qkv, ctx_kv, d_attended):
    rows, heads = qkv.shape[0] // TEAM, qkv.shape[1] // (3 * HD)

    def at(side):
        return pl.BlockSpec((rows, HD), lambda w, h, s: ((side ^ s[0]) * 2 + w, h))

    return pl.pallas_call(
        attend_back_kernel,
        grid_spec=pltpu.PrefetchScalarGridSpec(
            num_scalar_prefetch=1,
            grid=(2, heads),
            in_specs=attention_specs(rows, heads) + [at(0), at(1)],
            out_specs=[whole_block(qkv.shape), whole_block(ctx_kv.shape)],
        ),
        out_shape=[jax.ShapeDtypeStruct(qkv.shape, bf16), jax.ShapeDtypeStruct(ctx_kv.shape, bf16)],
        compiler_params=SMALL,
        name="attend_back",
    )(half, *[qkv] * 6, ctx_kv, ctx_kv, d_attended, d_attended)


def pack_kernel(rate, gin, gout, g_one, g_two, out):
    for k, ref in enumerate((rate, gin, gout)):
        out[0, k * NST : (k + 1) * NST, :] = ref[...].astype(f32).T.astype(bf16)
    out[0, 3 * NST : 3 * NST + 1, :] = g_one[...]
    out[0, 3 * NST + 1 : 3 * NST + 2, :] = g_two[...]


def norm_kernel(idx, gain, x0, x1, x2, x3, low_ref, inv_ref, u_ref):
    rows, dim = x0.shape
    cols = dim // TEAM
    for r, ref in enumerate((x0, x1, x2, x3)):
        x = ref[...].astype(f32)
        inv = lax.rsqrt(jnp.mean(x * x, axis=-1, keepdims=True) + epsilon)
        inv_ref[r * rows : (r + 1) * rows, :] = inv
        low_ref[r * rows : (r + 1) * rows, :] = (x * inv * gain[...]).astype(bf16)
        for c in range(cols // LANES):
            at = pl.multiple_of(idx[0] * cols + c * LANES, LANES)
            u = low_ref[r * rows : (r + 1) * rows, pl.ds(at, LANES)].astype(f32)
            u_ref[:, r * (cols // LANES) + c, :] = u


def first_norm(idx, gain, blocks):
    rows, dim = blocks[0].shape
    shapes = (
        jax.ShapeDtypeStruct((TEAM * rows, dim), bf16),
        jax.ShapeDtypeStruct((TEAM * rows, 1), f32),
        jax.ShapeDtypeStruct((rows, dim // LANES, LANES), f32),
    )
    return call(norm_kernel, "first_norm", shapes, (idx, gain[None], *blocks))


def part_types(rows, dim):
    return tuple(jax.ShapeDtypeStruct((rows, dim), (f32, bf16)[r % 2]) for r in range(TEAM))


def dot_kernel(x_ref, w_ref, *parts):
    rows = parts[0].shape[0]
    for r in (3, 1, 2, 0):
        part = dot_nn(x_ref[r * rows : (r + 1) * rows, :], w_ref[...])
        parts[r][...] = part.astype(parts[r].dtype)


def dot_parts(name, x, w):
    return call(dot_kernel, name, part_types(x.shape[0] // TEAM, w.shape[1]), (x, w), 0)


def out_kernel(idx, x_ref, w0, w1, w2, w3, *parts):
    rows, cols = parts[0].shape[0], w0.shape[1]
    for r in (3, 1, 2, 0):
        for q, w in enumerate((w0, w1, w2, w3)):
            at = pl.multiple_of((idx[0] ^ q) * cols, LANES)
            part = dot_nn(x_ref[r * rows : (r + 1) * rows, :], w[...])
            parts[r][:, pl.ds(at, cols)] = part.astype(parts[r].dtype)


def context_kv_kernel(idx, w_ref, c0, c1, c2, c3, kv_ref, context_ref):
    cols = c0.shape[1]
    width = w_ref.shape[1] // 3
    for r, part in enumerate((c0, c1, c2, c3)):
        at = pl.multiple_of((idx[0] ^ r) * cols, LANES)
        for w in (0, 1):
            v = w ^ (r & 1)
            context_ref[w * CTX : (w + 1) * CTX, pl.ds(at, cols)] = part[v * CTX : (v + 1) * CTX, :]
    kv_ref[...] = dot_nn(context_ref[...], w_ref[:, width:]).astype(bf16)


def mlp_kernel(m0, m1, m2, m3, g0, g1, g2, g3, up, down, act_ref, dpre_ref, *parts_and_sum):
    parts, total = parts_and_sum[:-1], parts_and_sum[-1]
    k = pl.program_id(0)
    rows = m0.shape[0]
    c = math.sqrt(2.0 / math.pi)
    for r, (m, g) in enumerate(((m0, g0), (m1, g1), (m2, g2), (m3, g3))):
        at = slice(r * rows, (r + 1) * rows)
        x = dot_nn(m[...], up[...])
        t = jnp.tanh(c * (x + 0.044715 * (x * x * x)))
        cdf = 0.5 * (1.0 + t)
        act_ref[at, :] = (x * cdf).astype(bf16)
        slope = cdf + (0.5 * c) * x * (1.0 - t * t) * (1.0 + (3 * 0.044715) * (x * x))
        d_pre = (dot_nt(g[...], down[...]) * slope).astype(bf16)
        dpre_ref[at, :] = d_pre
        new = dot_nt(d_pre, up[...])
        total[at, :] = jnp.where(k == 0, new, total[at, :] + new)

    @pl.when(k == pl.num_programs(0) - 1)
    def _():
        for r, part in enumerate(parts):
            part[...] = total[r * rows : (r + 1) * rows, :].astype(part.dtype)


def feed_forward(mlp_blocks, grad_blocks, up, down):
    rows, dim = mlp_blocks[0].shape
    units = up.shape[1]
    step = 256

    unit_out = jax.ShapeDtypeStruct((TEAM * rows, units), bf16)
    return pl.pallas_call(
        mlp_kernel,
        grid=(units // step,),
        out_shape=(unit_out, unit_out) + part_types(rows, dim),
        in_specs=[block_of((rows, dim))] * 8
        + [pl.BlockSpec((dim, step), lambda k: (0, k)), pl.BlockSpec((step, dim), lambda k: (k, 0))],
        out_specs=(pl.BlockSpec((TEAM * rows, step), lambda k: (0, k)),) * 2
        + (block_of((rows, dim)),) * TEAM,
        scratch_shapes=[pltpu.VMEM((TEAM * rows, dim), f32)],
        compiler_params=MIDDLE,
        name="feed_forward",
    )(*mlp_blocks, *grad_blocks, up, down)


def mlp_grad_kernel(x_ref, y0, y1, y2, y3, out):
    rows = y0.shape[0]
    grads = [dot_tn(x_ref[r * rows : (r + 1) * rows, :], y[...]) for r, y in enumerate((y0, y1, y2, y3))]
    out[...] = functools.reduce(jnp.add, grads).astype(bf16)


def down_grad(act, grad_blocks):
    rows, dim = grad_blocks[0].shape
    step = 256
    return pl.pallas_call(
        mlp_grad_kernel,
        grid=(act.shape[1] // step,),
        out_shape=jax.ShapeDtypeStruct((act.shape[1], dim), bf16),
        in_specs=[pl.BlockSpec((act.shape[0], step), lambda k: (0, k))]
        + [block_of((rows, dim))] * TEAM,
        out_specs=pl.BlockSpec((step, dim), lambda k: (k, 0)),
        compiler_params=SMALL,
        name="down_grad",
    )(act, *grad_blocks)


def up_grad_kernel(x0, x1, x2, x3, y_ref, out):
    rows = x0.shape[0]
    grads = [dot_tn(x[...], y_ref[r * rows : (r + 1) * rows, :]) for r, x in enumerate((x0, x1, x2, x3))]
    out[...] = functools.reduce(jnp.add, grads).astype(bf16)


def up_grad(mlp_blocks, d_pre):
    rows, dim = mlp_blocks[0].shape
    step = 256
    return pl.pallas_call(
        up_grad_kernel,
        grid=(dim // step,),
        out_shape=jax.ShapeDtypeStruct((dim, d_pre.shape[1]), bf16),
        in_specs=[pl.BlockSpec((rows, step), lambda k: (0, k))] * TEAM
        + [block_of(d_pre.shape)],
        out_specs=pl.BlockSpec((step, d_pre.shape[1]), lambda k: (k, 0)),
        compiler_params=SMALL,
        name="up_grad",
    )(*mlp_blocks, d_pre)


def attended_grad_kernel(idx, w0, w1, w2, w3, h0, h1, h2, h3, out):
    rows, cols = h0.shape[0], w0.shape[1]
    for r, h in enumerate((h0, h1, h2, h3)):
        grad = 0.0
        for q, w in enumerate((w0, w1, w2, w3)):
            at = pl.multiple_of((idx[0] ^ q) * cols, LANES)
            grad = grad + dot_nt(h[:, pl.ds(at, cols)], w[...])
        out[r * rows : (r + 1) * rows, :] = grad.astype(bf16)


def out_grad_kernel(idx, att_ref, h0, h1, h2, h3, *parts):
    rows, cols = h0.shape[0], parts[0].shape[1]
    for q, part in enumerate(parts):
        at = pl.multiple_of((idx[0] ^ q) * cols, LANES)
        grads = [
            dot_tn(att_ref[r * rows : (r + 1) * rows, :], h[:, pl.ds(at, cols)])
            for r, h in enumerate((h0, h1, h2, h3))
        ]
        part[...] = functools.reduce(jnp.add, grads).astype(bf16)


def context_grad_kernel(idx, d_ref, w_ref, *parts):
    cols = parts[0].shape[1]
    width = w_ref.shape[1] // 3
    for r, part in enumerate(parts):
        at = pl.multiple_of((idx[0] ^ r) * cols, 16)
        for w in (0, 1):
            v = w ^ (r & 1)
            grad = dot_nt(d_ref[w * CTX : (w + 1) * CTX, :], w_ref[pl.ds(at, cols), width:])
            part[v * CTX : (v + 1) * CTX, :] = grad.astype(part.dtype)


def inputs_grad_kernel(idx, dq_ref, w_ref, du_ref, inv_ref, x0, x1, x2, x3, *outs):
    parts, gain_ref, work = outs[:TEAM], outs[TEAM], outs[TEAM + 1]
    rows, dim = x0.shape
    cols = dim // TEAM
    gain = 0.0
    for r, x in enumerate((x0, x1, x2, x3)):
        at = slice(r * rows, (r + 1) * rows)
        work[...] = dot_nt(dq_ref[at, :], w_ref[...])
        for c in range(cols // LANES):
            col = pl.ds(pl.multiple_of(idx[0] * cols + c * LANES, LANES), LANES)
            work[:, col] = work[:, col] + du_ref[:, r * (cols // LANES) + c, :]
        grad = work[...]
        parts[r][...] = grad.astype(parts[r].dtype)
        gain = gain + jnp.sum(grad * (x[...].astype(f32) * inv_ref[at, :]), axis=0, keepdims=True)
    gain_ref[...] = gain


def cut_states_kernel(idx, init_ref, ends_ref, i0, i1, e0, e1, e2, e3):
    cols = i0.shape[1]
    for r, out in enumerate((e0, e1, e2, e3)):
        at = pl.multiple_of((idx[0] ^ r) * cols, 16)
        out[...] = ends_ref[pl.ds(at, cols), :].T
        if r < 2:
            (i0, i1)[r][...] = init_ref[pl.ds(at, cols), :].T


def join_states_kernel(late, i0, i1, e0, e1, e2, e3, init_ref, twice_ref, first_ref, second_ref):
    per = init_ref.shape[1] // 2
    for w in range(2):
        for c in range(per):
            at = slice(c * LANES, (c + 1) * LANES)
            init = (i0, i1)[w][:, at]
            init_ref[:, w * per + c, :] = init
            twice_ref[:, w * per + c, :] = init
            twice_ref[:, (2 + w) * per + c, :] = init
            own, other = (e0, e1)[w][:, at], (e2, e3)[w][:, at]
            first_ref[:, w * per + c, :] = jnp.where(late[0] == 1, other, own)
            second_ref[:, w * per + c, :] = jnp.where(late[0] == 1, own, other)


def cut_ends_kernel(late, first_ref, second_ref, e0, e1, e2, e3):
    per = first_ref.shape[1] // 2
    for w in range(2):
        for c in range(per):
            at = slice(c * LANES, (c + 1) * LANES)
            one, two = first_ref[:, w * per + c, :], second_ref[:, w * per + c, :]
            (e0, e1)[w][:, at] = jnp.where(late[0] == 1, two, one)
            (e2, e3)[w][:, at] = jnp.where(late[0] == 1, one, two)


def join_ends_kernel(idx, e0, e1, e2, e3, out):
    cols = e0.shape[1]
    for r, part in enumerate((e0, e1, e2, e3)):
        at = pl.multiple_of((idx[0] ^ r) * cols, 16)
        out[pl.ds(at, cols), :] = part[...].T


def small_kernel(spots, p0, p1, p2, p3, gains_ref, rate_ref, in_ref, out_ref, init_ref):
    packs = [p[...] for p in (p0, p1, p2, p3)]
    tiles = packs[0].shape[0] - 3 * NST * 2 - NST * 4
    one, two = 3 * NST * 2, 3 * NST * 2 + tiles
    gains = functools.reduce(jnp.add, [p[one:two] for p in packs])
    row = lax.broadcasted_iota(jnp.int32, gains.shape, 0)
    for k in (0, 1):
        mine = row == k * (tiles // 2) + spots[1]
        gains_ref[k : k + 1, :] = jnp.sum(jnp.where(mine, gains, 0.0), axis=0, keepdims=True)
    chosen = packs[0]
    for r in (1, 2, 3):
        chosen = jnp.where(spots[0] == r, packs[r], chosen)
    side = spots[1] % 2 == 1
    params = chosen[:one].reshape(3 * NST, 2, LANES)
    params = jnp.where(side, params[:, 1], params[:, 0])
    for k, ref in enumerate((rate_ref, in_ref, out_ref)):
        ref[...] = params[k * NST : (k + 1) * NST].T
    init = chosen[two:].reshape(NST, 4, LANES)
    window = [jnp.where(side, init[:, 2 * w + 1], init[:, 2 * w]) for w in (0, 1)]
    init_ref[...] = jnp.where(spots[0] % 2 == 1, window[1], window[0]).T


def added(p0, one, far):
    return p0[...] + one[...].astype(f32) + far[...].astype(f32)


def second_norm_kernel(tok, p0, one, far, gain, hidden_ref, inv_ref, low_ref):
    hidden = tok[...].astype(f32) + added(p0, one, far)
    inv = lax.rsqrt(jnp.mean(hidden * hidden, axis=-1, keepdims=True) + epsilon)
    hidden_ref[...] = hidden
    inv_ref[...] = inv
    low_ref[...] = (hidden * inv * gain[...]).astype(bf16)


def result_kernel(hidden, p0, one, far, out):
    out[...] = (hidden[...] + added(p0, one, far)).astype(bf16)


def norm_back(grad, normed, inv, gain):
    scaled = grad * gain
    return inv * (scaled - normed * jnp.mean(scaled * normed, axis=-1, keepdims=True))


def hidden_grad_kernel(cot, hidden, inv, gain, p0, one, far, out_ref, low_ref, gain_ref):
    grad = added(p0, one, far)
    normed = hidden[...] * inv[...]
    gain_ref[...] = jnp.sum(grad * normed, axis=0, keepdims=True)
    out = cot[...].astype(f32) + norm_back(grad, normed, inv[...], gain[...])
    out_ref[...] = out
    low_ref[...] = out.astype(bf16)


def tokens_grad_kernel(d_hidden, tok, inv, gain, p0, one, far, out):
    grad = added(p0, one, far)
    normed = tok[...].astype(f32) * inv[...]
    out[...] = (d_hidden[...] + norm_back(grad, normed, inv[...], gain[...])).astype(bf16)


def context_sum_kernel(p0, one, far, out):
    out[...] = added(p0, one, far).astype(bf16)


def context_rows_kernel(flags, came, own, dy_ref, dy_full, dy0_full):
    per = dy_ref.shape[1] // 2
    zero = jnp.zeros((CTX, LANES), f32)
    for w in range(2):
        for c in range(per):
            at = (slice(w * CTX, (w + 1) * CTX), slice(c * LANES, (c + 1) * LANES))
            dy = came[at].astype(f32)
            dy_ref[:, w * per + c, :] = dy
            dy_full[:, w * per + c, :] = jnp.where(flags[0] == 1, dy, zero)
            dy_full[:, (2 + w) * per + c, :] = jnp.where(flags[0] == 1, zero, dy)
            dy0_full[:, w * per + c, :] = jnp.where(flags[1] == 0, own[at].astype(f32), zero)
            dy0_full[:, (2 + w) * per + c, :] = zero


def on_device(
    tokens,
    w_qkv,
    w_out,
    w_up,
    w_down,
    g_attn,
    g_mlp,
    ssm_rate,
    ssm_in,
    ssm_out,
    h_init,
    cotangent,
    d_h_ends,
):
    nd, ns = lax.axis_size("dp"), lax.axis_size("seq")
    ny = nd // 2
    dp, seq = lax.axis_index("dp"), lax.axis_index("seq")
    late = seq % 2 == 1
    block = seq // 2
    me = (seq % 2) * 2 + dp % 2
    idx = jnp.stack([me, dp // 2]).astype(jnp.int32)
    place = (seq * ny + dp // 2).astype(jnp.int32).reshape(1)
    half = (seq % 2).astype(jnp.int32).reshape(1)
    rows, dim = tokens.shape[1:]
    shard = w_qkv.shape[0]
    width = HEADS * HD // TEAM
    cols = dim // TEAM
    fb = w_down.shape[0] // TEAM
    tile = (dim // LANES, LANES)
    half_tile = (dim // LANES // 2, LANES)

    def like(shape, dtype):
        return jax.ShapeDtypeStruct(shape, dtype)


    share_attn, share_up, *share_down = shares(idx, w_qkv, w_out, w_up, w_down, ny, ns)
    attn, up = Gathering(*share_attn, True), Gathering(*share_up, True)
    down = [Gathering(*share, False) for share in share_down]
    attn_pair = attn.step()
    x_blocks = gather_team(after(tokens[0], attn_pair))
    up.step(attn_pair)
    attn_first = attn.rest()
    for part in down:
        part.step(attn_first)
    attn_second = attn.step()
    attn_third = attn.across(0)
    attn_last = attn.across(1)
    up_first = up.rest(attn_second)
    small = call(
        pack_kernel,
        "pack_small",
        jax.ShapeDtypeStruct((1, 3 * NST + 2, shard), bf16),
        (ssm_rate, ssm_in, ssm_out, g_attn[None], after(g_mlp[None], share_attn[1])),
        0,
    )
    for bit in [1] + high_bits("seq")[::-1]:
        got = swap(small, "seq", bit)
        upper = (seq & bit) != 0
        small = jnp.concatenate([jnp.where(upper, got, small), jnp.where(upper, small, got)], axis=0)
    small = small.astype(f32)
    gain_one = small[:, 3 * NST].reshape(dim)
    gain_two = small[:, 3 * NST + 1].reshape(dim)
    params = small[:, : 3 * NST].transpose(1, 0, 2).reshape(3 * NST, dim)
    params = lax.dynamic_slice_in_dim(params, me * cols, cols, 1)
    params = jnp.broadcast_to(params[:, None], (3 * NST, TEAM, cols)).reshape((3, NST) + tile)
    rate, gin, gout = params[0], params[1], params[2]
    half_rate = rate[:, : tile[0] // 2]

    by_channel = like((NST, cols), f32)
    init, near_init, *end_cot = call(
        cut_states_kernel,
        "cut_states",
        (by_channel,) * 6,
        (idx, h_init[0], after(d_h_ends[0, 0], share_attn[1])),
    )
    init, init_twice, end_first, end_second = call(
        join_states_kernel,
        "join_states",
        tuple(like((NST,) + t, f32) for t in (half_tile, tile, half_tile, half_tile)),
        (half, init, swap_team(near_init, 1), *trade_team(end_cot)),
    )
    end_cot = [end_first, end_second]
    g_blocks = gather_team(after(cotangent[0], attn_first))

    def by_half(a, axis=1):
        n = a.shape[axis] // 2
        own, other = lax.slice_in_dim(a, 0, n, axis=axis), lax.slice_in_dim(a, n, 2 * n, axis=axis)
        return ordered([own, other], seq % 2)

    def by_owner(first, second):
        return jnp.concatenate(ordered([first, second], seq % 2), axis=1)

    inputs_low, inv_one, u = first_norm(idx, after(gain_one, attn_first), x_blocks)

    a = jnp.exp(-rate)
    s_mid, s_end = local_ends(u, a)
    decay = jnp.exp(-half_rate * rows)
    first_end, second_end = by_half(gin * s_end)
    span = 2 * rows

    def chain(inclusive, back, meanwhile):
        exclusive, step = jnp.zeros_like(inclusive), 1
        while step < ns // 2:
            pairs = [(k, k + 2 * step) for k in range(ns - 2 * step)]
            got = lax.ppermute(inclusive, "seq", [(t, f) for f, t in pairs] if back else pairs)
            got = after(got, meanwhile)
            exclusive = exclusive + jnp.exp(-half_rate * (span * (step - 1))) * got
            inclusive = inclusive + jnp.exp(-half_rate * (span * step)) * got
            step *= 2
        return exclusive

    entering = chain(decay * first_end + second_end, False, up_first)
    state_zero = jnp.exp(-half_rate * (span * block).astype(f32)) * init + entering
    state_one = decay * state_zero + first_end
    state_two = decay * state_one + second_end
    state_in = by_owner(state_zero, state_one)
    ends = call(cut_ends_kernel, "cut_ends", (by_channel,) * TEAM, (half, state_one, state_two))
    ends = call(join_ends_kernel, "join_ends", like((dim, NST), f32), (idx, *trade_team(ends)))
    on_second = by_owner(jnp.zeros_like(init), jnp.ones_like(init))
    h_mid = jnp.exp(-rate * (rows - CTX)) * state_in + gin * s_mid
    h_mid = jnp.where(on_second > 0, h_mid, init_twice)
    h_mid = after(h_mid, (attn_second, attn_third))
    y_first, y_second = contexts(half, u, a, gin * on_second, gout, h_mid)
    passed = lax.ppermute(y_second, "seq", [(k, k + 2) for k in range(ns - 2)])
    up_second = up.step(entering)
    up_third = up.across(0, attn_last)
    context = jnp.where(block == 0, y_first, after(passed, up_second))
    down_first = down[0].rest(passed)
    down_second = down[1].rest(up_third)
    context = gather_team(context)

    places = jnp.stack([place[0], seq]).astype(jnp.int32)
    full_qkv, *full_out = place_weight(idx, places, [(attn.pieces, 0, 1, 0)], 3 * width)
    full_qkv = after(full_qkv, (down_first, up_third))
    full_out = trade_team(full_out)
    qkv = dot_nn(inputs_low, full_qkv).astype(bf16)
    ctx_kv, context = call(
        context_kv_kernel,
        "context_kv",
        (like((2 * CTX, 2 * width), bf16), like((2 * CTX, dim), bf16)),
        (idx, full_qkv, *context),
    )
    attended = attend(half, qkv, ctx_kv)

    down_third = down[0].step(down_second)
    up_last = up.across(1, up_third)
    attended = after(attended, (g_blocks[2], down_second))
    attended_parts = call(out_kernel, "out_dot", part_types(rows, dim), (idx, attended, *full_out))
    attended_parts = sum_team(attended_parts, None, (ends, down_third, up_last))
    down[1].step(down_third)
    (full_up,) = place_weight(idx, places, [(up.pieces, 0, 1, 0)])
    down = [(part.pieces, 1, 2, h) for h, part in enumerate(down)]
    (full_down,) = place_weight(idx, places, down)

    hidden, inv_two, mlp_in = call(
        second_norm_kernel,
        "second_norm",
        (like((rows, dim), f32), like((rows, 1), f32), like((rows, dim), bf16)),
        (tokens[0], *attended_parts[:3], gain_two[None]),
        0,
    )
    mlp_in = gather_team(mlp_in)
    act, d_pre, *d_mlp = feed_forward(mlp_in, g_blocks, full_up, full_down)
    d_down = down_grad(act, g_blocks)
    reduction = HalvedReduction if (nd, ns) == (4, 8) else Reduction
    sum_down = reduction(d_down, place)
    sum_down.step()
    d_up = up_grad(mlp_in, after(d_pre, sum_down.sent))
    sum_up = reduction(d_up, place)
    sum_up.step()
    result = dot_parts("down_dot", after(act, sum_up.sent), full_down)
    d_mlp = sum_team(d_mlp, d_down, result)
    sum_down.step(d_mlp[3])
    d_hidden, d_hidden_low, d_gain_two = call(
        hidden_grad_kernel,
        "hidden_grad",
        (like((rows, dim), f32), like((rows, dim), bf16), like((1, dim), f32)),
        (after(cotangent[0], sum_down.sent), hidden, inv_two, gain_two[None], *d_mlp[:3]),
        0,
    )
    hidden_blocks = gather_team(d_hidden_low)
    sum_down.step(d_hidden)

    d_attended = call(
        attended_grad_kernel,
        "attended_grad",
        jax.ShapeDtypeStruct(attended.shape, bf16),
        (idx, after(full_out[0], sum_down.sent), *full_out[1:], *hidden_blocks),
    )
    d_out = call(
        out_grad_kernel,
        "out_grad",
        (jax.ShapeDtypeStruct((width, cols), bf16),) * TEAM,
        (idx, after(attended, d_attended), *hidden_blocks),
    )
    d_qkv, d_ctx_kv = attend_back(half, qkv, ctx_kv, after(d_attended, d_out))
    d_out = trade_team(d_out)
    sum_up.step(d_ctx_kv)
    d_context = call(
        context_grad_kernel,
        "context_grad",
        part_types(2 * CTX, cols),
        (idx, after(d_ctx_kv, sum_up.sent), full_qkv),
    )
    d_attn = attn_grad(idx, inputs_low, after(d_qkv, d_context), context, d_ctx_kv, d_out)
    sum_attn = reduction(d_attn, place)
    sum_attn.step()
    d_context = sum_team(d_context, None, sum_attn.sent)
    d_context = call(context_sum_kernel, "context_sum", like((2 * CTX, cols), bf16), d_context[:3], 0)
    came = lax.ppermute(d_context, "seq", [(k + 2, k) for k in range(ns - 2)])
    flags = jnp.stack([seq % 2, block]).astype(jnp.int32)
    dy, dy_full, dy0_full = call(
        context_rows_kernel,
        "context_rows",
        (like((CTX,) + half_tile, f32), like((CTX,) + tile, f32), like((CTX,) + tile, f32)),
        (flags, came, d_context),
    )

    lam_mid = tail_adjoint(dy, a, gout)
    g_second = jnp.exp(-half_rate * (rows - CTX + 1)) * lam_mid + decay * end_cot[1]
    d_a, d_gout, g_init = first_context_back(after(dy0_full, lam_mid), a, gout, init_twice)
    leaving = chain(decay * (end_cot[0] + g_second), True, g_init)
    sum_up.step(leaving)
    sum_attn.step(sum_up.sent)
    sum_down.step(sum_attn.sent)
    lam_end = by_owner(end_cot[0] + g_second + decay * leaving, end_cot[1] + leaving)
    du, d_gin, d_a, d_gout, g_in = ssm_back(
        u, dy_full, a, gin, gout, state_in, after(lam_end, sum_down.sent), d_a, d_gout
    )
    g_first = by_half(g_in)[0]
    d_init = g_init[:, : tile[0] // 2] + jnp.where(block == 0, g_first, jnp.zeros_like(g_first))
    d_rate = -a * d_a

    *d_inputs, d_gain_one = call(
        inputs_grad_kernel,
        "inputs_grad",
        part_types(rows, dim) + (jax.ShapeDtypeStruct((1, dim), f32),),
        (idx, d_qkv, full_qkv, du, inv_one, *x_blocks),
        scratch_shapes=[pltpu.VMEM((rows, dim), f32)],
    )
    d_down = spread_weight("down", sum_down.last(), idx, [w_down.shape])[0]
    sum_up.step(d_gain_one)
    sum_attn.step(sum_up.sent)
    result = sum_team(result, d_context, du)
    result = call(result_kernel, "result_sum", like((rows, dim), bf16), (hidden, *result[:3]), 0)
    *d_inputs, d_inputs_far = sum_team(d_inputs, None, d_down)
    d_tokens = call(
        tokens_grad_kernel,
        "tokens_grad",
        like((rows, dim), bf16),
        (d_hidden, tokens[0], inv_one[:rows], gain_one[None], *d_inputs),
        0,
    )

    d_params = after(jnp.stack([d_rate, d_gin, d_gout]), d_gain_one)
    d_params = d_params.reshape(3 * NST, TEAM, cols).sum(1)
    d_gains = jnp.concatenate([d_gain_one[0], d_gain_two[0]])
    pack = [d_params.reshape(-1, LANES), d_gains.reshape(-1, LANES), d_init.reshape(-1, LANES)]
    pack = after(jnp.concatenate(pack, axis=0), (sum_attn.sent, d_inputs_far))
    for n, bit in enumerate(high_bits("seq")):
        if n == 1:
            pack = after(pack, sum_attn.step())
        pack = pack + swap(pack, "seq", bit)
    one, two = 3 * NST * cols // LANES, 3 * NST * cols // LANES + 2 * dim // LANES
    shared = pack[:two]
    for bit in high_bits("dp"):
        shared = shared + swap(shared, "dp", bit)
    packs = gather_team(jnp.concatenate([shared, pack[two:]], axis=0))
    if shard == LANES:
        spots = jnp.stack([me ^ (seq * shard // cols), seq]).astype(jnp.int32)
        gains, *d_params, state_grad = call(
            small_kernel,
            "small_grads",
            (like((2, shard), f32),) + (like((shard, NST), f32),) * 4,
            (spots, *packs),
        )
        state_grad = state_grad[None]
    else:
        packs = jnp.stack(packs)
        gains = packs[:, one:two].sum(0).reshape(2, ns, shard)
        gains = pick(gains, seq, 1)
        member = me ^ (seq * shard // cols)
        inner = seq * shard % cols
        chosen = pick(packs, member)
        d_params = chosen[:one].reshape(3 * NST, cols)
        d_params = lax.dynamic_slice_in_dim(d_params, inner, shard, 1).reshape(3, NST, shard)
        d_params = d_params.transpose(0, 2, 1)
        state_grad = chosen[two:].reshape(NST, 2, cols)
        state_grad = pick(state_grad, member % 2, 1)
        state_grad = lax.dynamic_slice_in_dim(state_grad, inner, shard, 1).T[None]

    if fb % LANES:
        d_up = spread_narrow(sum_up.last(), idx, w_up.shape, fb)
    else:
        d_up = spread_weight("up", sum_up.last(), idx, [w_up.shape], fb)[0]
    d_wqkv, d_out = spread_weight("attn", sum_attn.last(), idx, [w_qkv.shape, w_out.shape])
    return (
        result[None],
        d_tokens[None],
        d_wqkv,
        d_out,
        d_up,
        d_down,
        gains[0],
        gains[1],
        d_params[0],
        d_params[1],
        d_params[2],
        state_grad,
        ends[None, None],
    )


def solution(mesh):
    return jax.shard_map(
        on_device,
        mesh=mesh,
        in_specs=(
            P("dp", "seq", None),
            P("seq", None),
            P("seq", None),
            P("seq", None),
            P("seq", None),
            P("seq"),
            P("seq"),
            P("seq", None),
            P("seq", None),
            P("seq", None),
            P("dp", None, None),
            P("dp", "seq", None),
            P("dp", "seq", None, None),
        ),
        out_specs=(
            P("dp", "seq", None),
            P("dp", "seq", None),
            P("seq", None),
            P("seq", None),
            P("seq", None),
            P("seq", None),
            P("seq"),
            P("seq"),
            P("seq", None),
            P("seq", None),
            P("seq", None),
            P("dp", "seq", None),
            P("dp", "seq", None, None),
        ),
        check_vma=False,
    )
```

profile of v0, /device:TPU:1, one launch (start us, length us, event | category | flops | bytes accessed | tf_op | source)
XLA Modules:
  0.0 391.2 jit_solution(1670186520921994810)
XLA Ops:
  3.8 3.2 shares.1
  7.1 2.1 collective-permute-start
  14.2 2.2 collective-permute-start.2
  18.2 3.3 collective-permute-start.5
  21.5 10.7 %collective-permute-done.4.b_ref = bf16[2,64,1024]{2,1,0:T(8,128)(2,1)S(1)} collective-permute-done((bf16[2,64,1024]{2,1,0:T(8,128)(2,1)S(1)}, bf16[2,64,1024]{2,1,0:T(8,128)(2,1)S(1)}, u32[]{:S(2)}, u32[]{:S(2)}) %collective-permute-start.4) | collective-permute-done | bytes 262176 | tf_op jit(solution)/shard_map/ppermute | solution.py:26
  35.7 3.7 collective-permute-done.17.b_ref
  40.1 4.6 %collective-permute-done.8.refs_1_ = bf16[4,64,1024]{2,1,0:T(8,128)(2,1)} collective-permute-done((bf16[4,64,1024]{2,1,0:T(8,128)(2,1)S(1)}, bf16[4,64,1024]{2,1,0:T(8,128)(2,1)}, u32[]{:S(2)}, u32[]{:S(2)}) %collective-permute-start.8) | collective-permute-done | bytes 524320 | tf_op jit(solution)/shard_map/ppermute | solution.py:26
  47.5 2.0 first_norm.1
  52.7 3.1 collective-permute-start.16
  58.6 2.7 collective-permute-start.12
  64.8 2.9 collective-permute-start.19
  77.1 5.9 %collective-permute-done.9.refs_2_ = bf16[4,64,1024]{2,1,0:T(8,128)(2,1)S(1)} collective-permute-done((bf16[4,64,1024]{2,1,0:T(8,128)(2,1)S(1)}, bf16[4,64,1024]{2,1,0:T(8,128)(2,1)S(1)}, u32[]{:S(2)}, u32[]{:S(2)}) %collective-permute-start.9) | collective-permute-done | bytes 524320 | tf_op jit(solution)/shard_map/ppermute | solution.py:26
  83.0 2.7 ssm_context.1
  85.7 2.8 collective-permute-start.20
  88.6 5.5 %collective-permute-done.10.refs_3_ = bf16[4,64,1024]{2,1,0:T(8,128)(2,1)S(1)} collective-permute-done((bf16[4,64,1024]{2,1,0:T(8,128)(2,1)}, bf16[4,64,1024]{2,1,0:T(8,128)(2,1)S(1)}, u32[]{:S(2)}, u32[]{:S(2)}) %collective-permute-start.10) | collective-permute-done | bytes 524320 | tf_op jit(solution)/shard_map/ppermute | solution.py:26
  94.9 1.7 collective-permute-start.22
  97.5 1.6 append.16.a_ref
  100.1 1.6 collective-permute-start.25
  101.8 1.7 collective-permute-start.24
  104.5 3.5 collective-permute-start.26
  114.5 1.7 collective-permute-start.30
  117.9 2.3 collective-permute-start.29
  120.2 1.8 convolution_convert_fusion.q0.q1.k0.k1.v0.v1
  123.5 5.0 %attend.1.x_ref.att_ref = bf16[1024,256]{1,0:T(8,128)(2,1)S(1)} custom-call(s32[1]{0:T(128)} %bitcast.3.late.half_ref, bf16[1024,768]{1,0:T(8,128)(2,1)S(1)} %convolution_convert_fusion.q0.q1.k0.k1.v0.v1, bf16[1024,768]{1,0:T(8,128)(2,1)S(1)} %convolution_convert_fusion.q0.q1.k0.k1.v0.v1, bf16[1024,768]{1,0:T(8,128)(2,1)S(1)} %convolution_convert_fusion.q0.q1.k0.k1.v0.v1, ...), custom_call_target="tpu_custom_call" | custom-call | tf_op jit(solution)/shard_map/attend/pallas_call | solution.py:771
  128.6 3.6 collective-permute-done.29.b_ref
  138.9 10.8 %collective-permute-done.37.e2 = f32[16,256]{1,0:T(8,128)S(1)} collective-permute-done((f32[16,256]{1,0:T(8,128)S(1)}, f32[16,256]{1,0:T(8,128)S(1)}, u32[]{:S(2)}, u32[]{:S(2)}) %collective-permute-start.37) | collective-permute-done | bytes 16416 | tf_op jit(solution)/shard_map/ppermute | solution.py:26
  150.8 2.0 collective-permute-done.38.e3
  155.4 1.8 collective-permute-start.46
  158.7 8.1 %collective-permute-done.42.m2.x2 = bf16[256,1024]{1,0:T(8,128)(2,1)S(1)} collective-permute-done((bf16[256,1024]{1,0:T(8,128)(2,1)S(1)}, bf16[256,1024]{1,0:T(8,128)(2,1)S(1)}, u32[]{:S(2)}, u32[]{:S(2)}) %collective-permute-start.42) | collective-permute-done | bytes 524320 | tf_op jit(solution)/shard_map/ppermute | solution.py:26
  166.7 1.9 collective-permute-start.43
  170.8 11.6 %feed_forward.1 = (bf16[1024,1024]{1,0:T(8,128)(2,1)S(1)}, bf16[1024,1024]{1,0:T(8,128)(2,1)S(1)}, f32[256,1024]{1,0:T(8,128)S(1)}, bf16[256,1024]{1,0:T(8,128)(...) custom-call(bf16[256,1024]{1,0:T(8,128)(2,1)S(1)} %get-tuple-element.237.m0.x0, ...), custom_call_target="tpu_custom_call" | custom-call | tf_op jit(solution)/shard_map/feed_forward/pallas_call | solution.py:900
  182.5 3.2 down_grad.1
  189.1 3.5 up_grad.1
  193.4 2.9 down_dot.1
  199.1 2.6 collective-permute-done.54.far
  204.3 1.8 collective-permute-start.52
  206.3 1.6 collective-permute-start.55
  207.9 8.1 %collective-permute-done.56.h2 = bf16[256,1024]{1,0:T(8,128)(2,1)S(1)} collective-permute-done((bf16[256,1024]{1,0:T(8,128)(2,1)S(1)}, bf16[256,1024]{1,0:T(8,128)(2,1)S(1)}, u32[]{:S(2)}, u32[]{:S(2)}) %collective-permute-start.56) | collective-permute-done | bytes 524320 | tf_op jit(solution)/shard_map/ppermute | solution.py:26
  216.0 1.7 collective-permute-start.57
  221.9 7.2 %attend_back.1 = (bf16[1024,768]{1,0:T(8,128)(2,1)S(1)}, bf16[256,512]{1,0:T(8,128)(2,1)S(1)}) custom-call(s32[1]{0:T(128)} %bitcast.3.late.half_ref, bf16[1024,768]{1,0:T(8,128)(2,1)S(1)} %convolution_convert_fusion.q0.q1.k0.k1.v0.v1, bf16[1024,768]{1,0:T(8,128)(2,1)S(1)} %convolution_convert_fusion.q0.q1.k0.k1.v0.v1, ...), custom_call_target="tpu_custom_call" | custom-call | tf_op jit(solution)/shard_map/attend_back/pallas_call | solution.py:791
  229.1 2.1 collective-permute-done.58.came_ref
  239.1 4.3 %collective-permute-done.64.refs_3_ = bf16[256,256]{1,0:T(8,128)(2,1)S(1)} collective-permute-done((bf16[256,256]{1,0:T(8,128)(2,1)S(1)}, bf16[256,256]{1,0:T(8,128)(2,1)S(1)}, u32[]{:S(2)}, u32[]{:S(2)}) %collective-permute-start.64) | collective-permute-done | bytes 131104 | tf_op jit(solution)/shard_map/ppermute | solution.py:36
  243.4 5.1 %attn_grad.1 = bf16[1024,1024]{1,0:T(8,128)(2,1)S(1)} custom-call(s32[2]{0:T(128)S(1)} %copy-done.54, bf16[1024,1024]{1,0:T(8,128)(2,1)S(1)} %copy-done.15, bf16[1024,768]{1,0:T(8,128)(2,1)S(1)} %get-tuple-element.279.dq_ref, bf16[256,1024]{1,0:T(8,128)(2,1)S(1)} %get-tuple-element.280.ctx_ref, bf16[256,512]{1,0:T(8,128)(2,1)S(1)} %get-tuple-element.273.d_ref.dctx_ref, ...), custom_call_target="tpu_custom_call" | custom-call | tf_op jit(solution)/shard_map/attn_grad/pallas_call | solution.py:279
  252.1 5.7 %collective-permute-done.66.came = bf16[256,256]{1,0:T(8,128)(2,1)S(1)} collective-permute-done((bf16[256,256]{1,0:T(8,128)(2,1)S(1)}, bf16[256,256]{1,0:T(8,128)(2,1)S(1)}, u32[]{:S(2)}, u32[]{:S(2)}) %collective-permute-start.66) | collective-permute-done | bytes 131104 | tf_op jit(solution)/shard_map/ppermute | solution.py:1331
  262.9 2.4 collective-permute-start.72
  266.8 5.1 %first_context.1 = (f32[16,8,128]{2,1,0:T(8,128)}, f32[16,8,128]{2,1,0:T(8,128)}, f32[16,8,128]{2,1,0:T(8,128)}) custom-call(f32[128,8,128]{2,1,0:T(8,128)} %copy-done.43, f32[16,8,128]{2,1,0:T(8,128)} %copy-done.12, f32[16,8,128]{2,1,0:T(8,128)} %copy-done.25, f32[16,8,128]{2,1,0:T(8,128)} %copy-done.53), custom_call_target="tpu_custom_call" | custom-call | tf_op jit(solution)/shard_map/first_context/pallas_call | solution.py:590
  274.5 3.3 collective-permute-done.68
  280.3 9.6 %collective-permute-done.70.came_ref = bf16[4,64,1024]{2,1,0:T(8,128)(2,1)} collective-permute-done((bf16[4,64,1024]{2,1,0:T(8,128)(2,1)}, bf16[4,64,1024]{2,1,0:T(8,128)(2,1)}, u32[]{:S(2)}, u32[]{:S(2)}) %collective-permute-start.70) | collective-permute-done | bytes 524320 | tf_op jit(solution)/shard_map/ppermute | solution.py:26
  291.8 2.0 collective-permute-start.81
  294.0 10.0 %ssm_back.1 = (f32[256,8,128]{2,1,0:T(8,128)S(1)}, f32[16,8,128]{2,1,0:T(8,128)S(1)}, f32[16,8,128]{2,1,0:T(8,128)S(1)}, f32[16,8,128]{2,1,0:T(8,128)S(1)}, f32[16,8,128]{2,1,0:T(8,128)S(1)}) custom-call(f32[256,8,128]{2,1,0:T(8,128)S(1)} %get-tuple-element.187.u_ref, f32[128,8,128]{2,1,0:T(8,128)S(1)} %copy-done.47, f32[16,8,128]{2,1,0:T(8,128)S(1)} %copy-done.13, ...), custom_call_target="tpu_custom_call" | custom-call | tf_op jit(solution)/shard_map/ssm_back/pallas_call | solution.py:672
  304.1 4.7 %inputs_grad.1 = (f32[256,1024]{1,0:T(8,128)S(1)}, bf16[256,1024]{1,0:T(8,128)(2,1)S(1)}, f32[256,1024]{1,0:T(8,128)S(1)}, bf16[256,1024]{1,0:T(8,128)(2,1)}, f32[1,1024]{1,0:T(1,128)S(1)}) custom-call(s32[2]{0:T(128)S(1)} %copy-done.54, bf16[1024,768]{1,0:T(8,128)(2,1)S(1)} %copy-done.7, bf16[1024,768]{1,0:T(8,128)(2,1)S(1)} %copy-done.3, ...), custom_call_target="tpu_custom_call" | custom-call | tf_op jit(solution)/shard_map/inputs_grad/pallas_call | solution.py:109
  310.6 3.3 collective-permute-start.74
  318.4 1.8 collective-permute-done.76.b_ref
  322.9 1.7 reduce_sum.9
  327.0 4.6 %collective-permute-done.82.refs_0_ = bf16[2,64,1024]{2,1,0:T(8,128)(2,1)} collective-permute-done((bf16[2,64,1024]{2,1,0:T(8,128)(2,1)}, bf16[2,64,1024]{2,1,0:T(8,128)(2,1)}, u32[]{:S(2)}, u32[]{:S(2)}) %collective-permute-start.82) | collective-permute-done | bytes 262176 | tf_op jit(solution)/shard_map/ppermute | solution.py:26
  333.9 2.0 far_sum.9
  344.2 2.5 collective-permute-start.73
  347.4 2.9 collective-permute-start.78
  351.7 2.3 collective-permute-done.91
  358.9 9.9 %collective-permute-done.93.p2 = f32[176,128]{1,0:T(8,128)S(1)} collective-permute-done((f32[176,128]{1,0:T(8,128)S(1)}, f32[176,128]{1,0:T(8,128)S(1)}, u32[]{:S(2)}, u32[]{:S(2)}) %collective-permute-start.93) | collective-permute-done | bytes 90144 | tf_op jit(solution)/shard_map/ppermute | solution.py:26
  376.5 2.7 final_down.1
  379.2 2.3 tokens_grad.1
  381.5 2.8 final_up.1
  388.7 2.5 final_attn.1
  (426 shorter events, 142.6 us)
Async XLA Ops:
  13.2 19.1 %collective-permute-start.6 = (bf16[256,1024]{1,0:T(8,128)(2,1)S(1)}, bf16[256,1024]{1,0:T(8,128)(2,1)S(1)}, u32[]{:S(2)}, u32[]{:S(2)}) collective-permute-start(bf16[256,1024]{1,0:T(8,128)(2,1)S(1)} %bitcast.67), channel_id=1, source_target_pairs={{0,1},{1,0},{2,3},{3,2},{4,5},{5,4},{6,7},{7,6},{8,9},{9,8},{10,11... | collective-permute-start | bytes 1572872 | tf_op jit(solution)/shard_map/ppermute | solution.py:26
  17.3 14.9 %collective-permute-start.4 = (bf16[2,64,1024]{2,1,0:T(8,128)(2,1)S(1)}, bf16[2,64,1024]{2,1,0:T(8,128)(2,1)S(1)}, u32[]{:S(2)}, u32[]{:S(2)}) collective-permute-start(bf16[2,64,1024]{2,1,0:T(8,128)(2,1)S(1)} %append.14.a_ref), channel_id=1, source_target_pairs={{0,4},{1,5},{2,6},{3,7},{4,0},{5,1},{6,2},{7,3},{8,12},{9,13},{10,... | collective-permute-start | bytes 786440 | tf_op jit(solution)/shard_map/ppermute | solution.py:26
  18.2 27.3 %collective-permute-start.5 = (bf16[256,1024]{1,0:T(8,128)(2,1)S(1)}, bf16[256,1024]{1,0:T(8,128)(2,1)S(1)}, u32[]{:S(2)}, u32[]{:S(2)}) collective-permute-start(bf16[256,1024]{1,0:T(8,128)(2,1)S(1)} %bitcast.68), channel_id=1, source_target_pairs={{0,8},{8,0},{16,24},{24,16},{1,9},{9,1},{17,25},{25,17},{2,10},{10... | collective-permute-start | bytes 1572872 | tf_op jit(solution)/shard_map/ppermute | solution.py:26
  32.2 12.5 %collective-permute-start.8 = (bf16[4,64,1024]{2,1,0:T(8,128)(2,1)S(1)}, bf16[4,64,1024]{2,1,0:T(8,128)(2,1)}, u32[]{:S(2)}, u32[]{:S(2)}) collective-permute-start(bf16[4,64,1024]{2,1,0:T(8,128)(2,1)S(1)} %append.15.refs_0_), channel_id=1, source_target_pairs={{0,2},{1,3},{2,0},{3,1},{4,6},{5,7},{6,4},{7,5},{8,10},{9,11},{10,... | collective-permute-start | bytes 1572872 | tf_op jit(solution)/shard_map/ppermute | solution.py:26
  32.3 13.3 %collective-permute-start.7 = (bf16[256,1024]{1,0:T(8,128)(2,1)S(1)}, bf16[256,1024]{1,0:T(8,128)(2,1)S(1)}, u32[]{:S(2)}, u32[]{:S(2)}) collective-permute-start(bf16[256,1024]{1,0:T(8,128)(2,1)S(1)} %collective-permute-done.6.x2), channel_id=1, source_target_pairs={{0,8},{8,0},{16,24},{24,16},{1,9},{9,1},{17,25},{25,17},{2,10},{10... | collective-permute-start | bytes 1572872 | tf_op jit(solution)/shard_map/ppermute | solution.py:26
  44.7 17.7 %collective-permute-start.18 = (bf16[2,64,1024]{2,1,0:T(8,128)(2,1)}, bf16[2,64,1024]{2,1,0:T(8,128)(2,1)}, u32[]{:S(2)}, u32[]{:S(2)}) collective-permute-start(bf16[2,64,1024]{2,1,0:T(8,128)(2,1)} %append.17.a_ref), channel_id=1, source_target_pairs={{0,4},{1,5},{2,6},{3,7},{4,0},{5,1},{6,2},{7,3},{8,12},{9,13},{10,... | collective-permute-start | bytes 786440 | tf_op jit(solution)/shard_map/ppermute | solution.py:26
  52.7 10.7 %collective-permute-start.16 = (f32[16,4,128]{2,1,0:T(4,128)}, f32[16,4,128]{2,1,0:T(4,128)S(1)}, u32[]{:S(2)}, u32[]{:S(2)}) collective-permute-start(f32[16,4,128]{2,1,0:T(4,128)} %multiply_add_fusion.7), channel_id=1, source_target_pairs={{0,2},{1,3},{2,4},{3,5},{4,6},{5,7},{8,10},{9,11},{10,12},{11,13},... | collective-permute-start | bytes 98312 | tf_op jit(solution)/shard_map/ppermute | solution.py:1226
  69.8 13.2 %collective-permute-start.9 = (bf16[4,64,1024]{2,1,0:T(8,128)(2,1)S(1)}, bf16[4,64,1024]{2,1,0:T(8,128)(2,1)S(1)}, u32[]{:S(2)}, u32[]{:S(2)}) collective-permute-start(bf16[4,64,1024]{2,1,0:T(8,128)(2,1)S(1)} %append.15.refs_0_), channel_id=1, source_target_pairs={{0,16},{8,24},{16,0},{24,8},{1,17},{9,25},{17,1},{25,9},{2,18},{10... | collective-permute-start | bytes 1572872 | tf_op jit(solution)/shard_map/ppermute | solution.py:26
  71.3 25.3 %collective-permute-start.11 = (bf16[1,64,1024]{2,1,0:T(8,128)(2,1)}, bf16[1,64,1024]{2,1,0:T(8,128)(2,1)}, u32[]{:S(2)}, u32[]{:S(2)}) collective-permute-start(bf16[1,64,1024]{2,1,0:T(8,128)(2,1)} %bitcast.102), channel_id=1, source_target_pairs={{0,1},{1,0},{2,3},{3,2},{4,5},{5,4},{6,7},{7,6},{8,9},{9,8},{10,11... | collective-permute-start | bytes 393224 | tf_op jit(solution)/shard_map/ppermute | solution.py:26
  72.6 21.5 %collective-permute-start.10 = (bf16[4,64,1024]{2,1,0:T(8,128)(2,1)}, bf16[4,64,1024]{2,1,0:T(8,128)(2,1)S(1)}, u32[]{:S(2)}, u32[]{:S(2)}) collective-permute-start(bf16[4,64,1024]{2,1,0:T(8,128)(2,1)} %collective-permute-done.8.refs_1_), channel_id=1, source_target_pairs={{0,16},{8,24},{16,0},{24,8},{1,17},{9,25},{17,1},{25,9},{2,18},{10... | collective-permute-start | bytes 1572872 | tf_op jit(solution)/shard_map/ppermute | solution.py:26
  75.6 23.6 %collective-permute-start.23 = (bf16[4,64,1024]{2,1,0:T(8,128)(2,1)S(1)}, bf16[4,64,1024]{2,1,0:T(8,128)(2,1)}, u32[]{:S(2)}, u32[]{:S(2)}) collective-permute-start(bf16[4,64,1024]{2,1,0:T(8,128)(2,1)S(1)} %append.18.refs_0_), channel_id=1, source_target_pairs={{0,2},{1,3},{2,0},{3,1},{4,6},{5,7},{6,4},{7,5},{8,10},{9,11},{10,... | collective-permute-start | bytes 1572872 | tf_op jit(solution)/shard_map/ppermute | solution.py:26
  85.7 13.4 %collective-permute-start.20 = (bf16[256,256]{1,0:T(8,128)(2,1)}, bf16[256,256]{1,0:T(8,128)(2,1)}, u32[]{:S(2)}, u32[]{:S(2)}) collective-permute-start(bf16[256,256]{1,0:T(8,128)(2,1)} %get-tuple-element.206), channel_id=1, source_target_pairs={{0,2},{1,3},{2,4},{3,5},{4,6},{5,7},{8,10},{9,11},{10,12},{11,13},... | collective-permute-start | bytes 393224 | tf_op jit(solution)/shard_map/ppermute | solution.py:1245
  94.9 19.5 %collective-permute-start.22 = (bf16[4,64,1024]{2,1,0:T(8,128)(2,1)S(1)}, bf16[4,64,1024]{2,1,0:T(8,128)(2,1)}, u32[]{:S(2)}, u32[]{:S(2)}) collective-permute-start(bf16[4,64,1024]{2,1,0:T(8,128)(2,1)S(1)} %append.18.refs_0_), channel_id=1, source_target_pairs={{0,16},{8,24},{16,0},{24,8},{1,17},{9,25},{17,1},{25,9},{2,18},{10... | collective-permute-start | bytes 1572872 | tf_op jit(solution)/shard_map/ppermute | solution.py:26
  99.1 17.0 %collective-permute-start.21 = (bf16[2,64,1024]{2,1,0:T(8,128)(2,1)}, bf16[2,64,1024]{2,1,0:T(8,128)(2,1)}, u32[]{:S(2)}, u32[]{:S(2)}) collective-permute-start(bf16[2,64,1024]{2,1,0:T(8,128)(2,1)} %append.16.a_ref), channel_id=1, source_target_pairs={{0,4},{1,5},{2,6},{3,7},{4,0},{5,1},{6,2},{7,3},{8,12},{9,13},{10,... | collective-permute-start | bytes 786440 | tf_op jit(solution)/shard_map/ppermute | solution.py:26
  101.8 14.6 %collective-permute-start.24 = (bf16[256,256]{1,0:T(8,128)(2,1)S(1)}, bf16[256,256]{1,0:T(8,128)(2,1)}, u32[]{:S(2)}, u32[]{:S(2)}) collective-permute-start(bf16[256,256]{1,0:T(8,128)(2,1)S(1)} %broadcast_select_fusion.c0), channel_id=1, source_target_pairs={{0,8},{8,0},{16,24},{24,16},{1,9},{9,1},{17,25},{25,17},{2,10},{10... | collective-permute-start | bytes 393224 | tf_op jit(solution)/shard_map/ppermute | solution.py:26
  104.5 13.4 %collective-permute-start.26 = (bf16[256,256]{1,0:T(8,128)(2,1)}, bf16[256,256]{1,0:T(8,128)(2,1)}, u32[]{:S(2)}, u32[]{:S(2)}) collective-permute-start(bf16[256,256]{1,0:T(8,128)(2,1)} %collective-permute-done.25.c2), channel_id=1, source_target_pairs={{0,8},{8,0},{16,24},{24,16},{1,9},{9,1},{17,25},{25,17},{2,10},{10... | collective-permute-start | bytes 393224 | tf_op jit(solution)/shard_map/ppermute | solution.py:26
  108.0 20.6 %collective-permute-start.27 = (bf16[256,1024]{1,0:T(8,128)(2,1)S(1)}, bf16[256,1024]{1,0:T(8,128)(2,1)S(1)}, u32[]{:S(2)}, u32[]{:S(2)}) collective-permute-start(bf16[256,1024]{1,0:T(8,128)(2,1)S(1)} %bitcast.73), channel_id=1, source_target_pairs={{0,1},{1,0},{2,3},{3,2},{4,5},{5,4},{6,7},{7,6},{8,9},{9,8},{10,11... | collective-permute-start | bytes 1572872 | tf_op jit(solution)/shard_map/ppermute | solution.py:26
  114.5 17.8 %collective-permute-start.30 = (bf16[256,256]{1,0:T(8,128)(2,1)S(1)}, bf16[256,256]{1,0:T(8,128)(2,1)S(1)}, u32[]{:S(2)}, u32[]{:S(2)}) collective-permute-start(bf16[256,256]{1,0:T(8,128)(2,1)S(1)} %get-tuple-element.221), channel_id=1, source_target_pairs={{0,8},{8,0},{16,24},{24,16},{1,9},{9,1},{17,25},{25,17},{2,10},{10... | collective-permute-start | bytes 393224 | tf_op jit(solution)/shard_map/ppermute | solution.py:26
  116.1 16.1 %collective-permute-start.31 = (bf16[256,256]{1,0:T(8,128)(2,1)S(1)}, bf16[256,256]{1,0:T(8,128)(2,1)S(1)}, u32[]{:S(2)}, u32[]{:S(2)}) collective-permute-start(bf16[256,256]{1,0:T(8,128)(2,1)S(1)} %get-tuple-element.222), channel_id=1, source_target_pairs={{0,1},{1,0},{2,3},{3,2},{4,5},{5,4},{6,7},{7,6},{8,9},{9,8},{10,11... | collective-permute-start | bytes 393224 | tf_op jit(solution)/shard_map/ppermute | solution.py:26
  116.4 15.8 %collective-permute-start.32 = (bf16[256,256]{1,0:T(8,128)(2,1)S(1)}, bf16[256,256]{1,0:T(8,128)(2,1)S(1)}, u32[]{:S(2)}, u32[]{:S(2)}) collective-permute-start(bf16[256,256]{1,0:T(8,128)(2,1)S(1)} %get-tuple-element.223), channel_id=1, source_target_pairs={{0,9},{1,8},{2,11},{3,10},{4,13},{5,12},{6,15},{7,14},{8,1},{9,0},... | collective-permute-start | bytes 393224 | tf_op jit(solution)/shard_map/ppermute | solution.py:36
  117.9 14.3 %collective-permute-start.29 = (bf16[2,64,1024]{2,1,0:T(8,128)(2,1)S(1)}, bf16[2,64,1024]{2,1,0:T(8,128)(2,1)S(1)}, u32[]{:S(2)}, u32[]{:S(2)}) collective-permute-start(bf16[2,64,1024]{2,1,0:T(8,128)(2,1)S(1)} %append.19.a_ref), channel_id=1, source_target_pairs={{0,4},{1,5},{2,6},{3,7},{4,0},{5,1},{6,2},{7,3},{8,12},{9,13},{10,... | collective-permute-start | bytes 786440 | tf_op jit(solution)/shard_map/ppermute | solution.py:26
  135.2 18.4 %collective-permute-start.40 = (bf16[4,64,1024]{2,1,0:T(8,128)(2,1)}, bf16[4,64,1024]{2,1,0:T(8,128)(2,1)S(1)}, u32[]{:S(2)}, u32[]{:S(2)}) collective-permute-start(bf16[4,64,1024]{2,1,0:T(8,128)(2,1)} %collective-permute-done.23.refs_1_), channel_id=1, source_target_pairs={{0,16},{8,24},{16,0},{24,8},{1,17},{9,25},{17,1},{25,9},{2,18},{10... | collective-permute-start | bytes 1572872 | tf_op jit(solution)/shard_map/ppermute | solution.py:26
  135.4 18.1 %collective-permute-start.39 = (bf16[4,64,1024]{2,1,0:T(8,128)(2,1)S(1)}, bf16[4,64,1024]{2,1,0:T(8,128)(2,1)S(1)}, u32[]{:S(2)}, u32[]{:S(2)}) collective-permute-start(bf16[4,64,1024]{2,1,0:T(8,128)(2,1)S(1)} %append.20.refs_0_), channel_id=1, source_target_pairs={{0,2},{1,3},{2,0},{3,1},{4,6},{5,7},{6,4},{7,5},{8,10},{9,11},{10,... | collective-permute-start | bytes 1572872 | tf_op jit(solution)/shard_map/ppermute | solution.py:26
  135.4 18.1 %collective-permute-start.33 = (bf16[256,1024]{1,0:T(8,128)(2,1)S(1)}, bf16[256,1024]{1,0:T(8,128)(2,1)S(1)}, u32[]{:S(2)}, u32[]{:S(2)}) collective-permute-start(bf16[256,1024]{1,0:T(8,128)(2,1)S(1)} %get-tuple-element.225), channel_id=1, source_target_pairs={{0,8},{8,0},{16,24},{24,16},{1,9},{9,1},{17,25},{25,17},{2,10},{10... | collective-permute-start | bytes 1572872 | tf_op jit(solution)/shard_map/ppermute | solution.py:26
  135.9 17.7 %collective-permute-start.35 = (bf16[256,1024]{1,0:T(8,128)(2,1)S(1)}, bf16[256,1024]{1,0:T(8,128)(2,1)S(1)}, u32[]{:S(2)}, u32[]{:S(2)}) collective-permute-start(bf16[256,1024]{1,0:T(8,128)(2,1)S(1)} %far_sum.5), channel_id=1, source_target_pairs={{0,1},{1,0},{2,3},{3,2},{4,5},{5,4},{6,7},{7,6},{8,9},{9,8},{10,11... | collective-permute-start | bytes 1572872 | tf_op jit(solution)/shard_map/ppermute | solution.py:26
  137.7 12.0 %collective-permute-start.37 = (f32[16,256]{1,0:T(8,128)S(1)}, f32[16,256]{1,0:T(8,128)S(1)}, u32[]{:S(2)}, u32[]{:S(2)}) collective-permute-start(f32[16,256]{1,0:T(8,128)S(1)} %get-tuple-element.230), channel_id=1, source_target_pairs={{0,1},{1,0},{2,3},{3,2},{4,5},{5,4},{6,7},{7,6},{8,9},{9,8},{10,11... | collective-permute-start | bytes 49160 | tf_op jit(solution)/shard_map/ppermute | solution.py:26
  154.3 12.4 %collective-permute-start.42 = (bf16[256,1024]{1,0:T(8,128)(2,1)S(1)}, bf16[256,1024]{1,0:T(8,128)(2,1)S(1)}, u32[]{:S(2)}, u32[]{:S(2)}) collective-permute-start(bf16[256,1024]{1,0:T(8,128)(2,1)S(1)} %get-tuple-element.237.m0.x0), channel_id=1, source_target_pairs={{0,1},{1,0},{2,3},{3,2},{4,5},{5,4},{6,7},{7,6},{8,9},{9,8},{10,11... | collective-permute-start | bytes 1572872 | tf_op jit(solution)/shard_map/ppermute | solution.py:26
  155.4 14.6 %collective-permute-start.46 = (bf16[4,64,1024]{2,1,0:T(8,128)(2,1)S(1)}, bf16[4,64,1024]{2,1,0:T(8,128)(2,1)S(1)}, u32[]{:S(2)}, u32[]{:S(2)}) collective-permute-start(bf16[4,64,1024]{2,1,0:T(8,128)(2,1)S(1)} %append.21.refs_2_), channel_id=1, source_target_pairs={{0,2},{1,3},{2,0},{3,1},{4,6},{5,7},{6,4},{7,5},{8,10},{9,11},{10,... | collective-permute-start | bytes 1572872 | tf_op jit(solution)/shard_map/ppermute | solution.py:26
  157.2 13.5 %collective-permute-start.44 = (bf16[256,1024]{1,0:T(8,128)(2,1)S(1)}, bf16[256,1024]{1,0:T(8,128)(2,1)S(1)}, u32[]{:S(2)}, u32[]{:S(2)}) collective-permute-start(bf16[256,1024]{1,0:T(8,128)(2,1)S(1)} %bitcast.74), channel_id=1, source_target_pairs={{0,8},{8,0},{16,24},{24,16},{1,9},{9,1},{17,25},{25,17},{2,10},{10... | collective-permute-start | bytes 1572872 | tf_op jit(solution)/shard_map/ppermute | solution.py:26
  158.2 12.6 %collective-permute-start.45 = (bf16[256,1024]{1,0:T(8,128)(2,1)S(1)}, bf16[256,1024]{1,0:T(8,128)(2,1)S(1)}, u32[]{:S(2)}, u32[]{:S(2)}) collective-permute-start(bf16[256,1024]{1,0:T(8,128)(2,1)S(1)} %collective-permute-done.27.g2.y2), channel_id=1, source_target_pairs={{0,8},{8,0},{16,24},{24,16},{1,9},{9,1},{17,25},{25,17},{2,10},{10... | collective-permute-start | bytes 1572872 | tf_op jit(solution)/shard_map/ppermute | solution.py:26
  158.2 12.6 %collective-permute-start.41 = (bf16[256,1024]{1,0:T(8,128)(2,1)S(1)}, bf16[256,1024]{1,0:T(8,128)(2,1)S(1)}, u32[]{:S(2)}, u32[]{:S(2)}) collective-permute-start(bf16[256,1024]{1,0:T(8,128)(2,1)S(1)} %get-tuple-element.237.m0.x0), channel_id=1, source_target_pairs={{0,8},{8,0},{16,24},{24,16},{1,9},{9,1},{17,25},{25,17},{2,10},{10... | collective-permute-start | bytes 1572872 | tf_op jit(solution)/shard_map/ppermute | solution.py:26
  185.8 13.1 %collective-permute-start.50 = (bf16[4,64,1024]{2,1,0:T(8,128)(2,1)S(1)}, bf16[4,64,1024]{2,1,0:T(8,128)(2,1)S(1)}, u32[]{:S(2)}, u32[]{:S(2)}) collective-permute-start(bf16[4,64,1024]{2,1,0:T(8,128)(2,1)S(1)} %get-tuple-element.241), channel_id=1, source_target_pairs={{0,16},{8,24},{16,0},{24,8},{1,17},{9,25},{17,1},{25,9},{2,18},{10... | collective-permute-start | bytes 1572872 | tf_op jit(solution)/shard_map/ppermute | solution.py:26
  187.2 11.8 %collective-permute-start.53 = (bf16[256,1024]{1,0:T(8,128)(2,1)S(1)}, bf16[256,1024]{1,0:T(8,128)(2,1)S(1)}, u32[]{:S(2)}, u32[]{:S(2)}) collective-permute-start(bf16[256,1024]{1,0:T(8,128)(2,1)S(1)} %get-tuple-element.257), channel_id=1, source_target_pairs={{0,8},{8,0},{16,24},{24,16},{1,9},{9,1},{17,25},{25,17},{2,10},{10... | collective-permute-start | bytes 1572872 | tf_op jit(solution)/shard_map/ppermute | solution.py:26
  188.1 13.6 %collective-permute-start.54 = (bf16[256,1024]{1,0:T(8,128)(2,1)S(1)}, bf16[256,1024]{1,0:T(8,128)(2,1)S(1)}, u32[]{:S(2)}, u32[]{:S(2)}) collective-permute-start(bf16[256,1024]{1,0:T(8,128)(2,1)S(1)} %far_sum.6), channel_id=1, source_target_pairs={{0,1},{1,0},{2,3},{3,2},{4,5},{5,4},{6,7},{7,6},{8,9},{9,8},{10,11... | collective-permute-start | bytes 1572872 | tf_op jit(solution)/shard_map/ppermute | solution.py:26
  203.4 12.7 %collective-permute-start.56 = (bf16[256,1024]{1,0:T(8,128)(2,1)S(1)}, bf16[256,1024]{1,0:T(8,128)(2,1)S(1)}, u32[]{:S(2)}, u32[]{:S(2)}) collective-permute-start(bf16[256,1024]{1,0:T(8,128)(2,1)S(1)} %get-tuple-element.264.h0), channel_id=1, source_target_pairs={{0,1},{1,0},{2,3},{3,2},{4,5},{5,4},{6,7},{7,6},{8,9},{9,8},{10,11... | collective-permute-start | bytes 1572872 | tf_op jit(solution)/shard_map/ppermute | solution.py:26
  204.3 13.6 %collective-permute-start.52 = (bf16[4,64,1024]{2,1,0:T(8,128)(2,1)S(1)}, bf16[4,64,1024]{2,1,0:T(8,128)(2,1)S(1)}, u32[]{:S(2)}, u32[]{:S(2)}) collective-permute-start(bf16[4,64,1024]{2,1,0:T(8,128)(2,1)S(1)} %leave_sum.3), channel_id=1, source_target_pairs={{0,2},{1,3},{2,0},{3,1},{4,6},{5,7},{6,4},{7,5},{8,10},{9,11},{10,... | collective-permute-start | bytes 1572872 | tf_op jit(solution)/shard_map/ppermute | solution.py:26
  206.0 12.1 %collective-permute-start.49 = (bf16[4,64,1024]{2,1,0:T(8,128)(2,1)S(1)}, bf16[4,64,1024]{2,1,0:T(8,128)(2,1)S(1)}, u32[]{:S(2)}, u32[]{:S(2)}) collective-permute-start(bf16[4,64,1024]{2,1,0:T(8,128)(2,1)S(1)} %get-tuple-element.249), channel_id=1, source_target_pairs={{0,16},{8,24},{16,0},{24,8},{1,17},{9,25},{17,1},{25,9},{2,18},{10... | collective-permute-start | bytes 1572872 | tf_op jit(solution)/shard_map/ppermute | solution.py:26
  206.3 12.1 %collective-permute-start.55 = (bf16[256,1024]{1,0:T(8,128)(2,1)S(1)}, bf16[256,1024]{1,0:T(8,128)(2,1)S(1)}, u32[]{:S(2)}, u32[]{:S(2)}) collective-permute-start(bf16[256,1024]{1,0:T(8,128)(2,1)S(1)} %get-tuple-element.264.h0), channel_id=1, source_target_pairs={{0,8},{8,0},{16,24},{24,16},{1,9},{9,1},{17,25},{25,17},{2,10},{10... | collective-permute-start | bytes 1572872 | tf_op jit(solution)/shard_map/ppermute | solution.py:26
  217.7 13.6 %collective-permute-start.58 = (bf16[4,64,1024]{2,1,0:T(8,128)(2,1)S(1)}, bf16[4,64,1024]{2,1,0:T(8,128)(2,1)S(1)}, u32[]{:S(2)}, u32[]{:S(2)}) collective-permute-start(bf16[4,64,1024]{2,1,0:T(8,128)(2,1)S(1)} %get-tuple-element.243), channel_id=1, source_target_pairs={{0,16},{8,24},{16,0},{24,8},{1,17},{9,25},{17,1},{25,9},{2,18},{10... | collective-permute-start | bytes 1572872 | tf_op jit(solution)/shard_map/ppermute | solution.py:26
  236.5 14.1 %collective-permute-start.59 = (bf16[256,256]{1,0:T(8,128)(2,1)S(1)}, bf16[256,256]{1,0:T(8,128)(2,1)S(1)}, u32[]{:S(2)}, u32[]{:S(2)}) collective-permute-start(bf16[256,256]{1,0:T(8,128)(2,1)S(1)} %get-tuple-element.275), channel_id=1, source_target_pairs={{0,8},{8,0},{16,24},{24,16},{1,9},{9,1},{17,25},{25,17},{2,10},{10... | collective-permute-start | bytes 393224 | tf_op jit(solution)/shard_map/ppermute | solution.py:26
  236.6 14.1 %collective-permute-start.61 = (bf16[256,256]{1,0:T(8,128)(2,1)S(1)}, bf16[256,256]{1,0:T(8,128)(2,1)S(1)}, u32[]{:S(2)}, u32[]{:S(2)}) collective-permute-start(bf16[256,256]{1,0:T(8,128)(2,1)S(1)} %far_sum.7), channel_id=1, source_target_pairs={{0,1},{1,0},{2,3},{3,2},{4,5},{5,4},{6,7},{7,6},{8,9},{9,8},{10,11... | collective-permute-start | bytes 393224 | tf_op jit(solution)/shard_map/ppermute | solution.py:26
  262.9 15.6 %collective-permute-start.72 = (bf16[4,64,1024]{2,1,0:T(8,128)(2,1)}, bf16[4,64,1024]{2,1,0:T(8,128)(2,1)}, u32[]{:S(2)}, u32[]{:S(2)}) collective-permute-start(bf16[4,64,1024]{2,1,0:T(8,128)(2,1)} %leave_sum.4), channel_id=1, source_target_pairs={{0,2},{1,3},{2,0},{3,1},{4,6},{5,7},{6,4},{7,5},{8,10},{9,11},{10,... | collective-permute-start | bytes 1572872 | tf_op jit(solution)/shard_map/ppermute | solution.py:26
  265.4 13.5 %collective-permute-start.71 = (bf16[4,64,1024]{2,1,0:T(8,128)(2,1)}, bf16[4,64,1024]{2,1,0:T(8,128)(2,1)}, u32[]{:S(2)}, u32[]{:S(2)}) collective-permute-start(bf16[4,64,1024]{2,1,0:T(8,128)(2,1)} %get-tuple-element.295), channel_id=1, source_target_pairs={{0,16},{8,24},{16,0},{24,8},{1,17},{9,25},{17,1},{25,9},{2,18},{10... | collective-permute-start | bytes 1572872 | tf_op jit(solution)/shard_map/ppermute | solution.py:26
  265.6 24.4 %collective-permute-start.70 = (bf16[4,64,1024]{2,1,0:T(8,128)(2,1)}, bf16[4,64,1024]{2,1,0:T(8,128)(2,1)}, u32[]{:S(2)}, u32[]{:S(2)}) collective-permute-start(bf16[4,64,1024]{2,1,0:T(8,128)(2,1)} %get-tuple-element.281), channel_id=1, source_target_pairs={{0,16},{8,24},{16,0},{24,8},{1,17},{9,25},{17,1},{25,9},{2,18},{10... | collective-permute-start | bytes 1572872 | tf_op jit(solution)/shard_map/ppermute | solution.py:26
  273.4 63.5 %collective-permute-start.48 = (bf16[256,1024]{1,0:T(8,128)(2,1)}, bf16[256,1024]{1,0:T(8,128)(2,1)}, u32[]{:S(2)}, u32[]{:S(2)}) collective-permute-start(bf16[256,1024]{1,0:T(8,128)(2,1)} %copy-done.73), channel_id=1, source_target_pairs={{0,8},{8,0},{16,24},{24,16},{1,9},{9,1},{17,25},{25,17},{2,10},{10... | collective-permute-start | bytes 1572872 | tf_op jit(solution)/shard_map/ppermute | solution.py:26
  277.8 16.1 %collective-permute-start.69 = (bf16[2,64,1024]{2,1,0:T(8,128)(2,1)}, bf16[2,64,1024]{2,1,0:T(8,128)(2,1)S(1)}, u32[]{:S(2)}, u32[]{:S(2)}) collective-permute-start(bf16[2,64,1024]{2,1,0:T(8,128)(2,1)} %copy-done.77), channel_id=1, source_target_pairs={{0,4},{1,5},{2,6},{3,7},{4,0},{5,1},{6,2},{7,3},{8,12},{9,13},{10,... | collective-permute-start | bytes 786440 | tf_op jit(solution)/shard_map/ppermute | solution.py:26
  278.6 38.3 %collective-permute-start.79 = (bf16[4,64,1024]{2,1,0:T(8,128)(2,1)}, bf16[4,64,1024]{2,1,0:T(8,128)(2,1)S(1)}, u32[]{:S(2)}, u32[]{:S(2)}) collective-permute-start(bf16[4,64,1024]{2,1,0:T(8,128)(2,1)} %copy-done.76), channel_id=1, source_target_pairs={{0,16},{8,24},{16,0},{24,8},{1,17},{9,25},{17,1},{25,9},{2,18},{10... | collective-permute-start | bytes 1572872 | tf_op jit(solution)/shard_map/ppermute | solution.py:26
  291.3 24.0 %collective-permute-start.80 = (bf16[4,64,1024]{2,1,0:T(8,128)(2,1)S(1)}, bf16[4,64,1024]{2,1,0:T(8,128)(2,1)S(1)}, u32[]{:S(2)}, u32[]{:S(2)}) collective-permute-start(bf16[4,64,1024]{2,1,0:T(8,128)(2,1)S(1)} %leave_sum.5), channel_id=1, source_target_pairs={{0,2},{1,3},{2,0},{3,1},{4,6},{5,7},{6,4},{7,5},{8,10},{9,11},{10,... | collective-permute-start | bytes 1572872 | tf_op jit(solution)/shard_map/ppermute | solution.py:26
  291.8 22.1 %collective-permute-start.81 = (bf16[2,64,1024]{2,1,0:T(8,128)(2,1)S(1)}, bf16[2,64,1024]{2,1,0:T(8,128)(2,1)S(1)}, u32[]{:S(2)}, u32[]{:S(2)}) collective-permute-start(bf16[2,64,1024]{2,1,0:T(8,128)(2,1)S(1)} %get-tuple-element.297), channel_id=1, source_target_pairs={{0,4},{1,5},{2,6},{3,7},{4,0},{5,1},{6,2},{7,3},{8,12},{9,13},{10,... | collective-permute-start | bytes 786440 | tf_op jit(solution)/shard_map/ppermute | solution.py:26
  310.6 22.4 %collective-permute-start.74 = (bf16[256,1024]{1,0:T(8,128)(2,1)}, bf16[256,1024]{1,0:T(8,128)(2,1)}, u32[]{:S(2)}, u32[]{:S(2)}) collective-permute-start(bf16[256,1024]{1,0:T(8,128)(2,1)} %get-tuple-element.311), channel_id=1, source_target_pairs={{0,8},{8,0},{16,24},{24,16},{1,9},{9,1},{17,25},{25,17},{2,10},{10... | collective-permute-start | bytes 1572872 | tf_op jit(solution)/shard_map/ppermute | solution.py:26
  313.9 29.0 %collective-permute-start.47 = (bf16[256,1024]{1,0:T(8,128)(2,1)}, bf16[256,1024]{1,0:T(8,128)(2,1)S(1)}, u32[]{:S(2)}, u32[]{:S(2)}) collective-permute-start(bf16[256,1024]{1,0:T(8,128)(2,1)} %get-tuple-element.246), channel_id=1, source_target_pairs={{0,8},{8,0},{16,24},{24,16},{1,9},{9,1},{17,25},{25,17},{2,10},{10... | collective-permute-start | bytes 1572872 | tf_op jit(solution)/shard_map/ppermute | solution.py:26
  317.7 13.9 %collective-permute-start.82 = (bf16[2,64,1024]{2,1,0:T(8,128)(2,1)}, bf16[2,64,1024]{2,1,0:T(8,128)(2,1)}, u32[]{:S(2)}, u32[]{:S(2)}) collective-permute-start(bf16[2,64,1024]{2,1,0:T(8,128)(2,1)} %get-tuple-element.322), channel_id=1, source_target_pairs={{0,4},{1,5},{2,6},{3,7},{4,0},{5,1},{6,2},{7,3},{8,12},{9,13},{10,... | collective-permute-start | bytes 786440 | tf_op jit(solution)/shard_map/ppermute | solution.py:26
  320.8 15.2 %collective-permute-start.86 = (bf16[1,64,1024]{2,1,0:T(8,128)(2,1)}, bf16[1,64,1024]{2,1,0:T(8,128)(2,1)}, u32[]{:S(2)}, u32[]{:S(2)}) collective-permute-start(bf16[1,64,1024]{2,1,0:T(8,128)(2,1)} %get-tuple-element.319), channel_id=1, source_target_pairs={{0,1},{1,0},{2,3},{3,2},{4,5},{5,4},{6,7},{7,6},{8,9},{9,8},{10,11... | collective-permute-start | bytes 393224 | tf_op jit(solution)/shard_map/ppermute | solution.py:26
  331.7 12.5 %collective-permute-start.77 = (bf16[2,64,1024]{2,1,0:T(8,128)(2,1)S(1)}, bf16[2,64,1024]{2,1,0:T(8,128)(2,1)S(1)}, u32[]{:S(2)}, u32[]{:S(2)}) collective-permute-start(bf16[2,64,1024]{2,1,0:T(8,128)(2,1)S(1)} %append.22.a_ref), channel_id=1, source_target_pairs={{0,16},{8,24},{16,0},{24,8},{1,17},{9,25},{17,1},{25,9},{2,18},{10... | collective-permute-start | bytes 786440 | tf_op jit(solution)/shard_map/ppermute | solution.py:26
  336.9 13.4 %collective-permute-start.87 = (bf16[2,64,1024]{2,1,0:T(8,128)(2,1)S(1)}, bf16[2,64,1024]{2,1,0:T(8,128)(2,1)S(1)}, u32[]{:S(2)}, u32[]{:S(2)}) collective-permute-start(bf16[2,64,1024]{2,1,0:T(8,128)(2,1)S(1)} %append.26.a_ref), channel_id=1, source_target_pairs={{0,16},{8,24},{16,0},{24,8},{1,17},{9,25},{17,1},{25,9},{2,18},{10... | collective-permute-start | bytes 786440 | tf_op jit(solution)/shard_map/ppermute | solution.py:26
  339.4 17.2 %collective-permute-start.65 = (bf16[256,1024]{1,0:T(8,128)(2,1)S(1)}, bf16[256,1024]{1,0:T(8,128)(2,1)S(1)}, u32[]{:S(2)}, u32[]{:S(2)}) collective-permute-start(bf16[256,1024]{1,0:T(8,128)(2,1)S(1)} %far_sum.8), channel_id=1, source_target_pairs={{0,1},{1,0},{2,3},{3,2},{4,5},{5,4},{6,7},{7,6},{8,9},{9,8},{10,11... | collective-permute-start | bytes 1572872 | tf_op jit(solution)/shard_map/ppermute | solution.py:26
  341.7 13.7 %collective-permute-start.84 = (bf16[2,64,1024]{2,1,0:T(8,128)(2,1)S(1)}, bf16[2,64,1024]{2,1,0:T(8,128)(2,1)S(1)}, u32[]{:S(2)}, u32[]{:S(2)}) collective-permute-start(bf16[2,64,1024]{2,1,0:T(8,128)(2,1)S(1)} %append.24.a_ref), channel_id=1, source_target_pairs={{0,16},{8,24},{16,0},{24,8},{1,17},{9,25},{17,1},{25,9},{2,18},{10... | collective-permute-start | bytes 786440 | tf_op jit(solution)/shard_map/ppermute | solution.py:26
  344.2 13.1 %collective-permute-start.73 = (bf16[256,1024]{1,0:T(8,128)(2,1)S(1)}, bf16[256,1024]{1,0:T(8,128)(2,1)S(1)}, u32[]{:S(2)}, u32[]{:S(2)}) collective-permute-start(bf16[256,1024]{1,0:T(8,128)(2,1)S(1)} %copy-done.75), channel_id=1, source_target_pairs={{0,8},{8,0},{16,24},{24,16},{1,9},{9,1},{17,25},{25,17},{2,10},{10... | collective-permute-start | bytes 1572872 | tf_op jit(solution)/shard_map/ppermute | solution.py:26
  347.4 10.7 %collective-permute-start.78 = (bf16[4,64,1024]{2,1,0:T(8,128)(2,1)S(1)}, bf16[4,64,1024]{2,1,0:T(8,128)(2,1)}, u32[]{:S(2)}, u32[]{:S(2)}) collective-permute-start(bf16[4,64,1024]{2,1,0:T(8,128)(2,1)S(1)} %append.23.mine_ref), channel_id=1, source_target_pairs={{0,8},{8,0},{16,24},{24,16},{1,9},{9,1},{17,25},{25,17},{2,10},{10... | collective-permute-start | bytes 1572872 | tf_op jit(solution)/shard_map/ppermute | solution.py:26
  353.9 25.2 %collective-permute-start.75 = (bf16[256,1024]{1,0:T(8,128)(2,1)}, bf16[256,1024]{1,0:T(8,128)(2,1)}, u32[]{:S(2)}, u32[]{:S(2)}) collective-permute-start(bf16[256,1024]{1,0:T(8,128)(2,1)} %far_sum.9), channel_id=1, source_target_pairs={{0,1},{1,0},{2,3},{3,2},{4,5},{5,4},{6,7},{7,6},{8,9},{9,8},{10,11... | collective-permute-start | bytes 1572872 | tf_op jit(solution)/shard_map/ppermute | solution.py:26
  355.4 26.1 %collective-permute-start.88 = (bf16[4,64,1024]{2,1,0:T(8,128)(2,1)}, bf16[4,64,1024]{2,1,0:T(8,128)(2,1)}, u32[]{:S(2)}, u32[]{:S(2)}) collective-permute-start(bf16[4,64,1024]{2,1,0:T(8,128)(2,1)} %append.27.mine_ref), channel_id=1, source_target_pairs={{0,8},{8,0},{16,24},{24,16},{1,9},{9,1},{17,25},{25,17},{2,10},{10... | collective-permute-start | bytes 1572872 | tf_op jit(solution)/shard_map/ppermute | solution.py:26
  357.3 31.4 %collective-permute-start.85 = (bf16[4,64,1024]{2,1,0:T(8,128)(2,1)S(1)}, bf16[4,64,1024]{2,1,0:T(8,128)(2,1)}, u32[]{:S(2)}, u32[]{:S(2)}) collective-permute-start(bf16[4,64,1024]{2,1,0:T(8,128)(2,1)S(1)} %append.25.mine_ref), channel_id=1, source_target_pairs={{0,8},{8,0},{16,24},{24,16},{1,9},{9,1},{17,25},{25,17},{2,10},{10... | collective-permute-start | bytes 1572872 | tf_op jit(solution)/shard_map/ppermute | solution.py:26
  358.2 26.2 %collective-permute-start.92 = (f32[176,128]{1,0:T(8,128)S(1)}, f32[176,128]{1,0:T(8,128)}, u32[]{:S(2)}, u32[]{:S(2)}) collective-permute-start(f32[176,128]{1,0:T(8,128)S(1)} %pad_maximum_fusion.2.p0), channel_id=1, source_target_pairs={{0,8},{8,0},{16,24},{24,16},{1,9},{9,1},{17,25},{25,17},{2,10},{10... | collective-permute-start | bytes 270344 | tf_op jit(solution)/shard_map/ppermute | solution.py:26
  368.9 15.5 %collective-permute-start.94 = (f32[176,128]{1,0:T(8,128)S(1)}, f32[176,128]{1,0:T(8,128)}, u32[]{:S(2)}, u32[]{:S(2)}) collective-permute-start(f32[176,128]{1,0:T(8,128)S(1)} %collective-permute-done.93.p2), channel_id=1, source_target_pairs={{0,8},{8,0},{16,24},{24,16},{1,9},{9,1},{17,25},{25,17},{2,10},{10... | collective-permute-start | bytes 270344 | tf_op jit(solution)/shard_map/ppermute | solution.py:26
  (116 other events, 1477.6 us)
where the time goes:
time: 393 us; the launch traced here: 391 us
  waiting for transfers between devices  120 us (31%)
  Pallas kernels  114 us (29%)
  starting transfers between devices  104 us (26%)
  local copies, waits for them, and re-layouts  38.9 us (10%)
  other arithmetic  10.5 us (3%)
    ppermute x85, waiting for transfers between devices, swap(): lax.ppermute(a, axis, [(k, k ^ bit) for k in range(lax.axis_size(axis))])  104 us
    ppermute x85, starting transfers between devices, swap(): lax.ppermute(a, axis, [(k, k ^ bit) for k in range(lax.axis_size(axis))])  86.5 us
    pallas_call x60, Pallas kernels, call(): pl.pallas_call(kernel, grid=(1,), out_shape=out_shape, in_specs=specs, ou...  60.1 us
    unnamed x180, local copies, waits for them, and re-layouts  33.3 us
    pallas_call x1, Pallas kernels, feed_forward(): pl.pallas_call(mlp_kernel, grid=(units // step,), out_shape=(unit_out, un...  11.6 us
    pallas_call x1, Pallas kernels, ssm_back(): pl.pallas_call(back_kernel, grid=(NST // GROUP,), out_shape=(jax.ShapeDty...  9.99 us
    ppermute x4, starting transfers between devices, chain(): lax.ppermute(inclusive, 'seq', [(t, f) for f, t in pairs] if back else pa...  8.68 us
  transfers between devices with their start and end apart: 95, of which 32 were waited for; matrix products, arithmetic and copies ran while one was open for 6% of the time, Pallas kernels for 23%

commit v1 on v0

--- a/solution.py
+++ b/solution.py
@@ -804,7 +804,7 @@
 
 def pack_kernel(rate, gin, gout, g_one, g_two, out):
     for k, ref in enumerate((rate, gin, gout)):
-        out[0, k * NST : (k + 1) * NST, :] = ref[...].astype(f32).T.astype(bf16)
+        out[0, k * NST : (k + 1) * NST, :] = ref[...]
     out[0, 3 * NST : 3 * NST + 1, :] = g_one[...]
     out[0, 3 * NST + 1 : 3 * NST + 2, :] = g_two[...]
 
@@ -1005,10 +1005,10 @@
 def cut_states_kernel(idx, init_ref, ends_ref, i0, i1, e0, e1, e2, e3):
     cols = i0.shape[1]
     for r, out in enumerate((e0, e1, e2, e3)):
-        at = pl.multiple_of((idx[0] ^ r) * cols, 16)
-        out[...] = ends_ref[pl.ds(at, cols), :].T
+        at = pl.multiple_of((idx[0] ^ r) * cols, LANES)
+        out[...] = ends_ref[:, pl.ds(at, cols)]
         if r < 2:
-            (i0, i1)[r][...] = init_ref[pl.ds(at, cols), :].T
+            (i0, i1)[r][...] = init_ref[:, pl.ds(at, cols)]
 
 
 def join_states_kernel(late, i0, i1, e0, e1, e2, e3, init_ref, twice_ref, first_ref, second_ref):
@@ -1038,8 +1038,8 @@
 def join_ends_kernel(idx, e0, e1, e2, e3, out):
     cols = e0.shape[1]
     for r, part in enumerate((e0, e1, e2, e3)):
-        at = pl.multiple_of((idx[0] ^ r) * cols, 16)
-        out[pl.ds(at, cols), :] = part[...].T
+        at = pl.multiple_of((idx[0] ^ r) * cols, LANES)
+        out[:, pl.ds(at, cols)] = part[...]
 
 
 def small_kernel(spots, p0, p1, p2, p3, gains_ref, rate_ref, in_ref, out_ref, init_ref):
@@ -1058,10 +1058,10 @@
     params = chosen[:one].reshape(3 * NST, 2, LANES)
     params = jnp.where(side, params[:, 1], params[:, 0])
     for k, ref in enumerate((rate_ref, in_ref, out_ref)):
-        ref[...] = params[k * NST : (k + 1) * NST].T
+        ref[...] = params[k * NST : (k + 1) * NST]
     init = chosen[two:].reshape(NST, 4, LANES)
     window = [jnp.where(side, init[:, 2 * w + 1], init[:, 2 * w]) for w in (0, 1)]
-    init_ref[...] = jnp.where(spots[0] % 2 == 1, window[1], window[0]).T
+    init_ref[...] = jnp.where(spots[0] % 2 == 1, window[1], window[0])
 
 
 def added(p0, one, far):
@@ -1166,12 +1166,11 @@
     attn_second = attn.step()
     attn_third = attn.across(0)
     attn_last = attn.across(1)
-    up_first = up.rest(attn_second)
     small = call(
         pack_kernel,
         "pack_small",
         jax.ShapeDtypeStruct((1, 3 * NST + 2, shard), bf16),
-        (ssm_rate, ssm_in, ssm_out, g_attn[None], after(g_mlp[None], share_attn[1])),
+        after((ssm_rate.T, ssm_in.T, ssm_out.T, g_attn[None], g_mlp[None]), share_attn[1]),
         0,
     )
     for bit in [1] + high_bits("seq")[::-1]:
@@ -1192,7 +1191,7 @@
         cut_states_kernel,
         "cut_states",
         (by_channel,) * 6,
-        (idx, h_init[0], after(d_h_ends[0, 0], share_attn[1])),
+        (idx, h_init[0].T, after(d_h_ends[0, 0].T, share_attn[1])),
     )
     init, init_twice, end_first, end_second = call(
         join_states_kernel,
@@ -1215,36 +1214,38 @@
 
     a = jnp.exp(-rate)
     s_mid, s_end = local_ends(u, a)
+    up_first = up.rest((attn_second, s_end))
     decay = jnp.exp(-half_rate * rows)
     first_end, second_end = by_half(gin * s_end)
     span = 2 * rows
 
-    def chain(inclusive, back, meanwhile):
+    def chain(inclusive, back, wait):
         exclusive, step = jnp.zeros_like(inclusive), 1
         while step < ns // 2:
             pairs = [(k, k + 2 * step) for k in range(ns - 2 * step)]
             got = lax.ppermute(inclusive, "seq", [(t, f) for f, t in pairs] if back else pairs)
-            got = after(got, meanwhile)
+            if step == 1:
+                got = after(got, wait)
             exclusive = exclusive + jnp.exp(-half_rate * (span * (step - 1))) * got
             inclusive = inclusive + jnp.exp(-half_rate * (span * step)) * got
             step *= 2
         return exclusive
 
-    entering = chain(decay * first_end + second_end, False, up_first)
+    entering = chain(after(decay * first_end + second_end, attn_third), False, up_first)
     state_zero = jnp.exp(-half_rate * (span * block).astype(f32)) * init + entering
     state_one = decay * state_zero + first_end
     state_two = decay * state_one + second_end
     state_in = by_owner(state_zero, state_one)
     ends = call(cut_ends_kernel, "cut_ends", (by_channel,) * TEAM, (half, state_one, state_two))
-    ends = call(join_ends_kernel, "join_ends", like((dim, NST), f32), (idx, *trade_team(ends)))
+    ends = call(join_ends_kernel, "join_ends", like((NST, dim), f32), (idx, *trade_team(ends)))
     on_second = by_owner(jnp.zeros_like(init), jnp.ones_like(init))
     h_mid = jnp.exp(-rate * (rows - CTX)) * state_in + gin * s_mid
     h_mid = jnp.where(on_second > 0, h_mid, init_twice)
-    h_mid = after(h_mid, (attn_second, attn_third))
+    h_mid = after(h_mid, (attn_second, attn_last))
     y_first, y_second = contexts(half, u, a, gin * on_second, gout, h_mid)
     passed = lax.ppermute(y_second, "seq", [(k, k + 2) for k in range(ns - 2)])
     up_second = up.step(entering)
-    up_third = up.across(0, attn_last)
+    up_third = up.across(0)
     context = jnp.where(block == 0, y_first, after(passed, up_second))
     down_first = down[0].rest(passed)
     down_second = down[1].rest(up_third)
@@ -1340,10 +1341,12 @@
     lam_mid = tail_adjoint(dy, a, gout)
     g_second = jnp.exp(-half_rate * (rows - CTX + 1)) * lam_mid + decay * end_cot[1]
     d_a, d_gout, g_init = first_context_back(after(dy0_full, lam_mid), a, gout, init_twice)
-    leaving = chain(decay * (end_cot[0] + g_second), True, g_init)
+    leaving = chain(decay * (end_cot[0] + g_second), True, (g_init, sum_attn.out if reduction is HalvedReduction else g_init))
     sum_up.step(leaving)
     sum_attn.step(sum_up.sent)
     sum_down.step(sum_attn.sent)
+    result = sum_team(result, d_context)
+    result = call(result_kernel, "result_sum", like((rows, dim), bf16), (hidden, *result[:3]), 0)
     lam_end = by_owner(end_cot[0] + g_second + decay * leaving, end_cot[1] + leaving)
     du, d_gin, d_a, d_gout, g_in = ssm_back(
         u, dy_full, a, gin, gout, state_in, after(lam_end, sum_down.sent), d_a, d_gout
@@ -1356,15 +1359,13 @@
         inputs_grad_kernel,
         "inputs_grad",
         part_types(rows, dim) + (jax.ShapeDtypeStruct((1, dim), f32),),
-        (idx, d_qkv, full_qkv, du, inv_one, *x_blocks),
+        (idx, d_qkv, full_qkv, after(du, result), inv_one, *x_blocks),
         scratch_shapes=[pltpu.VMEM((rows, dim), f32)],
     )
+    *d_inputs, d_inputs_far = sum_team(d_inputs)
+    sum_up.step(d_inputs_far)
+    sum_attn.step(sum_up.sent)
     d_down = spread_weight("down", sum_down.last(), idx, [w_down.shape])[0]
-    sum_up.step(d_gain_one)
-    sum_attn.step(sum_up.sent)
-    result = sum_team(result, d_context, du)
-    result = call(result_kernel, "result_sum", like((rows, dim), bf16), (hidden, *result[:3]), 0)
-    *d_inputs, d_inputs_far = sum_team(d_inputs, None, d_down)
     d_tokens = call(
         tokens_grad_kernel,
         "tokens_grad",
@@ -1377,13 +1378,14 @@
     d_params = d_params.reshape(3 * NST, TEAM, cols).sum(1)
     d_gains = jnp.concatenate([d_gain_one[0], d_gain_two[0]])
     pack = [d_params.reshape(-1, LANES), d_gains.reshape(-1, LANES), d_init.reshape(-1, LANES)]
-    pack = after(jnp.concatenate(pack, axis=0), (sum_attn.sent, d_inputs_far))
+    pack = after(jnp.concatenate(pack, axis=0), d_inputs_far)
     for n, bit in enumerate(high_bits("seq")):
         if n == 1:
             pack = after(pack, sum_attn.step())
         pack = pack + swap(pack, "seq", bit)
     one, two = 3 * NST * cols // LANES, 3 * NST * cols // LANES + 2 * dim // LANES
     shared = pack[:two]
+    shared = after(shared, d_down)
     for bit in high_bits("dp"):
         shared = shared + swap(shared, "dp", bit)
     packs = gather_team(jnp.concatenate([shared, pack[two:]], axis=0))
@@ -1392,10 +1394,10 @@
         gains, *d_params, state_grad = call(
             small_kernel,
             "small_grads",
-            (like((2, shard), f32),) + (like((shard, NST), f32),) * 4,
+            (like((2, shard), f32),) + (like((NST, shard), f32),) * 4,
             (spots, *packs),
         )
-        state_grad = state_grad[None]
+        d_params, state_grad = [p.T for p in d_params], state_grad.T[None]
     else:
         packs = jnp.stack(packs)
         gains = packs[:, one:two].sum(0).reshape(2, ns, shard)
@@ -1428,7 +1430,7 @@
         d_params[1],
         d_params[2],
         state_grad,
-        ends[None, None],
+        ends.T[None, None],
     )
 
 

time: 393 us -> 371 us (0.944)
  local copies, waits for them, and re-layouts: 38.9 us -> 21.5 us
  Pallas kernels: 114 us -> 108 us
  starting transfers between devices: 104 us -> 110 us
    unnamed x180 -> x156, local copies, waits for them, and re-layouts: 33.3 us -> 16.6 us
    pallas_call x60, Pallas kernels: 60.1 us -> 54.3 us  [call(): pl.pallas_call(kernel, grid=(1,), out_shape=out_shape, in_specs=specs, ou...]
  transfers between devices with their start and end apart: 95 -> 95, of which waited for: 32 -> 30; matrix products, arithmetic and copies ran while one was open for 6% -> 4% of each run, Pallas kernels for 23% -> 22%
where the time goes in v1:
time: 371 us; the launch traced here: 370 us
  waiting for transfers between devices  118 us (32%)
  starting transfers between devices  110 us (30%)
  Pallas kernels  108 us (29%)
  local copies, waits for them, and re-layouts  21.5 us (6%)
  other arithmetic  8.34 us (2%)
    ppermute x85, waiting for transfers between devices, swap(): lax.ppermute(a, axis, [(k, k ^ bit) for k in range(lax.axis_size(axis))])  105 us
    ppermute x85, starting transfers between devices, swap(): lax.ppermute(a, axis, [(k, k ^ bit) for k in range(lax.axis_size(axis))])  88.3 us
    pallas_call x60, Pallas kernels, call(): pl.pallas_call(kernel, grid=(1,), out_shape=out_shape, in_specs=specs, ou...  54.3 us
    unnamed x156, local copies, waits for them, and re-layouts  16.6 us
    ppermute x4, starting transfers between devices, chain(): lax.ppermute(inclusive, 'seq', [(t, f) for f, t in pairs] if back else pa...  12.1 us
    pallas_call x1, Pallas kernels, feed_forward(): pl.pallas_call(mlp_kernel, grid=(units // step,), out_shape=(unit_out, un...  11.6 us
    pallas_call x1, Pallas kernels, ssm_back(): pl.pallas_call(back_kernel, grid=(NST // GROUP,), out_shape=(jax.ShapeDty...  9.99 us
  transfers between devices with their start and end apart: 95, of which 30 were waited for; matrix products, arithmetic and copies ran while one was open for 4% of the time, Pallas kernels for 22%

profile of v1, /device:TPU:1, one launch (start us, length us, event | category | flops | bytes accessed | tf_op | source)
XLA Modules:
  0.0 369.8 jit_solution(16510391984327588351)
XLA Ops:
  1.3 3.2 shares.1
  4.6 2.1 collective-permute-start
  7.9 1.6 collective-permute-start.1
  11.7 2.2 collective-permute-start.2
  15.8 3.3 collective-permute-start.5
  19.1 10.7 %collective-permute-done.4.b_ref = bf16[2,64,1024]{2,1,0:T(8,128)(2,1)S(1)} collective-permute-done((bf16[2,64,1024]{2,1,0:T(8,128)(2,1)S(1)}, bf16[2,64,1024]{2,1,0:T(8,128)(2,1)S(1)}, u32[]{:S(2)}, u32[]{:S(2)}) %collective-permute-start.4) | collective-permute-done | bytes 262176 | tf_op jit(solution)/shard_map/ppermute | solution.py:26
  34.5 2.4 collective-permute-done.17.b_ref
  39.5 2.0 first_norm.1
  44.0 2.3 collective-permute-start.18
  47.2 2.8 collective-permute-start.16
  50.6 1.6 collective-permute-start.12
  52.4 2.2 collective-permute-start.15
  54.5 3.3 collective-permute-done.18.b_ref
  59.3 6.7 %collective-permute-start.19 = (f32[16,4,128]{2,1,0:T(4,128)}, f32[16,4,128]{2,1,0:T(4,128)}, u32[]{:S(2)}, u32[]{:S(2)}) collective-permute-start(f32[16,4,128]{2,1,0:T(4,128)} %multiply_add_fusion.6), channel_id=1, source_target_pairs={{0,4},{1,5},{2,6},{3,7},{8,12},{9,13},{10,14},{11,15},{16,20},{17,... | collective-permute-start | bytes 98312 | tf_op jit(solution)/shard_map/ppermute | solution.py:1226
  74.4 7.2 %collective-permute-done.10.refs_3_ = bf16[4,64,1024]{2,1,0:T(8,128)(2,1)S(1)} collective-permute-done((bf16[4,64,1024]{2,1,0:T(8,128)(2,1)}, bf16[4,64,1024]{2,1,0:T(8,128)(2,1)S(1)}, u32[]{:S(2)}, u32[]{:S(2)}) %collective-permute-start.10) | collective-permute-done | bytes 524320 | tf_op jit(solution)/shard_map/ppermute | solution.py:26
  81.6 2.8 ssm_context.1
  84.4 2.0 collective-permute-start.20
  88.5 1.6 append.16.a_ref
  91.1 2.0 collective-permute-start.25
  93.1 1.8 collective-permute-start.24
  95.8 3.5 collective-permute-start.26
  104.9 1.7 collective-permute-start.30
  108.3 2.0 collective-permute-start.29
  110.4 1.8 convolution_convert_fusion.q0.q1.k0.k1.v0.v1
  113.7 5.0 %attend.1.x_ref.att_ref = bf16[1024,256]{1,0:T(8,128)(2,1)S(1)} custom-call(s32[1]{0:T(128)} %bitcast.3.late.half_ref, bf16[1024,768]{1,0:T(8,128)(2,1)S(1)} %convolution_convert_fusion.q0.q1.k0.k1.v0.v1, bf16[1024,768]{1,0:T(8,128)(2,1)S(1)} %convolution_convert_fusion.q0.q1.k0.k1.v0.v1, bf16[1024,768]{1,0:T(8,128)(2,1)S(1)} %convolution_convert_fusion.q0.q1.k0.k1.v0.v1, ...), custom_call_target="tpu_custom_call" | custom-call | tf_op jit(solution)/shard_map/attend/pallas_call | solution.py:771
  118.7 4.1 %collective-permute-done.29.b_ref = bf16[2,64,1024]{2,1,0:T(8,128)(2,1)S(1)} collective-permute-done((bf16[2,64,1024]{2,1,0:T(8,128)(2,1)S(1)}, bf16[2,64,1024]{2,1,0:T(8,128)(2,1)S(1)}, u32[]{:S(2)}, u32[]{:S(2)}) %collective-permute-start.29) | collective-permute-done | bytes 262176 | tf_op jit(solution)/shard_map/ppermute | solution.py:26
  130.6 10.7 %collective-permute-done.37.e2 = f32[16,256]{1,0:T(8,128)S(1)} collective-permute-done((f32[16,256]{1,0:T(8,128)S(1)}, f32[16,256]{1,0:T(8,128)S(1)}, u32[]{:S(2)}, u32[]{:S(2)}) %collective-permute-start.37) | collective-permute-done | bytes 16416 | tf_op jit(solution)/shard_map/ppermute | solution.py:26
  142.5 2.0 collective-permute-done.38.e3
  147.3 1.8 collective-permute-start.46
  150.6 8.0 %collective-permute-done.42.m2.x2 = bf16[256,1024]{1,0:T(8,128)(2,1)S(1)} collective-permute-done((bf16[256,1024]{1,0:T(8,128)(2,1)S(1)}, bf16[256,1024]{1,0:T(8,128)(2,1)S(1)}, u32[]{:S(2)}, u32[]{:S(2)}) %collective-permute-start.42) | collective-permute-done | bytes 524320 | tf_op jit(solution)/shard_map/ppermute | solution.py:26
  158.6 1.9 collective-permute-start.43
  162.6 11.6 %feed_forward.1 = (bf16[1024,1024]{1,0:T(8,128)(2,1)S(1)}, bf16[1024,1024]{1,0:T(8,128)(2,1)S(1)}, f32[256,1024]{1,0:T(8,128)S(1)}, bf16[256,1024]{1,0:T(8,128)(...) custom-call(bf16[256,1024]{1,0:T(8,128)(2,1)S(1)} %get-tuple-element.240.m0.x0, ...), custom_call_target="tpu_custom_call" | custom-call | tf_op jit(solution)/shard_map/feed_forward/pallas_call | solution.py:900
  174.4 3.2 down_grad.1
  180.2 3.5 up_grad.1
  184.6 2.9 down_dot.1
  188.5 2.4 collective-permute-done.50.came_ref
  191.0 1.8 collective-permute-done.54.far
  198.2 1.6 collective-permute-start.55
  199.8 7.4 %collective-permute-done.56.h2 = bf16[256,1024]{1,0:T(8,128)(2,1)S(1)} collective-permute-done((bf16[256,1024]{1,0:T(8,128)(2,1)S(1)}, bf16[256,1024]{1,0:T(8,128)(2,1)S(1)}, u32[]{:S(2)}, u32[]{:S(2)}) %collective-permute-start.56) | collective-permute-done | bytes 524320 | tf_op jit(solution)/shard_map/ppermute | solution.py:26
  207.2 1.7 collective-permute-start.57
  213.0 7.2 %attend_back.1 = (bf16[1024,768]{1,0:T(8,128)(2,1)S(1)}, bf16[256,512]{1,0:T(8,128)(2,1)S(1)}) custom-call(s32[1]{0:T(128)} %bitcast.3.late.half_ref, bf16[1024,768]{1,0:T(8,128)(2,1)S(1)} %convolution_convert_fusion.q0.q1.k0.k1.v0.v1, bf16[1024,768]{1,0:T(8,128)(2,1)S(1)} %convolution_convert_fusion.q0.q1.k0.k1.v0.v1, ...), custom_call_target="tpu_custom_call" | custom-call | tf_op jit(solution)/shard_map/attend_back/pallas_call | solution.py:791
  220.3 2.1 collective-permute-done.58.came_ref
  230.2 4.3 %collective-permute-done.64.refs_3_ = bf16[256,256]{1,0:T(8,128)(2,1)S(1)} collective-permute-done((bf16[256,256]{1,0:T(8,128)(2,1)S(1)}, bf16[256,256]{1,0:T(8,128)(2,1)S(1)}, u32[]{:S(2)}, u32[]{:S(2)}) %collective-permute-start.64) | collective-permute-done | bytes 131104 | tf_op jit(solution)/shard_map/ppermute | solution.py:36
  234.5 5.1 %attn_grad.1 = bf16[1024,1024]{1,0:T(8,128)(2,1)S(1)} custom-call(s32[2]{0:T(128)S(1)} %copy-done.46, bf16[1024,1024]{1,0:T(8,128)(2,1)S(1)} %copy-done.15, bf16[1024,768]{1,0:T(8,128)(2,1)S(1)} %get-tuple-element.282.dq_ref, bf16[256,1024]{1,0:T(8,128)(2,1)S(1)} %get-tuple-element.283.ctx_ref, bf16[256,512]{1,0:T(8,128)(2,1)S(1)} %get-tuple-element.276.d_ref.dctx_ref, ...), custom_call_target="tpu_custom_call" | custom-call | tf_op jit(solution)/shard_map/attn_grad/pallas_call | solution.py:279
  244.1 6.4 %collective-permute-done.66.came = bf16[256,256]{1,0:T(8,128)(2,1)S(1)} collective-permute-done((bf16[256,256]{1,0:T(8,128)(2,1)S(1)}, bf16[256,256]{1,0:T(8,128)(2,1)S(1)}, u32[]{:S(2)}, u32[]{:S(2)}) %collective-permute-start.66) | collective-permute-done | bytes 131104 | tf_op jit(solution)/shard_map/ppermute | solution.py:1332
  255.7 2.4 collective-permute-start.72
  258.4 5.1 %first_context.1 = (f32[16,8,128]{2,1,0:T(8,128)}, f32[16,8,128]{2,1,0:T(8,128)}, f32[16,8,128]{2,1,0:T(8,128)}) custom-call(f32[128,8,128]{2,1,0:T(8,128)} %copy-done.35, f32[16,8,128]{2,1,0:T(8,128)} %copy-done.12, f32[16,8,128]{2,1,0:T(8,128)} %copy-done.23, f32[16,8,128]{2,1,0:T(8,128)} %copy-done.45), custom_call_target="tpu_custom_call" | custom-call | tf_op jit(solution)/shard_map/first_context/pallas_call | solution.py:590
  264.9 3.0 collective-permute-start.70
  272.8 2.7 collective-permute-done.72.near_ref
  278.4 2.4 collective-permute-done.70.refs_0_
  281.0 10.0 %ssm_back.1 = (f32[256,8,128]{2,1,0:T(8,128)S(1)}, f32[16,8,128]{2,1,0:T(8,128)S(1)}, f32[16,8,128]{2,1,0:T(8,128)S(1)}, f32[16,8,128]{2,1,0:T(8,128)S(1)}, f32[16,8,128]{2,1,0:T(8,128)S(1)}) custom-call(f32[256,8,128]{2,1,0:T(8,128)S(1)} %get-tuple-element.191.u_ref, f32[128,8,128]{2,1,0:T(8,128)S(1)} %copy-done.39, f32[16,8,128]{2,1,0:T(8,128)S(1)} %copy-done.13, ...), custom_call_target="tpu_custom_call" | custom-call | tf_op jit(solution)/shard_map/ssm_back/pallas_call | solution.py:672
  293.3 4.5 %inputs_grad.1 = (f32[256,1024]{1,0:T(8,128)S(1)}, bf16[256,1024]{1,0:T(8,128)(2,1)}, f32[256,1024]{1,0:T(8,128)S(1)}, bf16[256,1024]{1,0:T(8,128)(2,1)S(1)}, f32[1,1024]{1,0:T(1,128)S(1)}) custom-call(s32[2]{0:T(128)S(1)} %copy-done.46, bf16[1024,768]{1,0:T(8,128)(2,1)S(1)} %copy-done.7, bf16[1024,768]{1,0:T(8,128)(2,1)S(1)} %copy-done.3, ...), custom_call_target="tpu_custom_call" | custom-call | tf_op jit(solution)/shard_map/inputs_grad/pallas_call | solution.py:109
  301.0 4.0 %collective-permute-done.86.b_ref = bf16[1,64,1024]{2,1,0:T(8,128)(2,1)S(1)} collective-permute-done((bf16[1,64,1024]{2,1,0:T(8,128)(2,1)S(1)}, bf16[1,64,1024]{2,1,0:T(8,128)(2,1)S(1)}, u32[]{:S(2)}, u32[]{:S(2)}) %collective-permute-start.86) | collective-permute-done | bytes 131104 | tf_op jit(solution)/shard_map/ppermute | solution.py:26
  306.6 11.7 %collective-permute-done.87.b_ref = bf16[2,64,1024]{2,1,0:T(8,128)(2,1)S(1)} collective-permute-done((bf16[2,64,1024]{2,1,0:T(8,128)(2,1)S(1)}, bf16[2,64,1024]{2,1,0:T(8,128)(2,1)S(1)}, u32[]{:S(2)}, u32[]{:S(2)}) %collective-permute-start.87) | collective-permute-done | bytes 262176 | tf_op jit(solution)/shard_map/ppermute | solution.py:26
  324.4 9.9 %collective-permute-done.79.refs_0_ = bf16[2,64,1024]{2,1,0:T(8,128)(2,1)S(1)} collective-permute-done((bf16[2,64,1024]{2,1,0:T(8,128)(2,1)S(1)}, bf16[2,64,1024]{2,1,0:T(8,128)(2,1)S(1)}, u32[]{:S(2)}, u32[]{:S(2)}) %collective-permute-start.79) | collective-permute-done | bytes 262176 | tf_op jit(solution)/shard_map/ppermute | solution.py:26
  339.5 1.8 collective-permute-done.89
  342.1 2.0 final_down.1
  344.1 1.7 collective-permute-done.90
  347.0 3.4 collective-permute-start.85
  350.5 2.7 collective-permute-start.82
  354.3 3.1 collective-permute-done.93.p2
  360.5 2.3 tokens_grad.1
  364.6 2.7 final_up.1
  367.3 2.5 final_attn.1
  (402 shorter events, 122.0 us)
Async XLA Ops:
  10.8 19.1 %collective-permute-start.6 = (bf16[256,1024]{1,0:T(8,128)(2,1)S(1)}, bf16[256,1024]{1,0:T(8,128)(2,1)S(1)}, u32[]{:S(2)}, u32[]{:S(2)}) collective-permute-start(bf16[256,1024]{1,0:T(8,128)(2,1)S(1)} %bitcast.81), channel_id=1, source_target_pairs={{0,1},{1,0},{2,3},{3,2},{4,5},{5,4},{6,7},{7,6},{8,9},{9,8},{10,11... | collective-permute-start | bytes 1572872 | tf_op jit(solution)/shard_map/ppermute | solution.py:26
  14.9 14.9 %collective-permute-start.4 = (bf16[2,64,1024]{2,1,0:T(8,128)(2,1)S(1)}, bf16[2,64,1024]{2,1,0:T(8,128)(2,1)S(1)}, u32[]{:S(2)}, u32[]{:S(2)}) collective-permute-start(bf16[2,64,1024]{2,1,0:T(8,128)(2,1)S(1)} %append.14.a_ref), channel_id=1, source_target_pairs={{0,4},{1,5},{2,6},{3,7},{4,0},{5,1},{6,2},{7,3},{8,12},{9,13},{10,... | collective-permute-start | bytes 786440 | tf_op jit(solution)/shard_map/ppermute | solution.py:26
  15.8 21.8 %collective-permute-start.5 = (bf16[256,1024]{1,0:T(8,128)(2,1)S(1)}, bf16[256,1024]{1,0:T(8,128)(2,1)S(1)}, u32[]{:S(2)}, u32[]{:S(2)}) collective-permute-start(bf16[256,1024]{1,0:T(8,128)(2,1)S(1)} %bitcast.82), channel_id=1, source_target_pairs={{0,8},{8,0},{16,24},{24,16},{1,9},{9,1},{17,25},{25,17},{2,10},{10... | collective-permute-start | bytes 1572872 | tf_op jit(solution)/shard_map/ppermute | solution.py:26
  29.8 14.2 %collective-permute-start.8 = (bf16[4,64,1024]{2,1,0:T(8,128)(2,1)S(1)}, bf16[4,64,1024]{2,1,0:T(8,128)(2,1)}, u32[]{:S(2)}, u32[]{:S(2)}) collective-permute-start(bf16[4,64,1024]{2,1,0:T(8,128)(2,1)S(1)} %append.15.refs_0_), channel_id=1, source_target_pairs={{0,2},{1,3},{2,0},{3,1},{4,6},{5,7},{6,4},{7,5},{8,10},{9,11},{10,... | collective-permute-start | bytes 1572872 | tf_op jit(solution)/shard_map/ppermute | solution.py:26
  33.2 13.9 %collective-permute-start.9 = (bf16[4,64,1024]{2,1,0:T(8,128)(2,1)S(1)}, bf16[4,64,1024]{2,1,0:T(8,128)(2,1)}, u32[]{:S(2)}, u32[]{:S(2)}) collective-permute-start(bf16[4,64,1024]{2,1,0:T(8,128)(2,1)S(1)} %append.15.refs_0_), channel_id=1, source_target_pairs={{0,16},{8,24},{16,0},{24,8},{1,17},{9,25},{17,1},{25,9},{2,18},{10... | collective-permute-start | bytes 1572872 | tf_op jit(solution)/shard_map/ppermute | solution.py:26
  44.0 13.8 %collective-permute-start.18 = (bf16[2,64,1024]{2,1,0:T(8,128)(2,1)}, bf16[2,64,1024]{2,1,0:T(8,128)(2,1)S(1)}, u32[]{:S(2)}, u32[]{:S(2)}) collective-permute-start(bf16[2,64,1024]{2,1,0:T(8,128)(2,1)} %append.17.a_ref), channel_id=1, source_target_pairs={{0,4},{1,5},{2,6},{3,7},{4,0},{5,1},{6,2},{7,3},{8,12},{9,13},{10,... | collective-permute-start | bytes 786440 | tf_op jit(solution)/shard_map/ppermute | solution.py:26
  50.6 16.0 %collective-permute-start.12 = (f32[16,256]{1,0:T(8,128)S(1)}, f32[16,256]{1,0:T(8,128)S(1)}, u32[]{:S(2)}, u32[]{:S(2)}) collective-permute-start(f32[16,256]{1,0:T(8,128)S(1)} %get-tuple-element.194), channel_id=1, source_target_pairs={{0,8},{8,0},{16,24},{24,16},{1,9},{9,1},{17,25},{25,17},{2,10},{10... | collective-permute-start | bytes 49160 | tf_op jit(solution)/shard_map/ppermute | solution.py:26
  52.2 14.4 %collective-permute-start.13 = (f32[16,256]{1,0:T(8,128)S(1)}, f32[16,256]{1,0:T(8,128)S(1)}, u32[]{:S(2)}, u32[]{:S(2)}) collective-permute-start(f32[16,256]{1,0:T(8,128)S(1)} %get-tuple-element.196), channel_id=1, source_target_pairs={{0,8},{8,0},{16,24},{24,16},{1,9},{9,1},{17,25},{25,17},{2,10},{10... | collective-permute-start | bytes 49160 | tf_op jit(solution)/shard_map/ppermute | solution.py:26
  52.3 14.3 %collective-permute-start.14 = (f32[16,256]{1,0:T(8,128)S(1)}, f32[16,256]{1,0:T(8,128)S(1)}, u32[]{:S(2)}, u32[]{:S(2)}) collective-permute-start(f32[16,256]{1,0:T(8,128)S(1)} %get-tuple-element.197), channel_id=1, source_target_pairs={{0,1},{1,0},{2,3},{3,2},{4,5},{5,4},{6,7},{7,6},{8,9},{9,8},{10,11... | collective-permute-start | bytes 49160 | tf_op jit(solution)/shard_map/ppermute | solution.py:26
  52.4 14.2 %collective-permute-start.15 = (f32[16,256]{1,0:T(8,128)S(1)}, f32[16,256]{1,0:T(8,128)S(1)}, u32[]{:S(2)}, u32[]{:S(2)}) collective-permute-start(f32[16,256]{1,0:T(8,128)S(1)} %get-tuple-element.198), channel_id=1, source_target_pairs={{0,9},{1,8},{2,11},{3,10},{4,13},{5,12},{6,15},{7,14},{8,1},{9,0},... | collective-permute-start | bytes 49160 | tf_op jit(solution)/shard_map/ppermute | solution.py:36
  59.3 11.9 %collective-permute-start.19 = (f32[16,4,128]{2,1,0:T(4,128)}, f32[16,4,128]{2,1,0:T(4,128)}, u32[]{:S(2)}, u32[]{:S(2)}) collective-permute-start(f32[16,4,128]{2,1,0:T(4,128)} %multiply_add_fusion.6), channel_id=1, source_target_pairs={{0,4},{1,5},{2,6},{3,7},{8,12},{9,13},{10,14},{11,15},{16,20},{17,... | collective-permute-start | bytes 98312 | tf_op jit(solution)/shard_map/ppermute | solution.py:1226
  67.6 20.0 %collective-permute-start.11 = (bf16[1,64,1024]{2,1,0:T(8,128)(2,1)}, bf16[1,64,1024]{2,1,0:T(8,128)(2,1)}, u32[]{:S(2)}, u32[]{:S(2)}) collective-permute-start(bf16[1,64,1024]{2,1,0:T(8,128)(2,1)} %bitcast.118), channel_id=1, source_target_pairs={{0,1},{1,0},{2,3},{3,2},{4,5},{5,4},{6,7},{7,6},{8,9},{9,8},{10,11... | collective-permute-start | bytes 393224 | tf_op jit(solution)/shard_map/ppermute | solution.py:26
  68.1 13.5 %collective-permute-start.10 = (bf16[4,64,1024]{2,1,0:T(8,128)(2,1)}, bf16[4,64,1024]{2,1,0:T(8,128)(2,1)S(1)}, u32[]{:S(2)}, u32[]{:S(2)}) collective-permute-start(bf16[4,64,1024]{2,1,0:T(8,128)(2,1)} %collective-permute-done.8.refs_1_), channel_id=1, source_target_pairs={{0,16},{8,24},{16,0},{24,8},{1,17},{9,25},{17,1},{25,9},{2,18},{10... | collective-permute-start | bytes 1572872 | tf_op jit(solution)/shard_map/ppermute | solution.py:26
  72.8 17.3 %collective-permute-start.23 = (bf16[4,64,1024]{2,1,0:T(8,128)(2,1)S(1)}, bf16[4,64,1024]{2,1,0:T(8,128)(2,1)}, u32[]{:S(2)}, u32[]{:S(2)}) collective-permute-start(bf16[4,64,1024]{2,1,0:T(8,128)(2,1)S(1)} %append.18.refs_0_), channel_id=1, source_target_pairs={{0,2},{1,3},{2,0},{3,1},{4,6},{5,7},{6,4},{7,5},{8,10},{9,11},{10,... | collective-permute-start | bytes 1572872 | tf_op jit(solution)/shard_map/ppermute | solution.py:26
  86.3 18.6 %collective-permute-start.22 = (bf16[4,64,1024]{2,1,0:T(8,128)(2,1)S(1)}, bf16[4,64,1024]{2,1,0:T(8,128)(2,1)}, u32[]{:S(2)}, u32[]{:S(2)}) collective-permute-start(bf16[4,64,1024]{2,1,0:T(8,128)(2,1)S(1)} %append.18.refs_0_), channel_id=1, source_target_pairs={{0,16},{8,24},{16,0},{24,8},{1,17},{9,25},{17,1},{25,9},{2,18},{10... | collective-permute-start | bytes 1572872 | tf_op jit(solution)/shard_map/ppermute | solution.py:26
  90.1 16.5 %collective-permute-start.21 = (bf16[2,64,1024]{2,1,0:T(8,128)(2,1)}, bf16[2,64,1024]{2,1,0:T(8,128)(2,1)}, u32[]{:S(2)}, u32[]{:S(2)}) collective-permute-start(bf16[2,64,1024]{2,1,0:T(8,128)(2,1)} %append.16.a_ref), channel_id=1, source_target_pairs={{0,4},{1,5},{2,6},{3,7},{4,0},{5,1},{6,2},{7,3},{8,12},{9,13},{10,... | collective-permute-start | bytes 786440 | tf_op jit(solution)/shard_map/ppermute | solution.py:26
  93.1 13.7 %collective-permute-start.24 = (bf16[256,256]{1,0:T(8,128)(2,1)S(1)}, bf16[256,256]{1,0:T(8,128)(2,1)}, u32[]{:S(2)}, u32[]{:S(2)}) collective-permute-start(bf16[256,256]{1,0:T(8,128)(2,1)S(1)} %broadcast_select_fusion.c0), channel_id=1, source_target_pairs={{0,8},{8,0},{16,24},{24,16},{1,9},{9,1},{17,25},{25,17},{2,10},{10... | collective-permute-start | bytes 393224 | tf_op jit(solution)/shard_map/ppermute | solution.py:26
  95.8 12.5 %collective-permute-start.26 = (bf16[256,256]{1,0:T(8,128)(2,1)}, bf16[256,256]{1,0:T(8,128)(2,1)}, u32[]{:S(2)}, u32[]{:S(2)}) collective-permute-start(bf16[256,256]{1,0:T(8,128)(2,1)} %collective-permute-done.25.c2), channel_id=1, source_target_pairs={{0,8},{8,0},{16,24},{24,16},{1,9},{9,1},{17,25},{25,17},{2,10},{10... | collective-permute-start | bytes 393224 | tf_op jit(solution)/shard_map/ppermute | solution.py:26
  99.3 19.4 %collective-permute-start.27 = (bf16[256,1024]{1,0:T(8,128)(2,1)S(1)}, bf16[256,1024]{1,0:T(8,128)(2,1)S(1)}, u32[]{:S(2)}, u32[]{:S(2)}) collective-permute-start(bf16[256,1024]{1,0:T(8,128)(2,1)S(1)} %bitcast.87), channel_id=1, source_target_pairs={{0,1},{1,0},{2,3},{3,2},{4,5},{5,4},{6,7},{7,6},{8,9},{9,8},{10,11... | collective-permute-start | bytes 1572872 | tf_op jit(solution)/shard_map/ppermute | solution.py:26
  104.9 17.9 %collective-permute-start.30 = (bf16[256,256]{1,0:T(8,128)(2,1)S(1)}, bf16[256,256]{1,0:T(8,128)(2,1)S(1)}, u32[]{:S(2)}, u32[]{:S(2)}) collective-permute-start(bf16[256,256]{1,0:T(8,128)(2,1)S(1)} %get-tuple-element.224), channel_id=1, source_target_pairs={{0,8},{8,0},{16,24},{24,16},{1,9},{9,1},{17,25},{25,17},{2,10},{10... | collective-permute-start | bytes 393224 | tf_op jit(solution)/shard_map/ppermute | solution.py:26
  106.6 16.2 %collective-permute-start.31 = (bf16[256,256]{1,0:T(8,128)(2,1)S(1)}, bf16[256,256]{1,0:T(8,128)(2,1)S(1)}, u32[]{:S(2)}, u32[]{:S(2)}) collective-permute-start(bf16[256,256]{1,0:T(8,128)(2,1)S(1)} %get-tuple-element.225), channel_id=1, source_target_pairs={{0,1},{1,0},{2,3},{3,2},{4,5},{5,4},{6,7},{7,6},{8,9},{9,8},{10,11... | collective-permute-start | bytes 393224 | tf_op jit(solution)/shard_map/ppermute | solution.py:26
  106.9 15.9 %collective-permute-start.32 = (bf16[256,256]{1,0:T(8,128)(2,1)S(1)}, bf16[256,256]{1,0:T(8,128)(2,1)S(1)}, u32[]{:S(2)}, u32[]{:S(2)}) collective-permute-start(bf16[256,256]{1,0:T(8,128)(2,1)S(1)} %get-tuple-element.226), channel_id=1, source_target_pairs={{0,9},{1,8},{2,11},{3,10},{4,13},{5,12},{6,15},{7,14},{8,1},{9,0},... | collective-permute-start | bytes 393224 | tf_op jit(solution)/shard_map/ppermute | solution.py:36
  108.3 14.5 %collective-permute-start.29 = (bf16[2,64,1024]{2,1,0:T(8,128)(2,1)S(1)}, bf16[2,64,1024]{2,1,0:T(8,128)(2,1)S(1)}, u32[]{:S(2)}, u32[]{:S(2)}) collective-permute-start(bf16[2,64,1024]{2,1,0:T(8,128)(2,1)S(1)} %append.19.a_ref), channel_id=1, source_target_pairs={{0,4},{1,5},{2,6},{3,7},{4,0},{5,1},{6,2},{7,3},{8,12},{9,13},{10,... | collective-permute-start | bytes 786440 | tf_op jit(solution)/shard_map/ppermute | solution.py:26
  126.0 19.7 %collective-permute-start.40 = (bf16[4,64,1024]{2,1,0:T(8,128)(2,1)}, bf16[4,64,1024]{2,1,0:T(8,128)(2,1)S(1)}, u32[]{:S(2)}, u32[]{:S(2)}) collective-permute-start(bf16[4,64,1024]{2,1,0:T(8,128)(2,1)} %collective-permute-done.23.refs_1_), channel_id=1, source_target_pairs={{0,16},{8,24},{16,0},{24,8},{1,17},{9,25},{17,1},{25,9},{2,18},{10... | collective-permute-start | bytes 1572872 | tf_op jit(solution)/shard_map/ppermute | solution.py:26
  127.2 18.5 %collective-permute-start.39 = (bf16[4,64,1024]{2,1,0:T(8,128)(2,1)S(1)}, bf16[4,64,1024]{2,1,0:T(8,128)(2,1)S(1)}, u32[]{:S(2)}, u32[]{:S(2)}) collective-permute-start(bf16[4,64,1024]{2,1,0:T(8,128)(2,1)S(1)} %append.20.refs_0_), channel_id=1, source_target_pairs={{0,2},{1,3},{2,0},{3,1},{4,6},{5,7},{6,4},{7,5},{8,10},{9,11},{10,... | collective-permute-start | bytes 1572872 | tf_op jit(solution)/shard_map/ppermute | solution.py:26
  127.2 18.5 %collective-permute-start.33 = (bf16[256,1024]{1,0:T(8,128)(2,1)S(1)}, bf16[256,1024]{1,0:T(8,128)(2,1)S(1)}, u32[]{:S(2)}, u32[]{:S(2)}) collective-permute-start(bf16[256,1024]{1,0:T(8,128)(2,1)S(1)} %get-tuple-element.228), channel_id=1, source_target_pairs={{0,8},{8,0},{16,24},{24,16},{1,9},{9,1},{17,25},{25,17},{2,10},{10... | collective-permute-start | bytes 1572872 | tf_op jit(solution)/shard_map/ppermute | solution.py:26
  127.6 18.1 %collective-permute-start.35 = (bf16[256,1024]{1,0:T(8,128)(2,1)S(1)}, bf16[256,1024]{1,0:T(8,128)(2,1)S(1)}, u32[]{:S(2)}, u32[]{:S(2)}) collective-permute-start(bf16[256,1024]{1,0:T(8,128)(2,1)S(1)} %far_sum.5), channel_id=1, source_target_pairs={{0,1},{1,0},{2,3},{3,2},{4,5},{5,4},{6,7},{7,6},{8,9},{9,8},{10,11... | collective-permute-start | bytes 1572872 | tf_op jit(solution)/shard_map/ppermute | solution.py:26
  129.4 11.9 %collective-permute-start.37 = (f32[16,256]{1,0:T(8,128)S(1)}, f32[16,256]{1,0:T(8,128)S(1)}, u32[]{:S(2)}, u32[]{:S(2)}) collective-permute-start(f32[16,256]{1,0:T(8,128)S(1)} %get-tuple-element.233), channel_id=1, source_target_pairs={{0,1},{1,0},{2,3},{3,2},{4,5},{5,4},{6,7},{7,6},{8,9},{9,8},{10,11... | collective-permute-start | bytes 49160 | tf_op jit(solution)/shard_map/ppermute | solution.py:26
  146.1 12.5 %collective-permute-start.42 = (bf16[256,1024]{1,0:T(8,128)(2,1)S(1)}, bf16[256,1024]{1,0:T(8,128)(2,1)S(1)}, u32[]{:S(2)}, u32[]{:S(2)}) collective-permute-start(bf16[256,1024]{1,0:T(8,128)(2,1)S(1)} %get-tuple-element.240.m0.x0), channel_id=1, source_target_pairs={{0,1},{1,0},{2,3},{3,2},{4,5},{5,4},{6,7},{7,6},{8,9},{9,8},{10,11... | collective-permute-start | bytes 1572872 | tf_op jit(solution)/shard_map/ppermute | solution.py:26
  147.3 14.6 %collective-permute-start.46 = (bf16[4,64,1024]{2,1,0:T(8,128)(2,1)S(1)}, bf16[4,64,1024]{2,1,0:T(8,128)(2,1)S(1)}, u32[]{:S(2)}, u32[]{:S(2)}) collective-permute-start(bf16[4,64,1024]{2,1,0:T(8,128)(2,1)S(1)} %append.21.refs_2_), channel_id=1, source_target_pairs={{0,2},{1,3},{2,0},{3,1},{4,6},{5,7},{6,4},{7,5},{8,10},{9,11},{10,... | collective-permute-start | bytes 1572872 | tf_op jit(solution)/shard_map/ppermute | solution.py:26
  149.1 13.5 %collective-permute-start.44 = (bf16[256,1024]{1,0:T(8,128)(2,1)S(1)}, bf16[256,1024]{1,0:T(8,128)(2,1)S(1)}, u32[]{:S(2)}, u32[]{:S(2)}) collective-permute-start(bf16[256,1024]{1,0:T(8,128)(2,1)S(1)} %bitcast.88), channel_id=1, source_target_pairs={{0,8},{8,0},{16,24},{24,16},{1,9},{9,1},{17,25},{25,17},{2,10},{10... | collective-permute-start | bytes 1572872 | tf_op jit(solution)/shard_map/ppermute | solution.py:26
  150.1 12.6 %collective-permute-start.45 = (bf16[256,1024]{1,0:T(8,128)(2,1)S(1)}, bf16[256,1024]{1,0:T(8,128)(2,1)S(1)}, u32[]{:S(2)}, u32[]{:S(2)}) collective-permute-start(bf16[256,1024]{1,0:T(8,128)(2,1)S(1)} %collective-permute-done.27.g2.y2), channel_id=1, source_target_pairs={{0,8},{8,0},{16,24},{24,16},{1,9},{9,1},{17,25},{25,17},{2,10},{10... | collective-permute-start | bytes 1572872 | tf_op jit(solution)/shard_map/ppermute | solution.py:26
  150.1 12.6 %collective-permute-start.41 = (bf16[256,1024]{1,0:T(8,128)(2,1)S(1)}, bf16[256,1024]{1,0:T(8,128)(2,1)S(1)}, u32[]{:S(2)}, u32[]{:S(2)}) collective-permute-start(bf16[256,1024]{1,0:T(8,128)(2,1)S(1)} %get-tuple-element.240.m0.x0), channel_id=1, source_target_pairs={{0,8},{8,0},{16,24},{24,16},{1,9},{9,1},{17,25},{25,17},{2,10},{10... | collective-permute-start | bytes 1572872 | tf_op jit(solution)/shard_map/ppermute | solution.py:26
  177.8 13.1 %collective-permute-start.50 = (bf16[4,64,1024]{2,1,0:T(8,128)(2,1)S(1)}, bf16[4,64,1024]{2,1,0:T(8,128)(2,1)S(1)}, u32[]{:S(2)}, u32[]{:S(2)}) collective-permute-start(bf16[4,64,1024]{2,1,0:T(8,128)(2,1)S(1)} %get-tuple-element.244), channel_id=1, source_target_pairs={{0,16},{8,24},{16,0},{24,8},{1,17},{9,25},{17,1},{25,9},{2,18},{10... | collective-permute-start | bytes 1572872 | tf_op jit(solution)/shard_map/ppermute | solution.py:26
  178.4 12.6 %collective-permute-start.53 = (bf16[256,1024]{1,0:T(8,128)(2,1)S(1)}, bf16[256,1024]{1,0:T(8,128)(2,1)S(1)}, u32[]{:S(2)}, u32[]{:S(2)}) collective-permute-start(bf16[256,1024]{1,0:T(8,128)(2,1)S(1)} %get-tuple-element.260), channel_id=1, source_target_pairs={{0,8},{8,0},{16,24},{24,16},{1,9},{9,1},{17,25},{25,17},{2,10},{10... | collective-permute-start | bytes 1572872 | tf_op jit(solution)/shard_map/ppermute | solution.py:26
  179.3 13.6 %collective-permute-start.54 = (bf16[256,1024]{1,0:T(8,128)(2,1)S(1)}, bf16[256,1024]{1,0:T(8,128)(2,1)S(1)}, u32[]{:S(2)}, u32[]{:S(2)}) collective-permute-start(bf16[256,1024]{1,0:T(8,128)(2,1)S(1)} %far_sum.6), channel_id=1, source_target_pairs={{0,1},{1,0},{2,3},{3,2},{4,5},{5,4},{6,7},{7,6},{8,9},{9,8},{10,11... | collective-permute-start | bytes 1572872 | tf_op jit(solution)/shard_map/ppermute | solution.py:26
  194.5 12.7 %collective-permute-start.56 = (bf16[256,1024]{1,0:T(8,128)(2,1)S(1)}, bf16[256,1024]{1,0:T(8,128)(2,1)S(1)}, u32[]{:S(2)}, u32[]{:S(2)}) collective-permute-start(bf16[256,1024]{1,0:T(8,128)(2,1)S(1)} %get-tuple-element.267.h0), channel_id=1, source_target_pairs={{0,1},{1,0},{2,3},{3,2},{4,5},{5,4},{6,7},{7,6},{8,9},{9,8},{10,11... | collective-permute-start | bytes 1572872 | tf_op jit(solution)/shard_map/ppermute | solution.py:26
  195.4 14.3 %collective-permute-start.52 = (bf16[4,64,1024]{2,1,0:T(8,128)(2,1)S(1)}, bf16[4,64,1024]{2,1,0:T(8,128)(2,1)S(1)}, u32[]{:S(2)}, u32[]{:S(2)}) collective-permute-start(bf16[4,64,1024]{2,1,0:T(8,128)(2,1)S(1)} %leave_sum.3), channel_id=1, source_target_pairs={{0,2},{1,3},{2,0},{3,1},{4,6},{5,7},{6,4},{7,5},{8,10},{9,11},{10,... | collective-permute-start | bytes 1572872 | tf_op jit(solution)/shard_map/ppermute | solution.py:26
  197.0 12.7 %collective-permute-start.49 = (bf16[4,64,1024]{2,1,0:T(8,128)(2,1)S(1)}, bf16[4,64,1024]{2,1,0:T(8,128)(2,1)S(1)}, u32[]{:S(2)}, u32[]{:S(2)}) collective-permute-start(bf16[4,64,1024]{2,1,0:T(8,128)(2,1)S(1)} %get-tuple-element.252), channel_id=1, source_target_pairs={{0,16},{8,24},{16,0},{24,8},{1,17},{9,25},{17,1},{25,9},{2,18},{10... | collective-permute-start | bytes 1572872 | tf_op jit(solution)/shard_map/ppermute | solution.py:26
  198.2 11.8 %collective-permute-start.55 = (bf16[256,1024]{1,0:T(8,128)(2,1)S(1)}, bf16[256,1024]{1,0:T(8,128)(2,1)S(1)}, u32[]{:S(2)}, u32[]{:S(2)}) collective-permute-start(bf16[256,1024]{1,0:T(8,128)(2,1)S(1)} %get-tuple-element.267.h0), channel_id=1, source_target_pairs={{0,8},{8,0},{16,24},{24,16},{1,9},{9,1},{17,25},{25,17},{2,10},{10... | collective-permute-start | bytes 1572872 | tf_op jit(solution)/shard_map/ppermute | solution.py:26
  208.9 13.6 %collective-permute-start.58 = (bf16[4,64,1024]{2,1,0:T(8,128)(2,1)S(1)}, bf16[4,64,1024]{2,1,0:T(8,128)(2,1)S(1)}, u32[]{:S(2)}, u32[]{:S(2)}) collective-permute-start(bf16[4,64,1024]{2,1,0:T(8,128)(2,1)S(1)} %get-tuple-element.246), channel_id=1, source_target_pairs={{0,16},{8,24},{16,0},{24,8},{1,17},{9,25},{17,1},{25,9},{2,18},{10... | collective-permute-start | bytes 1572872 | tf_op jit(solution)/shard_map/ppermute | solution.py:26
  227.7 15.0 %collective-permute-start.59 = (bf16[256,256]{1,0:T(8,128)(2,1)S(1)}, bf16[256,256]{1,0:T(8,128)(2,1)S(1)}, u32[]{:S(2)}, u32[]{:S(2)}) collective-permute-start(bf16[256,256]{1,0:T(8,128)(2,1)S(1)} %get-tuple-element.278), channel_id=1, source_target_pairs={{0,8},{8,0},{16,24},{24,16},{1,9},{9,1},{17,25},{25,17},{2,10},{10... | collective-permute-start | bytes 393224 | tf_op jit(solution)/shard_map/ppermute | solution.py:26
  227.7 14.9 %collective-permute-start.61 = (bf16[256,256]{1,0:T(8,128)(2,1)S(1)}, bf16[256,256]{1,0:T(8,128)(2,1)S(1)}, u32[]{:S(2)}, u32[]{:S(2)}) collective-permute-start(bf16[256,256]{1,0:T(8,128)(2,1)S(1)} %far_sum.7), channel_id=1, source_target_pairs={{0,1},{1,0},{2,3},{3,2},{4,5},{5,4},{6,7},{7,6},{8,9},{9,8},{10,11... | collective-permute-start | bytes 393224 | tf_op jit(solution)/shard_map/ppermute | solution.py:26
  241.8 21.8 %collective-permute-start.68 = (bf16[4,64,1024]{2,1,0:T(8,128)(2,1)}, bf16[4,64,1024]{2,1,0:T(8,128)(2,1)}, u32[]{:S(2)}, u32[]{:S(2)}) collective-permute-start(bf16[4,64,1024]{2,1,0:T(8,128)(2,1)} %get-tuple-element.284), channel_id=1, source_target_pairs={{0,16},{8,24},{16,0},{24,8},{1,17},{9,25},{17,1},{25,9},{2,18},{10... | collective-permute-start | bytes 1572872 | tf_op jit(solution)/shard_map/ppermute | solution.py:26
  244.0 23.9 %collective-permute-start.48 = (bf16[256,1024]{1,0:T(8,128)(2,1)}, bf16[256,1024]{1,0:T(8,128)(2,1)}, u32[]{:S(2)}, u32[]{:S(2)}) collective-permute-start(bf16[256,1024]{1,0:T(8,128)(2,1)} %get-tuple-element.251), channel_id=1, source_target_pairs={{0,8},{8,0},{16,24},{24,16},{1,9},{9,1},{17,25},{25,17},{2,10},{10... | collective-permute-start | bytes 1572872 | tf_op jit(solution)/shard_map/ppermute | solution.py:26
  255.7 19.8 %collective-permute-start.72 = (bf16[4,64,1024]{2,1,0:T(8,128)(2,1)}, bf16[4,64,1024]{2,1,0:T(8,128)(2,1)}, u32[]{:S(2)}, u32[]{:S(2)}) collective-permute-start(bf16[4,64,1024]{2,1,0:T(8,128)(2,1)} %leave_sum.4), channel_id=1, source_target_pairs={{0,2},{1,3},{2,0},{3,1},{4,6},{5,7},{6,4},{7,5},{8,10},{9,11},{10,... | collective-permute-start | bytes 1572872 | tf_op jit(solution)/shard_map/ppermute | solution.py:26
  258.1 17.4 %collective-permute-start.71 = (bf16[4,64,1024]{2,1,0:T(8,128)(2,1)}, bf16[4,64,1024]{2,1,0:T(8,128)(2,1)}, u32[]{:S(2)}, u32[]{:S(2)}) collective-permute-start(bf16[4,64,1024]{2,1,0:T(8,128)(2,1)} %get-tuple-element.298), channel_id=1, source_target_pairs={{0,16},{8,24},{16,0},{24,8},{1,17},{9,25},{17,1},{25,9},{2,18},{10... | collective-permute-start | bytes 1572872 | tf_op jit(solution)/shard_map/ppermute | solution.py:26
  264.9 15.9 %collective-permute-start.70 = (bf16[2,64,1024]{2,1,0:T(8,128)(2,1)}, bf16[2,64,1024]{2,1,0:T(8,128)(2,1)S(1)}, u32[]{:S(2)}, u32[]{:S(2)}) collective-permute-start(bf16[2,64,1024]{2,1,0:T(8,128)(2,1)} %copy-done.68), channel_id=1, source_target_pairs={{0,4},{1,5},{2,6},{3,7},{4,0},{5,1},{6,2},{7,3},{8,12},{9,13},{10,... | collective-permute-start | bytes 786440 | tf_op jit(solution)/shard_map/ppermute | solution.py:26
  267.9 23.1 %collective-permute-start.47 = (bf16[256,1024]{1,0:T(8,128)(2,1)}, bf16[256,1024]{1,0:T(8,128)(2,1)S(1)}, u32[]{:S(2)}, u32[]{:S(2)}) collective-permute-start(bf16[256,1024]{1,0:T(8,128)(2,1)} %copy-done.65), channel_id=1, source_target_pairs={{0,8},{8,0},{16,24},{24,16},{1,9},{9,1},{17,25},{25,17},{2,10},{10... | collective-permute-start | bytes 1572872 | tf_op jit(solution)/shard_map/ppermute | solution.py:26
  271.4 19.6 %collective-permute-start.65 = (bf16[256,1024]{1,0:T(8,128)(2,1)S(1)}, bf16[256,1024]{1,0:T(8,128)(2,1)S(1)}, u32[]{:S(2)}, u32[]{:S(2)}) collective-permute-start(bf16[256,1024]{1,0:T(8,128)(2,1)S(1)} %far_sum.8), channel_id=1, source_target_pairs={{0,1},{1,0},{2,3},{3,2},{4,5},{5,4},{6,7},{7,6},{8,9},{9,8},{10,11... | collective-permute-start | bytes 1572872 | tf_op jit(solution)/shard_map/ppermute | solution.py:26
  297.8 21.5 %collective-permute-start.74 = (bf16[256,1024]{1,0:T(8,128)(2,1)S(1)}, bf16[256,1024]{1,0:T(8,128)(2,1)S(1)}, u32[]{:S(2)}, u32[]{:S(2)}) collective-permute-start(bf16[256,1024]{1,0:T(8,128)(2,1)S(1)} %get-tuple-element.312), channel_id=1, source_target_pairs={{0,8},{8,0},{16,24},{24,16},{1,9},{9,1},{17,25},{25,17},{2,10},{10... | collective-permute-start | bytes 1572872 | tf_op jit(solution)/shard_map/ppermute | solution.py:26
  299.2 21.1 %collective-permute-start.77 = (bf16[4,64,1024]{2,1,0:T(8,128)(2,1)S(1)}, bf16[4,64,1024]{2,1,0:T(8,128)(2,1)S(1)}, u32[]{:S(2)}, u32[]{:S(2)}) collective-permute-start(bf16[4,64,1024]{2,1,0:T(8,128)(2,1)S(1)} %leave_sum.5), channel_id=1, source_target_pairs={{0,2},{1,3},{2,0},{3,1},{4,6},{5,7},{6,4},{7,5},{8,10},{9,11},{10,... | collective-permute-start | bytes 1572872 | tf_op jit(solution)/shard_map/ppermute | solution.py:26
  299.2 21.1 %collective-permute-start.76 = (bf16[4,64,1024]{2,1,0:T(8,128)(2,1)S(1)}, bf16[4,64,1024]{2,1,0:T(8,128)(2,1)S(1)}, u32[]{:S(2)}, u32[]{:S(2)}) collective-permute-start(bf16[4,64,1024]{2,1,0:T(8,128)(2,1)S(1)} %copy-done.67), channel_id=1, source_target_pairs={{0,16},{8,24},{16,0},{24,8},{1,17},{9,25},{17,1},{25,9},{2,18},{10... | collective-permute-start | bytes 1572872 | tf_op jit(solution)/shard_map/ppermute | solution.py:26
  305.1 13.2 %collective-permute-start.87 = (bf16[2,64,1024]{2,1,0:T(8,128)(2,1)S(1)}, bf16[2,64,1024]{2,1,0:T(8,128)(2,1)S(1)}, u32[]{:S(2)}, u32[]{:S(2)}) collective-permute-start(bf16[2,64,1024]{2,1,0:T(8,128)(2,1)S(1)} %append.26.a_ref), channel_id=1, source_target_pairs={{0,16},{8,24},{16,0},{24,8},{1,17},{9,25},{17,1},{25,9},{2,18},{10... | collective-permute-start | bytes 786440 | tf_op jit(solution)/shard_map/ppermute | solution.py:26
  305.5 14.7 %collective-permute-start.78 = (bf16[2,64,1024]{2,1,0:T(8,128)(2,1)S(1)}, bf16[2,64,1024]{2,1,0:T(8,128)(2,1)S(1)}, u32[]{:S(2)}, u32[]{:S(2)}) collective-permute-start(bf16[2,64,1024]{2,1,0:T(8,128)(2,1)S(1)} %get-tuple-element.300), channel_id=1, source_target_pairs={{0,4},{1,5},{2,6},{3,7},{4,0},{5,1},{6,2},{7,3},{8,12},{9,13},{10,... | collective-permute-start | bytes 786440 | tf_op jit(solution)/shard_map/ppermute | solution.py:26
  318.3 23.7 %collective-permute-start.88 = (bf16[4,64,1024]{2,1,0:T(8,128)(2,1)S(1)}, bf16[4,64,1024]{2,1,0:T(8,128)(2,1)S(1)}, u32[]{:S(2)}, u32[]{:S(2)}) collective-permute-start(bf16[4,64,1024]{2,1,0:T(8,128)(2,1)S(1)} %append.27.mine_ref), channel_id=1, source_target_pairs={{0,8},{8,0},{16,24},{24,16},{1,9},{9,1},{17,25},{25,17},{2,10},{10... | collective-permute-start | bytes 1572872 | tf_op jit(solution)/shard_map/ppermute | solution.py:26
  320.5 13.8 %collective-permute-start.79 = (bf16[2,64,1024]{2,1,0:T(8,128)(2,1)S(1)}, bf16[2,64,1024]{2,1,0:T(8,128)(2,1)S(1)}, u32[]{:S(2)}, u32[]{:S(2)}) collective-permute-start(bf16[2,64,1024]{2,1,0:T(8,128)(2,1)S(1)} %get-tuple-element.319), channel_id=1, source_target_pairs={{0,4},{1,5},{2,6},{3,7},{4,0},{5,1},{6,2},{7,3},{8,12},{9,13},{10,... | collective-permute-start | bytes 786440 | tf_op jit(solution)/shard_map/ppermute | solution.py:26
  323.4 30.6 %collective-permute-start.73 = (bf16[256,1024]{1,0:T(8,128)(2,1)}, bf16[256,1024]{1,0:T(8,128)(2,1)S(1)}, u32[]{:S(2)}, u32[]{:S(2)}) collective-permute-start(bf16[256,1024]{1,0:T(8,128)(2,1)} %get-tuple-element.310), channel_id=1, source_target_pairs={{0,8},{8,0},{16,24},{24,16},{1,9},{9,1},{17,25},{25,17},{2,10},{10... | collective-permute-start | bytes 1572872 | tf_op jit(solution)/shard_map/ppermute | solution.py:26
  323.7 12.3 %collective-permute-start.83 = (bf16[1,64,1024]{2,1,0:T(8,128)(2,1)S(1)}, bf16[1,64,1024]{2,1,0:T(8,128)(2,1)S(1)}, u32[]{:S(2)}, u32[]{:S(2)}) collective-permute-start(bf16[1,64,1024]{2,1,0:T(8,128)(2,1)S(1)} %get-tuple-element.316), channel_id=1, source_target_pairs={{0,1},{1,0},{2,3},{3,2},{4,5},{5,4},{6,7},{7,6},{8,9},{9,8},{10,11... | collective-permute-start | bytes 393224 | tf_op jit(solution)/shard_map/ppermute | solution.py:26
  336.1 10.9 %collective-permute-start.84 = (bf16[2,64,1024]{2,1,0:T(8,128)(2,1)S(1)}, bf16[2,64,1024]{2,1,0:T(8,128)(2,1)S(1)}, u32[]{:S(2)}, u32[]{:S(2)}) collective-permute-start(bf16[2,64,1024]{2,1,0:T(8,128)(2,1)S(1)} %append.24.a_ref), channel_id=1, source_target_pairs={{0,16},{8,24},{16,0},{24,8},{1,17},{9,25},{17,1},{25,9},{2,18},{10... | collective-permute-start | bytes 786440 | tf_op jit(solution)/shard_map/ppermute | solution.py:26
  338.3 12.2 %collective-permute-start.81 = (bf16[2,64,1024]{2,1,0:T(8,128)(2,1)S(1)}, bf16[2,64,1024]{2,1,0:T(8,128)(2,1)S(1)}, u32[]{:S(2)}, u32[]{:S(2)}) collective-permute-start(bf16[2,64,1024]{2,1,0:T(8,128)(2,1)S(1)} %append.22.a_ref), channel_id=1, source_target_pairs={{0,16},{8,24},{16,0},{24,8},{1,17},{9,25},{17,1},{25,9},{2,18},{10... | collective-permute-start | bytes 786440 | tf_op jit(solution)/shard_map/ppermute | solution.py:26
  341.2 18.0 %collective-permute-start.75 = (bf16[256,1024]{1,0:T(8,128)(2,1)}, bf16[256,1024]{1,0:T(8,128)(2,1)}, u32[]{:S(2)}, u32[]{:S(2)}) collective-permute-start(bf16[256,1024]{1,0:T(8,128)(2,1)} %far_sum.9), channel_id=1, source_target_pairs={{0,1},{1,0},{2,3},{3,2},{4,5},{5,4},{6,7},{7,6},{8,9},{9,8},{10,11... | collective-permute-start | bytes 1572872 | tf_op jit(solution)/shard_map/ppermute | solution.py:26
  347.0 17.6 %collective-permute-start.85 = (bf16[4,64,1024]{2,1,0:T(8,128)(2,1)S(1)}, bf16[4,64,1024]{2,1,0:T(8,128)(2,1)}, u32[]{:S(2)}, u32[]{:S(2)}) collective-permute-start(bf16[4,64,1024]{2,1,0:T(8,128)(2,1)S(1)} %append.25.mine_ref), channel_id=1, source_target_pairs={{0,8},{8,0},{16,24},{24,16},{1,9},{9,1},{17,25},{25,17},{2,10},{10... | collective-permute-start | bytes 1572872 | tf_op jit(solution)/shard_map/ppermute | solution.py:26
  350.5 16.8 %collective-permute-start.82 = (bf16[4,64,1024]{2,1,0:T(8,128)(2,1)S(1)}, bf16[4,64,1024]{2,1,0:T(8,128)(2,1)}, u32[]{:S(2)}, u32[]{:S(2)}) collective-permute-start(bf16[4,64,1024]{2,1,0:T(8,128)(2,1)S(1)} %append.23.mine_ref), channel_id=1, source_target_pairs={{0,8},{8,0},{16,24},{24,16},{1,9},{9,1},{17,25},{25,17},{2,10},{10... | collective-permute-start | bytes 1572872 | tf_op jit(solution)/shard_map/ppermute | solution.py:26
  (109 other events, 1354.4 us)

commit v2 on v1

--- a/solution.py
+++ b/solution.py
@@ -141,6 +141,7 @@
     shard, dim = w_out.shape
     quarter = dim // TEAM
     rows, fb = shard // ny, w_down.shape[0] // TEAM
+    low = fb // ny
     copies = []
     for away in (0, 1):
         def who(i, away=away):
@@ -155,19 +156,17 @@
             for k in range(ns):
                 copies.append((2, 2 + away, lambda i: i[1] * rows,
                                lambda i, w=who, k=k: (k * TEAM + w(i)) * fb, (rows, fb), k * fb))
-        for h in (0, 1):
-            copies.append((3, 4 + 2 * h + away, lambda i, w=who, h=h: w(i) * fb + h * (fb // 2),
-                           lambda i: 0, (fb // 2, dim), 0))
-    sizes = [(rows, dim)] * 2 + [(rows, ns * fb)] * 2 + [(fb // 2, dim)] * 4
+        copies.append((3, 4 + away, lambda i, w=who: w(i) * fb + i[1] * low, lambda i: 0, (low, dim), 0))
+    sizes = [(rows, dim)] * 2 + [(rows, ns * fb)] * 2 + [(low, dim)] * 2
     out = pl.pallas_call(
         functools.partial(share_kernel, 4, copies),
         out_shape=[jax.ShapeDtypeStruct(s, bf16) for s in sizes],
         in_specs=[scalar_spec()] + [any_spec()] * 4,
-        out_specs=[whole_spec()] * 8,
+        out_specs=[whole_spec()] * 6,
         scratch_shapes=[pltpu.SemaphoreType.DMA((len(copies),))],
         name="shares",
     )(idx, w_qkv, w_out, w_up, w_down)
-    out = [list(out[k : k + 2]) for k in (0, 2, 4, 6)]
+    out = [list(out[k : k + 2]) for k in (0, 2, 4)]
     if fb % LANES:
         mine = lax.dynamic_slice_in_dim(w_up, idx[1] * rows, rows, 0).reshape(rows, ns, TEAM, fb)
         out[1] = [pick(mine, idx[0] ^ r, 2).reshape(rows, ns * fb) for r in (0, 2)]
@@ -1154,18 +1153,17 @@
         return jax.ShapeDtypeStruct(shape, dtype)
 
 
-    share_attn, share_up, *share_down = shares(idx, w_qkv, w_out, w_up, w_down, ny, ns)
+    share_attn, share_up, share_down = shares(idx, w_qkv, w_out, w_up, w_down, ny, ns)
     attn, up = Gathering(*share_attn, True), Gathering(*share_up, True)
-    down = [Gathering(*share, False) for share in share_down]
+    down = Gathering(*share_down, True)
     attn_pair = attn.step()
     x_blocks = gather_team(after(tokens[0], attn_pair))
-    up.step(attn_pair)
+    up_pair = up.step(attn_pair)
     attn_first = attn.rest()
-    for part in down:
-        part.step(attn_first)
-    attn_second = attn.step()
+    attn_own = attn.a
+    down_pair = down.step(attn_first)
+    attn_second = attn.step(up_pair)
     attn_third = attn.across(0)
-    attn_last = attn.across(1)
     small = call(
         pack_kernel,
         "pack_small",
@@ -1174,7 +1172,7 @@
         0,
     )
     for bit in [1] + high_bits("seq")[::-1]:
-        got = swap(small, "seq", bit)
+        got = swap(after(small, attn_own) if bit > 2 else small, "seq", bit)
         upper = (seq & bit) != 0
         small = jnp.concatenate([jnp.where(upper, got, small), jnp.where(upper, small, got)], axis=0)
     small = small.astype(f32)
@@ -1214,6 +1212,7 @@
 
     a = jnp.exp(-rate)
     s_mid, s_end = local_ends(u, a)
+    attn_last = attn.across(1, s_end)
     up_first = up.rest((attn_second, s_end))
     decay = jnp.exp(-half_rate * rows)
     first_end, second_end = by_half(gin * s_end)
@@ -1231,7 +1230,7 @@
             step *= 2
         return exclusive
 
-    entering = chain(after(decay * first_end + second_end, attn_third), False, up_first)
+    entering = chain(after(decay * first_end + second_end, attn_third), False, (up_first, attn_last))
     state_zero = jnp.exp(-half_rate * (span * block).astype(f32)) * init + entering
     state_one = decay * state_zero + first_end
     state_two = decay * state_one + second_end
@@ -1241,21 +1240,19 @@
     on_second = by_owner(jnp.zeros_like(init), jnp.ones_like(init))
     h_mid = jnp.exp(-rate * (rows - CTX)) * state_in + gin * s_mid
     h_mid = jnp.where(on_second > 0, h_mid, init_twice)
-    h_mid = after(h_mid, (attn_second, attn_last))
     y_first, y_second = contexts(half, u, a, gin * on_second, gout, h_mid)
     passed = lax.ppermute(y_second, "seq", [(k, k + 2) for k in range(ns - 2)])
     up_second = up.step(entering)
     up_third = up.across(0)
-    context = jnp.where(block == 0, y_first, after(passed, up_second))
-    down_first = down[0].rest(passed)
-    down_second = down[1].rest(up_third)
-    context = gather_team(context)
-
     places = jnp.stack([place[0], seq]).astype(jnp.int32)
     full_qkv, *full_out = place_weight(idx, places, [(attn.pieces, 0, 1, 0)], 3 * width)
-    full_qkv = after(full_qkv, (down_first, up_third))
     full_out = trade_team(full_out)
+    context = jnp.where(block == 0, y_first, after(passed, (up_second, full_qkv, down_pair)))
+    down_first = down.rest(passed)
+
+    full_qkv = after(full_qkv, up_third)
     qkv = dot_nn(inputs_low, full_qkv).astype(bf16)
+    context = after(gather_team(context), qkv)
     ctx_kv, context = call(
         context_kv_kernel,
         "context_kv",
@@ -1264,15 +1261,15 @@
     )
     attended = attend(half, qkv, ctx_kv)
 
-    down_third = down[0].step(down_second)
     up_last = up.across(1, up_third)
-    attended = after(attended, (g_blocks[2], down_second))
+    attended = after(attended, (g_blocks[2], down_first, up_last))
+    down_second = down.step()
+    down_third = down.across(0, up_last)
     attended_parts = call(out_kernel, "out_dot", part_types(rows, dim), (idx, attended, *full_out))
-    attended_parts = sum_team(attended_parts, None, (ends, down_third, up_last))
-    down[1].step(down_third)
+    attended_parts = sum_team(attended_parts, None, (down_second, down_third))
+    down.across(1, down_third)
     (full_up,) = place_weight(idx, places, [(up.pieces, 0, 1, 0)])
-    down = [(part.pieces, 1, 2, h) for h, part in enumerate(down)]
-    (full_down,) = place_weight(idx, places, down)
+    (full_down,) = place_weight(idx, places, [(down.pieces, 0, 1, 0)])
 
     hidden, inv_two, mlp_in = call(
         second_norm_kernel,
@@ -1282,6 +1279,7 @@
         0,
     )
     mlp_in = gather_team(mlp_in)
+    mlp_in = after(mlp_in, full_up)
     act, d_pre, *d_mlp = feed_forward(mlp_in, g_blocks, full_up, full_down)
     d_down = down_grad(act, g_blocks)
     reduction = HalvedReduction if (nd, ns) == (4, 8) else Reduction
@@ -1318,16 +1316,17 @@
     d_qkv, d_ctx_kv = attend_back(half, qkv, ctx_kv, after(d_attended, d_out))
     d_out = trade_team(d_out)
     sum_up.step(d_ctx_kv)
+    sum_down.step(sum_up.sent)
     d_context = call(
         context_grad_kernel,
         "context_grad",
         part_types(2 * CTX, cols),
-        (idx, after(d_ctx_kv, sum_up.sent), full_qkv),
+        (idx, after(d_ctx_kv, (sum_up.sent, sum_down.sent, d_out)), full_qkv),
     )
     d_attn = attn_grad(idx, inputs_low, after(d_qkv, d_context), context, d_ctx_kv, d_out)
     sum_attn = reduction(d_attn, place)
     sum_attn.step()
-    d_context = sum_team(d_context, None, sum_attn.sent)
+    d_context = sum_team(d_context, None, d_attn)
     d_context = call(context_sum_kernel, "context_sum", like((2 * CTX, cols), bf16), d_context[:3], 0)
     came = lax.ppermute(d_context, "seq", [(k + 2, k) for k in range(ns - 2)])
     flags = jnp.stack([seq % 2, block]).astype(jnp.int32)
@@ -1335,37 +1334,43 @@
         context_rows_kernel,
         "context_rows",
         (like((CTX,) + half_tile, f32), like((CTX,) + tile, f32), like((CTX,) + tile, f32)),
-        (flags, came, d_context),
+        (flags, after(came, (ends, sum_attn.sent)), d_context),
     )
 
     lam_mid = tail_adjoint(dy, a, gout)
     g_second = jnp.exp(-half_rate * (rows - CTX + 1)) * lam_mid + decay * end_cot[1]
     d_a, d_gout, g_init = first_context_back(after(dy0_full, lam_mid), a, gout, init_twice)
-    leaving = chain(decay * (end_cot[0] + g_second), True, (g_init, sum_attn.out if reduction is HalvedReduction else g_init))
+    d_down_pair = sum_down.last()
+    leaving = chain(decay * (end_cot[0] + g_second), True, (g_init, d_down_pair[1], sum_attn.out if reduction is HalvedReduction else g_init))
     sum_up.step(leaving)
     sum_attn.step(sum_up.sent)
-    sum_down.step(sum_attn.sent)
     result = sum_team(result, d_context)
     result = call(result_kernel, "result_sum", like((rows, dim), bf16), (hidden, *result[:3]), 0)
     lam_end = by_owner(end_cot[0] + g_second + decay * leaving, end_cot[1] + leaving)
     du, d_gin, d_a, d_gout, g_in = ssm_back(
-        u, dy_full, a, gin, gout, state_in, after(lam_end, sum_down.sent), d_a, d_gout
+        u, dy_full, a, gin, gout, state_in, after(lam_end, sum_attn.sent), d_a, d_gout
     )
     g_first = by_half(g_in)[0]
     d_init = g_init[:, : tile[0] // 2] + jnp.where(block == 0, g_first, jnp.zeros_like(g_first))
     d_rate = -a * d_a
 
+    sum_up.step(du)
     *d_inputs, d_gain_one = call(
         inputs_grad_kernel,
         "inputs_grad",
         part_types(rows, dim) + (jax.ShapeDtypeStruct((1, dim), f32),),
-        (idx, d_qkv, full_qkv, after(du, result), inv_one, *x_blocks),
+        (idx, d_qkv, full_qkv, after(du, (result, sum_up.sent)), inv_one, *x_blocks),
         scratch_shapes=[pltpu.VMEM((rows, dim), f32)],
     )
+    sum_attn.step(d_gain_one)
+    d_inputs = after(d_inputs, sum_attn.sent)
     *d_inputs, d_inputs_far = sum_team(d_inputs)
-    sum_up.step(d_inputs_far)
-    sum_attn.step(sum_up.sent)
-    d_down = spread_weight("down", sum_down.last(), idx, [w_down.shape])[0]
+    d_up_pair = after(sum_up.last(), d_inputs_far)
+    d_down = spread_weight("down", d_down_pair, idx, [w_down.shape])[0]
+    if fb % LANES:
+        d_up = spread_narrow(d_up_pair, idx, w_up.shape, fb)
+    else:
+        d_up = spread_weight("up", d_up_pair, idx, [w_up.shape], fb)[0]
     d_tokens = call(
         tokens_grad_kernel,
         "tokens_grad",
@@ -1380,12 +1385,14 @@
     pack = [d_params.reshape(-1, LANES), d_gains.reshape(-1, LANES), d_init.reshape(-1, LANES)]
     pack = after(jnp.concatenate(pack, axis=0), d_inputs_far)
     for n, bit in enumerate(high_bits("seq")):
+        if n == 0:
+            pack = after(pack, (sum_attn.step(), d_tokens))
         if n == 1:
-            pack = after(pack, sum_attn.step())
+            pack = after(pack, d_down)
         pack = pack + swap(pack, "seq", bit)
     one, two = 3 * NST * cols // LANES, 3 * NST * cols // LANES + 2 * dim // LANES
     shared = pack[:two]
-    shared = after(shared, d_down)
+    shared = after(shared, d_up)
     for bit in high_bits("dp"):
         shared = shared + swap(shared, "dp", bit)
     packs = gather_team(jnp.concatenate([shared, pack[two:]], axis=0))
@@ -1412,10 +1419,6 @@
         state_grad = pick(state_grad, member % 2, 1)
         state_grad = lax.dynamic_slice_in_dim(state_grad, inner, shard, 1).T[None]
 
-    if fb % LANES:
-        d_up = spread_narrow(sum_up.last(), idx, w_up.shape, fb)
-    else:
-        d_up = spread_weight("up", sum_up.last(), idx, [w_up.shape], fb)[0]
     d_wqkv, d_out = spread_weight("attn", sum_attn.last(), idx, [w_qkv.shape, w_out.shape])
     return (
         result[None],

time: 371 us -> 350 us (0.943)
  waiting for transfers between devices: 118 us -> 85.8 us
  other arithmetic: 8.34 us -> 15.2 us
  starting transfers between devices: 110 us -> 114 us
    ppermute x85 -> x84, waiting for transfers between devices: 105 us -> 82 us  [swap(): lax.ppermute(a, axis, [(k, k ^ bit) for k in range(lax.axis_size(axis))])]
    ppermute x1, waiting for transfers between devices: 6.35 us -> 0.01 us  [on_device(): came = lax.ppermute(d_context, 'seq', [(k + 2, k) for k in range(ns - 2)])]
    ppermute x4, waiting for transfers between devices: 6.25 us -> 1.29 us  [swap_team(): return lax.ppermute(a, ('dp', 'seq'), pairs)]
    ppermute x85 -> x84, starting transfers between devices: 88.3 us -> 92.3 us  [swap(): lax.ppermute(a, axis, [(k, k ^ bit) for k in range(lax.axis_size(axis))])]
    pallas_call x60 -> x58, Pallas kernels: 54.3 us -> 52.6 us  [call(): pl.pallas_call(kernel, grid=(1,), out_shape=out_shape, in_specs=specs, ou...]
    unnamed x156 -> x138, local copies, waits for them, and re-layouts: 16.6 us -> 16.5 us
  transfers between devices with their start and end apart: 95 -> 94, of which waited for: 30 -> 28; matrix products, arithmetic and copies ran while one was open for 4% -> 6% of each run, Pallas kernels for 22% -> 25%
where the time goes in v2:
time: 350 us; the launch traced here: 348 us
  starting transfers between devices  114 us (33%)
  Pallas kernels  106 us (30%)
  waiting for transfers between devices  85.8 us (25%)
  local copies, waits for them, and re-layouts  23 us (7%)
  other arithmetic  15.2 us (4%)
    ppermute x84, starting transfers between devices, swap(): lax.ppermute(a, axis, [(k, k ^ bit) for k in range(lax.axis_size(axis))])  92.3 us
    ppermute x84, waiting for transfers between devices, swap(): lax.ppermute(a, axis, [(k, k ^ bit) for k in range(lax.axis_size(axis))])  82 us
    pallas_call x58, Pallas kernels, call(): pl.pallas_call(kernel, grid=(1,), out_shape=out_shape, in_specs=specs, ou...  52.6 us
    unnamed x138, local copies, waits for them, and re-layouts  16.5 us
    pallas_call x1, Pallas kernels, feed_forward(): pl.pallas_call(mlp_kernel, grid=(units // step,), out_shape=(unit_out, un...  11.5 us
    ppermute x4, starting transfers between devices, chain(): lax.ppermute(inclusive, 'seq', [(t, f) for f, t in pairs] if back else pa...  11.3 us
    pallas_call x1, Pallas kernels, ssm_back(): pl.pallas_call(back_kernel, grid=(NST // GROUP,), out_shape=(jax.ShapeDty...  9.99 us
    pallas_call x1, Pallas kernels, attend_back(): pl.pallas_call(attend_back_kernel, grid_spec=pltpu.PrefetchScalarGridSpec...  7.18 us
  transfers between devices with their start and end apart: 94, of which 28 were waited for; matrix products, arithmetic and copies ran while one was open for 6% of the time, Pallas kernels for 25%

profile of v2, /device:TPU:1, one launch (start us, length us, event | category | flops | bytes accessed | tf_op | source)
XLA Modules:
  0.0 348.4 jit_solution(9514890161413248968)
XLA Ops:
  1.3 3.0 shares.1
  4.4 2.1 collective-permute-start
  7.7 1.6 collective-permute-start.1
  12.5 2.2 collective-permute-start.3
  14.9 2.5 collective-permute-start.5
  17.4 1.6 collective-permute-start.8
  19.0 11.0 %collective-permute-done.4.b_ref = bf16[2,64,1024]{2,1,0:T(8,128)(2,1)S(1)} collective-permute-done((bf16[2,64,1024]{2,1,0:T(8,128)(2,1)S(1)}, bf16[2,64,1024]{2,1,0:T(8,128)(2,1)S(1)}, u32[]{:S(2)}, u32[]{:S(2)}) %collective-permute-start.4) | collective-permute-done | bytes 262176 | tf_op jit(solution)/shard_map/ppermute | solution.py:26
  36.8 2.0 first_norm.1
  44.0 3.2 collective-permute-start.12
  49.0 3.0 collective-permute-start.18
  54.3 2.2 collective-permute-start.14
  57.5 1.5 collective-permute-done.12.b_ref
  59.0 2.2 collective-permute-start.17
  62.0 5.7 %collective-permute-start.19 = (f32[16,4,128]{2,1,0:T(4,128)S(1)}, f32[16,4,128]{2,1,0:T(4,128)S(1)}, u32[]{:S(2)}, u32[]{:S(2)}) collective-permute-start(f32[16,4,128]{2,1,0:T(4,128)S(1)} %multiply_add_fusion.6), channel_id=1, source_target_pairs={{0,4},{1,5},{2,6},{3,7},{8,12},{9,13},{10,14},{11,15},{16,20},{17,... | collective-permute-start | bytes 98312 | tf_op jit(solution)/shard_map/ppermute | solution.py:1225
  70.8 1.6 multiply_add_fusion.3
  73.3 2.8 ssm_context.1
  76.7 4.0 %collective-permute-start.20 = (bf16[256,256]{1,0:T(8,128)(2,1)}, bf16[256,256]{1,0:T(8,128)(2,1)}, u32[]{:S(2)}, u32[]{:S(2)}) collective-permute-start(bf16[256,256]{1,0:T(8,128)(2,1)} %get-tuple-element.225), channel_id=1, source_target_pairs={{0,2},{1,3},{2,4},{3,5},{4,6},{5,7},{8,10},{9,11},{10,12},{11,13},... | collective-permute-start | bytes 393224 | tf_op jit(solution)/shard_map/ppermute | solution.py:1244
  82.7 1.7 place_weight.3
  84.4 2.2 collective-permute-done.20
  89.3 6.9 %collective-permute-done.24.c2 = bf16[256,256]{1,0:T(8,128)(2,1)S(1)} collective-permute-done((bf16[256,256]{1,0:T(8,128)(2,1)S(1)}, bf16[256,256]{1,0:T(8,128)(2,1)S(1)}, u32[]{:S(2)}, u32[]{:S(2)}) %collective-permute-start.24) | collective-permute-done | bytes 131104 | tf_op jit(solution)/shard_map/ppermute | solution.py:26
  96.2 1.7 collective-permute-start.25
  102.0 1.8 convolution_convert_fusion.q0.q1.k0.k1.v0.v1
  104.8 5.0 %attend.1.x_ref.att_ref = bf16[1024,256]{1,0:T(8,128)(2,1)S(1)} custom-call(s32[1]{0:T(128)} %bitcast.3.late.half_ref, bf16[1024,768]{1,0:T(8,128)(2,1)S(1)} %convolution_convert_fusion.q0.q1.k0.k1.v0.v1, bf16[1024,768]{1,0:T(8,128)(2,1)S(1)} %convolution_convert_fusion.q0.q1.k0.k1.v0.v1, bf16[1024,768]{1,0:T(8,128)(2,1)S(1)} %convolution_convert_fusion.q0.q1.k0.k1.v0.v1, ...), custom_call_target="tpu_custom_call" | custom-call | tf_op jit(solution)/shard_map/attend/pallas_call | solution.py:770
  109.8 5.6 %collective-permute-done.27.b_ref = bf16[2,64,1024]{2,1,0:T(8,128)(2,1)S(1)} collective-permute-done((bf16[2,64,1024]{2,1,0:T(8,128)(2,1)S(1)}, bf16[2,64,1024]{2,1,0:T(8,128)(2,1)S(1)}, u32[]{:S(2)}, u32[]{:S(2)}) %collective-permute-start.27) | collective-permute-done | bytes 262176 | tf_op jit(solution)/shard_map/ppermute | solution.py:26
  120.0 10.9 %collective-permute-done.35.refs_1_ = bf16[4,64,1024]{2,1,0:T(8,128)(2,1)S(1)} collective-permute-done((bf16[4,64,1024]{2,1,0:T(8,128)(2,1)S(1)}, bf16[4,64,1024]{2,1,0:T(8,128)(2,1)S(1)}, u32[]{:S(2)}, u32[]{:S(2)}) %collective-permute-start.35) | collective-permute-done | bytes 524320 | tf_op jit(solution)/shard_map/ppermute | solution.py:26
  130.9 1.7 collective-permute-done.34.far
  134.6 1.8 collective-permute-start.37
  136.3 9.2 %collective-permute-done.38.m2.x2 = bf16[256,1024]{1,0:T(8,128)(2,1)S(1)} collective-permute-done((bf16[256,1024]{1,0:T(8,128)(2,1)S(1)}, bf16[256,1024]{1,0:T(8,128)(2,1)S(1)}, u32[]{:S(2)}, u32[]{:S(2)}) %collective-permute-start.38) | collective-permute-done | bytes 524320 | tf_op jit(solution)/shard_map/ppermute | solution.py:26
  145.5 1.9 collective-permute-start.39
  150.4 11.5 %feed_forward.1 = (bf16[1024,1024]{1,0:T(8,128)(2,1)S(1)}, bf16[1024,1024]{1,0:T(8,128)(2,1)S(1)}, f32[256,1024]{1,0:T(8,128)S(1)}, bf16[256,1024]{1,0:T(8,128)(...) custom-call(bf16[256,1024]{1,0:T(8,128)(2,1)S(1)} %get-tuple-element.253.m0.x0, ...), custom_call_target="tpu_custom_call" | custom-call | tf_op jit(solution)/shard_map/feed_forward/pallas_call | solution.py:899
  162.4 3.2 down_grad.1
  167.9 3.5 %up_grad.1 = bf16[1024,1024]{1,0:T(8,128)(2,1)S(1)} custom-call(bf16[256,1024]{1,0:T(8,128)(2,1)S(1)} %get-tuple-element.253.m0.x0, bf16[256,1024]{1,0:T(8,128)(2,1)S(1)} %collective-permute-done.37.m1.x1, bf16[256,1024]{1,0:T(8,128)(2,1)S(1)} %collective-permute-done.38.m2.x2, bf16[256,1024]{1,0:T(8,128)(2,1)S(1)} %collective-permute-done.39.m3.x3, ...), custom_call_target="tpu_custom_call" | custom-call | tf_op jit(solution)/shard_map/up_grad/pallas_call | solution.py:943
  172.3 2.9 down_dot.1
  177.0 2.2 collective-permute-done.46.came_ref
  185.6 1.7 collective-permute-start.51
  187.3 7.6 %collective-permute-done.52.h2 = bf16[256,1024]{1,0:T(8,128)(2,1)S(1)} collective-permute-done((bf16[256,1024]{1,0:T(8,128)(2,1)S(1)}, bf16[256,1024]{1,0:T(8,128)(2,1)S(1)}, u32[]{:S(2)}, u32[]{:S(2)}) %collective-permute-start.52) | collective-permute-done | bytes 524320 | tf_op jit(solution)/shard_map/ppermute | solution.py:26
  194.9 1.8 collective-permute-start.53
  203.6 7.2 %attend_back.1 = (bf16[1024,768]{1,0:T(8,128)(2,1)S(1)}, bf16[256,512]{1,0:T(8,128)(2,1)S(1)}) custom-call(s32[1]{0:T(128)} %bitcast.3.late.half_ref, bf16[1024,768]{1,0:T(8,128)(2,1)S(1)} %convolution_convert_fusion.q0.q1.k0.k1.v0.v1, bf16[1024,768]{1,0:T(8,128)(2,1)S(1)} %convolution_convert_fusion.q0.q1.k0.k1.v0.v1, ...), custom_call_target="tpu_custom_call" | custom-call | tf_op jit(solution)/shard_map/attend_back/pallas_call | solution.py:790
  216.2 5.1 %attn_grad.1 = bf16[1024,1024]{1,0:T(8,128)(2,1)S(1)} custom-call(s32[2]{0:T(128)S(1)} %copy-done.41, bf16[1024,1024]{1,0:T(8,128)(2,1)S(1)} %copy-done.15, bf16[1024,768]{1,0:T(8,128)(2,1)S(1)} %get-tuple-element.301.dq_ref, bf16[256,1024]{1,0:T(8,128)(2,1)S(1)} %get-tuple-element.302.ctx_ref, bf16[256,512]{1,0:T(8,128)(2,1)S(1)} %get-tuple-element.295.d_ref.dctx_ref, ...), custom_call_target="tpu_custom_call" | custom-call | tf_op jit(solution)/shard_map/attn_grad/pallas_call | solution.py:278
  238.9 3.1 collective-permute-start.72
  243.3 5.1 %first_context.1 = (f32[16,8,128]{2,1,0:T(8,128)}, f32[16,8,128]{2,1,0:T(8,128)}, f32[16,8,128]{2,1,0:T(8,128)}) custom-call(f32[128,8,128]{2,1,0:T(8,128)} %copy-done.37, f32[16,8,128]{2,1,0:T(8,128)} %copy-done.12, f32[16,8,128]{2,1,0:T(8,128)} %copy-done.25, f32[16,8,128]{2,1,0:T(8,128)} %copy-done.40), custom_call_target="tpu_custom_call" | custom-call | tf_op jit(solution)/shard_map/first_context/pallas_call | solution.py:589
  258.7 1.9 collective-permute-start.75
  263.4 10.0 %ssm_back.1 = (f32[256,8,128]{2,1,0:T(8,128)S(1)}, f32[16,8,128]{2,1,0:T(8,128)S(1)}, f32[16,8,128]{2,1,0:T(8,128)S(1)}, f32[16,8,128]{2,1,0:T(8,128)S(1)}, f32[16,8,128]{2,1,0:T(8,128)S(1)}) custom-call(f32[256,8,128]{2,1,0:T(8,128)S(1)} %get-tuple-element.205.u_ref, f32[128,8,128]{2,1,0:T(8,128)S(1)} %copy-done.39, f32[16,8,128]{2,1,0:T(8,128)S(1)} %copy-done.13, ...), custom_call_target="tpu_custom_call" | custom-call | tf_op jit(solution)/shard_map/ssm_back/pallas_call | solution.py:671
  276.0 4.5 %inputs_grad.1 = (f32[256,1024]{1,0:T(8,128)S(1)}, bf16[256,1024]{1,0:T(8,128)(2,1)}, f32[256,1024]{1,0:T(8,128)S(1)}, bf16[256,1024]{1,0:T(8,128)(2,1)S(1)}, f32[1,1024]{1,0:T(1,128)S(1)}) custom-call(s32[2]{0:T(128)S(1)} %copy-done.41, bf16[1024,768]{1,0:T(8,128)(2,1)S(1)} %copy-done.7, bf16[1024,768]{1,0:T(8,128)(2,1)S(1)} %copy-done.3, ...), custom_call_target="tpu_custom_call" | custom-call | tf_op jit(solution)/shard_map/inputs_grad/pallas_call | solution.py:109
  280.8 2.6 collective-permute-start.77
  284.7 3.1 collective-permute-start.79
  290.4 2.1 collective-permute-start.87
  294.2 4.4 %collective-permute-done.79.refs_0_ = bf16[2,64,1024]{2,1,0:T(8,128)(2,1)S(1)} collective-permute-done((bf16[2,64,1024]{2,1,0:T(8,128)(2,1)S(1)}, bf16[2,64,1024]{2,1,0:T(8,128)(2,1)S(1)}, u32[]{:S(2)}, u32[]{:S(2)}) %collective-permute-start.79) | collective-permute-done | bytes 262176 | tf_op jit(solution)/shard_map/ppermute | solution.py:26
  299.5 2.5 collective-permute-start.85
  302.6 6.1 %collective-permute-done.80.b_ref = bf16[1,64,1024]{2,1,0:T(8,128)(2,1)S(1)} collective-permute-done((bf16[1,64,1024]{2,1,0:T(8,128)(2,1)S(1)}, bf16[1,64,1024]{2,1,0:T(8,128)(2,1)S(1)}, u32[]{:S(2)}, u32[]{:S(2)}) %collective-permute-start.80) | collective-permute-done | bytes 131104 | tf_op jit(solution)/shard_map/ppermute | solution.py:26
  309.8 1.7 reshape.70
  311.5 1.7 reduce_sum.9
  313.1 1.4 reshape.71
  316.6 2.3 tokens_grad.1
  319.0 3.5 %collective-permute-start.88 = (f32[176,128]{1,0:T(8,128)S(1)}, f32[176,128]{1,0:T(8,128)S(1)}, u32[]{:S(2)}, u32[]{:S(2)}) collective-permute-start(f32[176,128]{1,0:T(8,128)S(1)} %pad_maximum_fusion.1), channel_id=1, source_target_pairs={{0,4},{1,5},{2,6},{3,7},{4,0},{5,1},{6,2},{7,3},{8,12},{9,13},{10,... | collective-permute-start | bytes 270344 | tf_op jit(solution)/shard_map/ppermute | solution.py:26
  323.5 1.9 collective-permute-start.82
  325.4 2.5 final_down.1
  328.2 3.7 %collective-permute-done.89 = f32[176,128]{1,0:T(8,128)S(1)} collective-permute-done((f32[176,128]{1,0:T(8,128)S(1)}, f32[176,128]{1,0:T(8,128)S(1)}, u32[]{:S(2)}, u32[]{:S(2)}) %collective-permute-start.89) | collective-permute-done | bytes 90144 | tf_op jit(solution)/shard_map/ppermute | solution.py:26
  331.9 2.7 final_up.1
  334.6 1.6 collective-permute-start.90
  336.2 1.6 collective-permute-done.90
  338.6 2.3 collective-permute-start.91
  341.3 3.3 collective-permute-start.93
  344.6 2.0 final_attn.1
  (380 shorter events, 119.5 us)
Async XLA Ops:
  10.6 19.6 %collective-permute-start.6 = (bf16[256,1024]{1,0:T(8,128)(2,1)S(1)}, bf16[256,1024]{1,0:T(8,128)(2,1)S(1)}, u32[]{:S(2)}, u32[]{:S(2)}) collective-permute-start(bf16[256,1024]{1,0:T(8,128)(2,1)S(1)} %bitcast.79), channel_id=1, source_target_pairs={{0,1},{1,0},{2,3},{3,2},{4,5},{5,4},{6,7},{7,6},{8,9},{9,8},{10,11... | collective-permute-start | bytes 1572872 | tf_op jit(solution)/shard_map/ppermute | solution.py:26
  14.7 15.3 %collective-permute-start.4 = (bf16[2,64,1024]{2,1,0:T(8,128)(2,1)S(1)}, bf16[2,64,1024]{2,1,0:T(8,128)(2,1)S(1)}, u32[]{:S(2)}, u32[]{:S(2)}) collective-permute-start(bf16[2,64,1024]{2,1,0:T(8,128)(2,1)S(1)} %append.12.a_ref), channel_id=1, source_target_pairs={{0,4},{1,5},{2,6},{3,7},{4,0},{5,1},{6,2},{7,3},{8,12},{9,13},{10,... | collective-permute-start | bytes 786440 | tf_op jit(solution)/shard_map/ppermute | solution.py:26
  14.9 20.0 %collective-permute-start.5 = (bf16[256,1024]{1,0:T(8,128)(2,1)S(1)}, bf16[256,1024]{1,0:T(8,128)(2,1)S(1)}, u32[]{:S(2)}, u32[]{:S(2)}) collective-permute-start(bf16[256,1024]{1,0:T(8,128)(2,1)S(1)} %bitcast.80), channel_id=1, source_target_pairs={{0,8},{8,0},{16,24},{24,16},{1,9},{9,1},{17,25},{25,17},{2,10},{10... | collective-permute-start | bytes 1572872 | tf_op jit(solution)/shard_map/ppermute | solution.py:26
  17.4 12.7 %collective-permute-start.8 = (bf16[1,64,1024]{2,1,0:T(8,128)(2,1)}, bf16[1,64,1024]{2,1,0:T(8,128)(2,1)S(1)}, u32[]{:S(2)}, u32[]{:S(2)}) collective-permute-start(bf16[1,64,1024]{2,1,0:T(8,128)(2,1)} %bitcast.115), channel_id=1, source_target_pairs={{0,1},{1,0},{2,3},{3,2},{4,5},{5,4},{6,7},{7,6},{8,9},{9,8},{10,11... | collective-permute-start | bytes 393224 | tf_op jit(solution)/shard_map/ppermute | solution.py:26
  30.1 12.4 %collective-permute-start.9 = (bf16[4,64,1024]{2,1,0:T(8,128)(2,1)S(1)}, bf16[4,64,1024]{2,1,0:T(8,128)(2,1)}, u32[]{:S(2)}, u32[]{:S(2)}) collective-permute-start(bf16[4,64,1024]{2,1,0:T(8,128)(2,1)S(1)} %append.13.refs_0_), channel_id=1, source_target_pairs={{0,2},{1,3},{2,0},{3,1},{4,6},{5,7},{6,4},{7,5},{8,10},{9,11},{10,... | collective-permute-start | bytes 1572872 | tf_op jit(solution)/shard_map/ppermute | solution.py:26
  33.6 15.4 %collective-permute-start.10 = (bf16[4,64,1024]{2,1,0:T(8,128)(2,1)S(1)}, bf16[4,64,1024]{2,1,0:T(8,128)(2,1)}, u32[]{:S(2)}, u32[]{:S(2)}) collective-permute-start(bf16[4,64,1024]{2,1,0:T(8,128)(2,1)S(1)} %append.13.refs_0_), channel_id=1, source_target_pairs={{0,16},{8,24},{16,0},{24,8},{1,17},{9,25},{17,1},{25,9},{2,18},{10... | collective-permute-start | bytes 1572872 | tf_op jit(solution)/shard_map/ppermute | solution.py:26
  42.5 18.6 %collective-permute-start.11 = (bf16[4,64,1024]{2,1,0:T(8,128)(2,1)}, bf16[4,64,1024]{2,1,0:T(8,128)(2,1)}, u32[]{:S(2)}, u32[]{:S(2)}) collective-permute-start(bf16[4,64,1024]{2,1,0:T(8,128)(2,1)} %collective-permute-done.9.refs_1_), channel_id=1, source_target_pairs={{0,16},{8,24},{16,0},{24,8},{1,17},{9,25},{17,1},{25,9},{2,18},{10... | collective-permute-start | bytes 1572872 | tf_op jit(solution)/shard_map/ppermute | solution.py:26
  44.0 15.0 %collective-permute-start.12 = (bf16[2,64,1024]{2,1,0:T(8,128)(2,1)}, bf16[2,64,1024]{2,1,0:T(8,128)(2,1)}, u32[]{:S(2)}, u32[]{:S(2)}) collective-permute-start(bf16[2,64,1024]{2,1,0:T(8,128)(2,1)} %append.14.a_ref), channel_id=1, source_target_pairs={{0,4},{1,5},{2,6},{3,7},{4,0},{5,1},{6,2},{7,3},{8,12},{9,13},{10,... | collective-permute-start | bytes 786440 | tf_op jit(solution)/shard_map/ppermute | solution.py:26
  54.3 13.5 %collective-permute-start.14 = (f32[16,256]{1,0:T(8,128)S(1)}, f32[16,256]{1,0:T(8,128)S(1)}, u32[]{:S(2)}, u32[]{:S(2)}) collective-permute-start(f32[16,256]{1,0:T(8,128)S(1)} %get-tuple-element.214), channel_id=1, source_target_pairs={{0,8},{8,0},{16,24},{24,16},{1,9},{9,1},{17,25},{25,17},{2,10},{10... | collective-permute-start | bytes 49160 | tf_op jit(solution)/shard_map/ppermute | solution.py:26
  56.5 11.3 %collective-permute-start.15 = (f32[16,256]{1,0:T(8,128)S(1)}, f32[16,256]{1,0:T(8,128)S(1)}, u32[]{:S(2)}, u32[]{:S(2)}) collective-permute-start(f32[16,256]{1,0:T(8,128)S(1)} %get-tuple-element.216), channel_id=1, source_target_pairs={{0,8},{8,0},{16,24},{24,16},{1,9},{9,1},{17,25},{25,17},{2,10},{10... | collective-permute-start | bytes 49160 | tf_op jit(solution)/shard_map/ppermute | solution.py:26
  56.6 11.2 %collective-permute-start.16 = (f32[16,256]{1,0:T(8,128)S(1)}, f32[16,256]{1,0:T(8,128)S(1)}, u32[]{:S(2)}, u32[]{:S(2)}) collective-permute-start(f32[16,256]{1,0:T(8,128)S(1)} %get-tuple-element.217), channel_id=1, source_target_pairs={{0,1},{1,0},{2,3},{3,2},{4,5},{5,4},{6,7},{7,6},{8,9},{9,8},{10,11... | collective-permute-start | bytes 49160 | tf_op jit(solution)/shard_map/ppermute | solution.py:26
  68.8 15.7 %collective-permute-start.22 = (bf16[1,64,1024]{2,1,0:T(8,128)(2,1)}, bf16[1,64,1024]{2,1,0:T(8,128)(2,1)}, u32[]{:S(2)}, u32[]{:S(2)}) collective-permute-start(bf16[1,64,1024]{2,1,0:T(8,128)(2,1)} %bitcast.114), channel_id=1, source_target_pairs={{0,1},{1,0},{2,3},{3,2},{4,5},{5,4},{6,7},{7,6},{8,9},{9,8},{10,11... | collective-permute-start | bytes 393224 | tf_op jit(solution)/shard_map/ppermute | solution.py:26
  72.4 14.3 %collective-permute-start.21 = (bf16[4,64,1024]{2,1,0:T(8,128)(2,1)S(1)}, bf16[4,64,1024]{2,1,0:T(8,128)(2,1)}, u32[]{:S(2)}, u32[]{:S(2)}) collective-permute-start(bf16[4,64,1024]{2,1,0:T(8,128)(2,1)S(1)} %append.15.refs_0_), channel_id=1, source_target_pairs={{0,2},{1,3},{2,0},{3,1},{4,6},{5,7},{6,4},{7,5},{8,10},{9,11},{10,... | collective-permute-start | bytes 1572872 | tf_op jit(solution)/shard_map/ppermute | solution.py:26
  76.7 9.9 %collective-permute-start.20 = (bf16[256,256]{1,0:T(8,128)(2,1)}, bf16[256,256]{1,0:T(8,128)(2,1)}, u32[]{:S(2)}, u32[]{:S(2)}) collective-permute-start(bf16[256,256]{1,0:T(8,128)(2,1)} %get-tuple-element.225), channel_id=1, source_target_pairs={{0,2},{1,3},{2,4},{3,5},{4,6},{5,7},{8,10},{9,11},{10,12},{11,13},... | collective-permute-start | bytes 393224 | tf_op jit(solution)/shard_map/ppermute | solution.py:1244
  80.7 18.7 %collective-permute-start.26 = (bf16[256,1024]{1,0:T(8,128)(2,1)S(1)}, bf16[256,1024]{1,0:T(8,128)(2,1)S(1)}, u32[]{:S(2)}, u32[]{:S(2)}) collective-permute-start(bf16[256,1024]{1,0:T(8,128)(2,1)S(1)} %bitcast.85), channel_id=1, source_target_pairs={{0,1},{1,0},{2,3},{3,2},{4,5},{5,4},{6,7},{7,6},{8,9},{9,8},{10,11... | collective-permute-start | bytes 1572872 | tf_op jit(solution)/shard_map/ppermute | solution.py:26
  81.4 16.5 %collective-permute-start.13 = (bf16[4,64,1024]{2,1,0:T(8,128)(2,1)S(1)}, bf16[4,64,1024]{2,1,0:T(8,128)(2,1)}, u32[]{:S(2)}, u32[]{:S(2)}) collective-permute-start(bf16[4,64,1024]{2,1,0:T(8,128)(2,1)S(1)} %append.15.refs_0_), channel_id=1, source_target_pairs={{0,16},{8,24},{16,0},{24,8},{1,17},{9,25},{17,1},{25,9},{2,18},{10... | collective-permute-start | bytes 1572872 | tf_op jit(solution)/shard_map/ppermute | solution.py:26
  88.0 12.0 %collective-permute-start.23 = (bf16[256,256]{1,0:T(8,128)(2,1)S(1)}, bf16[256,256]{1,0:T(8,128)(2,1)S(1)}, u32[]{:S(2)}, u32[]{:S(2)}) collective-permute-start(bf16[256,256]{1,0:T(8,128)(2,1)S(1)} %broadcast_select_fusion.c0), channel_id=1, source_target_pairs={{0,8},{8,0},{16,24},{24,16},{1,9},{9,1},{17,25},{25,17},{2,10},{10... | collective-permute-start | bytes 393224 | tf_op jit(solution)/shard_map/ppermute | solution.py:26
  97.9 17.5 %collective-permute-start.28 = (bf16[4,64,1024]{2,1,0:T(8,128)(2,1)}, bf16[4,64,1024]{2,1,0:T(8,128)(2,1)S(1)}, u32[]{:S(2)}, u32[]{:S(2)}) collective-permute-start(bf16[4,64,1024]{2,1,0:T(8,128)(2,1)} %collective-permute-done.21.refs_1_), channel_id=1, source_target_pairs={{0,16},{8,24},{16,0},{24,8},{1,17},{9,25},{17,1},{25,9},{2,18},{10... | collective-permute-start | bytes 1572872 | tf_op jit(solution)/shard_map/ppermute | solution.py:26
  99.1 16.4 %collective-permute-start.29 = (bf16[256,256]{1,0:T(8,128)(2,1)S(1)}, bf16[256,256]{1,0:T(8,128)(2,1)S(1)}, u32[]{:S(2)}, u32[]{:S(2)}) collective-permute-start(bf16[256,256]{1,0:T(8,128)(2,1)S(1)} %get-tuple-element.241), channel_id=1, source_target_pairs={{0,8},{8,0},{16,24},{24,16},{1,9},{9,1},{17,25},{25,17},{2,10},{10... | collective-permute-start | bytes 393224 | tf_op jit(solution)/shard_map/ppermute | solution.py:26
  99.4 16.0 %collective-permute-start.30 = (bf16[256,256]{1,0:T(8,128)(2,1)S(1)}, bf16[256,256]{1,0:T(8,128)(2,1)S(1)}, u32[]{:S(2)}, u32[]{:S(2)}) collective-permute-start(bf16[256,256]{1,0:T(8,128)(2,1)S(1)} %get-tuple-element.242), channel_id=1, source_target_pairs={{0,1},{1,0},{2,3},{3,2},{4,5},{5,4},{6,7},{7,6},{8,9},{9,8},{10,11... | collective-permute-start | bytes 393224 | tf_op jit(solution)/shard_map/ppermute | solution.py:26
  100.0 15.4 %collective-permute-start.31 = (bf16[256,256]{1,0:T(8,128)(2,1)S(1)}, bf16[256,256]{1,0:T(8,128)(2,1)S(1)}, u32[]{:S(2)}, u32[]{:S(2)}) collective-permute-start(bf16[256,256]{1,0:T(8,128)(2,1)S(1)} %get-tuple-element.243), channel_id=1, source_target_pairs={{0,9},{1,8},{2,11},{3,10},{4,13},{5,12},{6,15},{7,14},{8,1},{9,0},... | collective-permute-start | bytes 393224 | tf_op jit(solution)/shard_map/ppermute | solution.py:36
  101.3 14.1 %collective-permute-start.27 = (bf16[2,64,1024]{2,1,0:T(8,128)(2,1)S(1)}, bf16[2,64,1024]{2,1,0:T(8,128)(2,1)S(1)}, u32[]{:S(2)}, u32[]{:S(2)}) collective-permute-start(bf16[2,64,1024]{2,1,0:T(8,128)(2,1)S(1)} %append.16.a_ref), channel_id=1, source_target_pairs={{0,4},{1,5},{2,6},{3,7},{4,0},{5,1},{6,2},{7,3},{8,12},{9,13},{10,... | collective-permute-start | bytes 786440 | tf_op jit(solution)/shard_map/ppermute | solution.py:26
  117.3 13.5 %collective-permute-start.35 = (bf16[4,64,1024]{2,1,0:T(8,128)(2,1)S(1)}, bf16[4,64,1024]{2,1,0:T(8,128)(2,1)S(1)}, u32[]{:S(2)}, u32[]{:S(2)}) collective-permute-start(bf16[4,64,1024]{2,1,0:T(8,128)(2,1)S(1)} %append.17.refs_0_), channel_id=1, source_target_pairs={{0,2},{1,3},{2,0},{3,1},{4,6},{5,7},{6,4},{7,5},{8,10},{9,11},{10,... | collective-permute-start | bytes 1572872 | tf_op jit(solution)/shard_map/ppermute | solution.py:26
  117.4 13.5 %collective-permute-start.36 = (bf16[4,64,1024]{2,1,0:T(8,128)(2,1)S(1)}, bf16[4,64,1024]{2,1,0:T(8,128)(2,1)S(1)}, u32[]{:S(2)}, u32[]{:S(2)}) collective-permute-start(bf16[4,64,1024]{2,1,0:T(8,128)(2,1)S(1)} %append.17.refs_0_), channel_id=1, source_target_pairs={{0,16},{8,24},{16,0},{24,8},{1,17},{9,25},{17,1},{25,9},{2,18},{10... | collective-permute-start | bytes 1572872 | tf_op jit(solution)/shard_map/ppermute | solution.py:26
  118.7 12.2 %collective-permute-start.32 = (bf16[256,1024]{1,0:T(8,128)(2,1)S(1)}, bf16[256,1024]{1,0:T(8,128)(2,1)S(1)}, u32[]{:S(2)}, u32[]{:S(2)}) collective-permute-start(bf16[256,1024]{1,0:T(8,128)(2,1)S(1)} %get-tuple-element.245), channel_id=1, source_target_pairs={{0,8},{8,0},{16,24},{24,16},{1,9},{9,1},{17,25},{25,17},{2,10},{10... | collective-permute-start | bytes 1572872 | tf_op jit(solution)/shard_map/ppermute | solution.py:26
  119.2 13.4 %collective-permute-start.34 = (bf16[256,1024]{1,0:T(8,128)(2,1)S(1)}, bf16[256,1024]{1,0:T(8,128)(2,1)S(1)}, u32[]{:S(2)}, u32[]{:S(2)}) collective-permute-start(bf16[256,1024]{1,0:T(8,128)(2,1)S(1)} %far_sum.5), channel_id=1, source_target_pairs={{0,1},{1,0},{2,3},{3,2},{4,5},{5,4},{6,7},{7,6},{8,9},{9,8},{10,11... | collective-permute-start | bytes 1572872 | tf_op jit(solution)/shard_map/ppermute | solution.py:26
  133.0 12.5 %collective-permute-start.38 = (bf16[256,1024]{1,0:T(8,128)(2,1)S(1)}, bf16[256,1024]{1,0:T(8,128)(2,1)S(1)}, u32[]{:S(2)}, u32[]{:S(2)}) collective-permute-start(bf16[256,1024]{1,0:T(8,128)(2,1)S(1)} %get-tuple-element.253.m0.x0), channel_id=1, source_target_pairs={{0,1},{1,0},{2,3},{3,2},{4,5},{5,4},{6,7},{7,6},{8,9},{9,8},{10,11... | collective-permute-start | bytes 1572872 | tf_op jit(solution)/shard_map/ppermute | solution.py:26
  133.8 15.5 %collective-permute-start.42 = (bf16[4,64,1024]{2,1,0:T(8,128)(2,1)S(1)}, bf16[4,64,1024]{2,1,0:T(8,128)(2,1)S(1)}, u32[]{:S(2)}, u32[]{:S(2)}) collective-permute-start(bf16[4,64,1024]{2,1,0:T(8,128)(2,1)S(1)} %collective-permute-done.35.refs_1_), channel_id=1, source_target_pairs={{0,16},{8,24},{16,0},{24,8},{1,17},{9,25},{17,1},{25,9},{2,18},{10... | collective-permute-start | bytes 1572872 | tf_op jit(solution)/shard_map/ppermute | solution.py:26
  134.6 15.4 %collective-permute-start.37 = (bf16[256,1024]{1,0:T(8,128)(2,1)S(1)}, bf16[256,1024]{1,0:T(8,128)(2,1)S(1)}, u32[]{:S(2)}, u32[]{:S(2)}) collective-permute-start(bf16[256,1024]{1,0:T(8,128)(2,1)S(1)} %get-tuple-element.253.m0.x0), channel_id=1, source_target_pairs={{0,8},{8,0},{16,24},{24,16},{1,9},{9,1},{17,25},{25,17},{2,10},{10... | collective-permute-start | bytes 1572872 | tf_op jit(solution)/shard_map/ppermute | solution.py:26
  165.7 13.5 %collective-permute-start.46 = (bf16[4,64,1024]{2,1,0:T(8,128)(2,1)S(1)}, bf16[4,64,1024]{2,1,0:T(8,128)(2,1)S(1)}, u32[]{:S(2)}, u32[]{:S(2)}) collective-permute-start(bf16[4,64,1024]{2,1,0:T(8,128)(2,1)S(1)} %get-tuple-element.260), channel_id=1, source_target_pairs={{0,16},{8,24},{16,0},{24,8},{1,17},{9,25},{17,1},{25,9},{2,18},{10... | collective-permute-start | bytes 1572872 | tf_op jit(solution)/shard_map/ppermute | solution.py:26
  166.5 12.8 %collective-permute-start.49 = (bf16[256,1024]{1,0:T(8,128)(2,1)S(1)}, bf16[256,1024]{1,0:T(8,128)(2,1)S(1)}, u32[]{:S(2)}, u32[]{:S(2)}) collective-permute-start(bf16[256,1024]{1,0:T(8,128)(2,1)S(1)} %get-tuple-element.276), channel_id=1, source_target_pairs={{0,8},{8,0},{16,24},{24,16},{1,9},{9,1},{17,25},{25,17},{2,10},{10... | collective-permute-start | bytes 1572872 | tf_op jit(solution)/shard_map/ppermute | solution.py:26
  167.1 13.6 %collective-permute-start.50 = (bf16[256,1024]{1,0:T(8,128)(2,1)S(1)}, bf16[256,1024]{1,0:T(8,128)(2,1)S(1)}, u32[]{:S(2)}, u32[]{:S(2)}) collective-permute-start(bf16[256,1024]{1,0:T(8,128)(2,1)S(1)} %far_sum.6), channel_id=1, source_target_pairs={{0,1},{1,0},{2,3},{3,2},{4,5},{5,4},{6,7},{7,6},{8,9},{9,8},{10,11... | collective-permute-start | bytes 1572872 | tf_op jit(solution)/shard_map/ppermute | solution.py:26
  182.3 12.6 %collective-permute-start.52 = (bf16[256,1024]{1,0:T(8,128)(2,1)S(1)}, bf16[256,1024]{1,0:T(8,128)(2,1)S(1)}, u32[]{:S(2)}, u32[]{:S(2)}) collective-permute-start(bf16[256,1024]{1,0:T(8,128)(2,1)S(1)} %get-tuple-element.283.h0), channel_id=1, source_target_pairs={{0,1},{1,0},{2,3},{3,2},{4,5},{5,4},{6,7},{7,6},{8,9},{9,8},{10,11... | collective-permute-start | bytes 1572872 | tf_op jit(solution)/shard_map/ppermute | solution.py:26
  183.1 14.3 %collective-permute-start.48 = (bf16[4,64,1024]{2,1,0:T(8,128)(2,1)S(1)}, bf16[4,64,1024]{2,1,0:T(8,128)(2,1)S(1)}, u32[]{:S(2)}, u32[]{:S(2)}) collective-permute-start(bf16[4,64,1024]{2,1,0:T(8,128)(2,1)S(1)} %leave_sum.3), channel_id=1, source_target_pairs={{0,2},{1,3},{2,0},{3,1},{4,6},{5,7},{6,4},{7,5},{8,10},{9,11},{10,... | collective-permute-start | bytes 1572872 | tf_op jit(solution)/shard_map/ppermute | solution.py:26
  184.4 13.0 %collective-permute-start.45 = (bf16[4,64,1024]{2,1,0:T(8,128)(2,1)S(1)}, bf16[4,64,1024]{2,1,0:T(8,128)(2,1)S(1)}, u32[]{:S(2)}, u32[]{:S(2)}) collective-permute-start(bf16[4,64,1024]{2,1,0:T(8,128)(2,1)S(1)} %get-tuple-element.268), channel_id=1, source_target_pairs={{0,16},{8,24},{16,0},{24,8},{1,17},{9,25},{17,1},{25,9},{2,18},{10... | collective-permute-start | bytes 1572872 | tf_op jit(solution)/shard_map/ppermute | solution.py:26
  185.6 13.1 %collective-permute-start.51 = (bf16[256,1024]{1,0:T(8,128)(2,1)S(1)}, bf16[256,1024]{1,0:T(8,128)(2,1)S(1)}, u32[]{:S(2)}, u32[]{:S(2)}) collective-permute-start(bf16[256,1024]{1,0:T(8,128)(2,1)S(1)} %get-tuple-element.283.h0), channel_id=1, source_target_pairs={{0,8},{8,0},{16,24},{24,16},{1,9},{9,1},{17,25},{25,17},{2,10},{10... | collective-permute-start | bytes 1572872 | tf_op jit(solution)/shard_map/ppermute | solution.py:26
  196.7 14.2 %collective-permute-start.54 = (bf16[4,64,1024]{2,1,0:T(8,128)(2,1)S(1)}, bf16[4,64,1024]{2,1,0:T(8,128)(2,1)S(1)}, u32[]{:S(2)}, u32[]{:S(2)}) collective-permute-start(bf16[4,64,1024]{2,1,0:T(8,128)(2,1)S(1)} %get-tuple-element.262), channel_id=1, source_target_pairs={{0,16},{8,24},{16,0},{24,8},{1,17},{9,25},{17,1},{25,9},{2,18},{10... | collective-permute-start | bytes 1572872 | tf_op jit(solution)/shard_map/ppermute | solution.py:26
  197.6 14.4 %collective-permute-start.55 = (bf16[2,64,1024]{2,1,0:T(8,128)(2,1)S(1)}, bf16[2,64,1024]{2,1,0:T(8,128)(2,1)S(1)}, u32[]{:S(2)}, u32[]{:S(2)}) collective-permute-start(bf16[2,64,1024]{2,1,0:T(8,128)(2,1)S(1)} %get-tuple-element.281), channel_id=1, source_target_pairs={{0,4},{1,5},{2,6},{3,7},{4,0},{5,1},{6,2},{7,3},{8,12},{9,13},{10,... | collective-permute-start | bytes 786440 | tf_op jit(solution)/shard_map/ppermute | solution.py:26
  201.3 10.7 %collective-permute-start.56 = (bf16[256,256]{1,0:T(8,128)(2,1)S(1)}, bf16[256,256]{1,0:T(8,128)(2,1)S(1)}, u32[]{:S(2)}, u32[]{:S(2)}) collective-permute-start(bf16[256,256]{1,0:T(8,128)(2,1)S(1)} %get-tuple-element.286), channel_id=1, source_target_pairs={{0,8},{8,0},{16,24},{24,16},{1,9},{9,1},{17,25},{25,17},{2,10},{10... | collective-permute-start | bytes 393224 | tf_op jit(solution)/shard_map/ppermute | solution.py:26
  201.9 10.1 %collective-permute-start.57 = (bf16[256,256]{1,0:T(8,128)(2,1)S(1)}, bf16[256,256]{1,0:T(8,128)(2,1)S(1)}, u32[]{:S(2)}, u32[]{:S(2)}) collective-permute-start(bf16[256,256]{1,0:T(8,128)(2,1)S(1)} %get-tuple-element.287), channel_id=1, source_target_pairs={{0,1},{1,0},{2,3},{3,2},{4,5},{5,4},{6,7},{7,6},{8,9},{9,8},{10,11... | collective-permute-start | bytes 393224 | tf_op jit(solution)/shard_map/ppermute | solution.py:26
  202.8 9.2 %collective-permute-start.58 = (bf16[256,256]{1,0:T(8,128)(2,1)S(1)}, bf16[256,256]{1,0:T(8,128)(2,1)S(1)}, u32[]{:S(2)}, u32[]{:S(2)}) collective-permute-start(bf16[256,256]{1,0:T(8,128)(2,1)S(1)} %get-tuple-element.288), channel_id=1, source_target_pairs={{0,9},{1,8},{2,11},{3,10},{4,13},{5,12},{6,15},{7,14},{8,1},{9,0},... | collective-permute-start | bytes 393224 | tf_op jit(solution)/shard_map/ppermute | solution.py:36
  214.4 9.9 %collective-permute-start.59 = (bf16[256,256]{1,0:T(8,128)(2,1)S(1)}, bf16[256,256]{1,0:T(8,128)(2,1)S(1)}, u32[]{:S(2)}, u32[]{:S(2)}) collective-permute-start(bf16[256,256]{1,0:T(8,128)(2,1)S(1)} %get-tuple-element.297), channel_id=1, source_target_pairs={{0,8},{8,0},{16,24},{24,16},{1,9},{9,1},{17,25},{25,17},{2,10},{10... | collective-permute-start | bytes 393224 | tf_op jit(solution)/shard_map/ppermute | solution.py:26
  215.4 8.9 %collective-permute-start.61 = (bf16[256,256]{1,0:T(8,128)(2,1)S(1)}, bf16[256,256]{1,0:T(8,128)(2,1)S(1)}, u32[]{:S(2)}, u32[]{:S(2)}) collective-permute-start(bf16[256,256]{1,0:T(8,128)(2,1)S(1)} %far_sum.7), channel_id=1, source_target_pairs={{0,1},{1,0},{2,3},{3,2},{4,5},{5,4},{6,7},{7,6},{8,9},{9,8},{10,11... | collective-permute-start | bytes 393224 | tf_op jit(solution)/shard_map/ppermute | solution.py:26
  223.5 24.9 %collective-permute-start.69 = (bf16[4,64,1024]{2,1,0:T(8,128)(2,1)}, bf16[4,64,1024]{2,1,0:T(8,128)(2,1)}, u32[]{:S(2)}, u32[]{:S(2)}) collective-permute-start(bf16[4,64,1024]{2,1,0:T(8,128)(2,1)} %get-tuple-element.311), channel_id=1, source_target_pairs={{0,16},{8,24},{16,0},{24,8},{1,17},{9,25},{17,1},{25,9},{2,18},{10... | collective-permute-start | bytes 1572872 | tf_op jit(solution)/shard_map/ppermute | solution.py:26
  228.5 22.9 %collective-permute-start.44 = (bf16[256,1024]{1,0:T(8,128)(2,1)}, bf16[256,1024]{1,0:T(8,128)(2,1)}, u32[]{:S(2)}, u32[]{:S(2)}) collective-permute-start(bf16[256,1024]{1,0:T(8,128)(2,1)} %get-tuple-element.267), channel_id=1, source_target_pairs={{0,8},{8,0},{16,24},{24,16},{1,9},{9,1},{17,25},{25,17},{2,10},{10... | collective-permute-start | bytes 1572872 | tf_op jit(solution)/shard_map/ppermute | solution.py:26
  232.2 9.8 %collective-permute-start.68 = (bf16[1,64,1024]{2,1,0:T(8,128)(2,1)S(1)}, bf16[1,64,1024]{2,1,0:T(8,128)(2,1)S(1)}, u32[]{:S(2)}, u32[]{:S(2)}) collective-permute-start(bf16[1,64,1024]{2,1,0:T(8,128)(2,1)S(1)} %get-tuple-element.294), channel_id=1, source_target_pairs={{0,1},{1,0},{2,3},{3,2},{4,5},{5,4},{6,7},{7,6},{8,9},{9,8},{10,11... | collective-permute-start | bytes 393224 | tf_op jit(solution)/shard_map/ppermute | solution.py:26
  237.6 10.8 %collective-permute-start.67 = (f32[16,4,128]{2,1,0:T(4,128)S(1)}, f32[16,4,128]{2,1,0:T(4,128)S(1)}, u32[]{:S(2)}, u32[]{:S(2)}) collective-permute-start(f32[16,4,128]{2,1,0:T(4,128)S(1)} %get-tuple-element.371), channel_id=1, source_target_pairs={{2,0},{3,1},{4,2},{5,3},{6,4},{7,5},{10,8},{11,9},{12,10},{13,11},... | collective-permute-start | bytes 98312 | tf_op jit(solution)/shard_map/ppermute | solution.py:1225
  238.9 16.9 %collective-permute-start.72 = (bf16[4,64,1024]{2,1,0:T(8,128)(2,1)}, bf16[4,64,1024]{2,1,0:T(8,128)(2,1)}, u32[]{:S(2)}, u32[]{:S(2)}) collective-permute-start(bf16[4,64,1024]{2,1,0:T(8,128)(2,1)} %leave_sum.4), channel_id=1, source_target_pairs={{0,2},{1,3},{2,0},{3,1},{4,6},{5,7},{6,4},{7,5},{8,10},{9,11},{10,... | collective-permute-start | bytes 1572872 | tf_op jit(solution)/shard_map/ppermute | solution.py:26
  242.6 13.3 %collective-permute-start.71 = (bf16[4,64,1024]{2,1,0:T(8,128)(2,1)}, bf16[4,64,1024]{2,1,0:T(8,128)(2,1)}, u32[]{:S(2)}, u32[]{:S(2)}) collective-permute-start(bf16[4,64,1024]{2,1,0:T(8,128)(2,1)} %get-tuple-element.321), channel_id=1, source_target_pairs={{0,16},{8,24},{16,0},{24,8},{1,17},{9,25},{17,1},{25,9},{2,18},{10... | collective-permute-start | bytes 1572872 | tf_op jit(solution)/shard_map/ppermute | solution.py:26
  250.6 22.9 %collective-permute-start.43 = (bf16[256,1024]{1,0:T(8,128)(2,1)}, bf16[256,1024]{1,0:T(8,128)(2,1)S(1)}, u32[]{:S(2)}, u32[]{:S(2)}) collective-permute-start(bf16[256,1024]{1,0:T(8,128)(2,1)} %copy-done.64), channel_id=1, source_target_pairs={{0,8},{8,0},{16,24},{24,16},{1,9},{9,1},{17,25},{25,17},{2,10},{10... | collective-permute-start | bytes 1572872 | tf_op jit(solution)/shard_map/ppermute | solution.py:26
  253.8 19.7 %collective-permute-start.62 = (bf16[256,1024]{1,0:T(8,128)(2,1)S(1)}, bf16[256,1024]{1,0:T(8,128)(2,1)S(1)}, u32[]{:S(2)}, u32[]{:S(2)}) collective-permute-start(bf16[256,1024]{1,0:T(8,128)(2,1)S(1)} %far_sum.8), channel_id=1, source_target_pairs={{0,1},{1,0},{2,3},{3,2},{4,5},{5,4},{6,7},{7,6},{8,9},{9,8},{10,11... | collective-permute-start | bytes 1572872 | tf_op jit(solution)/shard_map/ppermute | solution.py:26
  258.7 21.9 %collective-permute-start.75 = (bf16[4,64,1024]{2,1,0:T(8,128)(2,1)S(1)}, bf16[4,64,1024]{2,1,0:T(8,128)(2,1)S(1)}, u32[]{:S(2)}, u32[]{:S(2)}) collective-permute-start(bf16[4,64,1024]{2,1,0:T(8,128)(2,1)S(1)} %leave_sum.5), channel_id=1, source_target_pairs={{0,2},{1,3},{2,0},{3,1},{4,6},{5,7},{6,4},{7,5},{8,10},{9,11},{10,... | collective-permute-start | bytes 1572872 | tf_op jit(solution)/shard_map/ppermute | solution.py:26
  260.7 19.9 %collective-permute-start.74 = (bf16[4,64,1024]{2,1,0:T(8,128)(2,1)S(1)}, bf16[4,64,1024]{2,1,0:T(8,128)(2,1)S(1)}, u32[]{:S(2)}, u32[]{:S(2)}) collective-permute-start(bf16[4,64,1024]{2,1,0:T(8,128)(2,1)S(1)} %copy-done.66), channel_id=1, source_target_pairs={{0,16},{8,24},{16,0},{24,8},{1,17},{9,25},{17,1},{25,9},{2,18},{10... | collective-permute-start | bytes 1572872 | tf_op jit(solution)/shard_map/ppermute | solution.py:26
  261.2 14.7 %collective-permute-start.73 = (bf16[2,64,1024]{2,1,0:T(8,128)(2,1)S(1)}, bf16[2,64,1024]{2,1,0:T(8,128)(2,1)S(1)}, u32[]{:S(2)}, u32[]{:S(2)}) collective-permute-start(bf16[2,64,1024]{2,1,0:T(8,128)(2,1)S(1)} %get-tuple-element.323), channel_id=1, source_target_pairs={{0,4},{1,5},{2,6},{3,7},{4,0},{5,1},{6,2},{7,3},{8,12},{9,13},{10,... | collective-permute-start | bytes 786440 | tf_op jit(solution)/shard_map/ppermute | solution.py:26
  284.7 13.8 %collective-permute-start.79 = (bf16[2,64,1024]{2,1,0:T(8,128)(2,1)S(1)}, bf16[2,64,1024]{2,1,0:T(8,128)(2,1)S(1)}, u32[]{:S(2)}, u32[]{:S(2)}) collective-permute-start(bf16[2,64,1024]{2,1,0:T(8,128)(2,1)S(1)} %get-tuple-element.340), channel_id=1, source_target_pairs={{0,4},{1,5},{2,6},{3,7},{4,0},{5,1},{6,2},{7,3},{8,12},{9,13},{10,... | collective-permute-start | bytes 786440 | tf_op jit(solution)/shard_map/ppermute | solution.py:26
  288.8 10.7 %collective-permute-start.84 = (bf16[2,64,1024]{2,1,0:T(8,128)(2,1)S(1)}, bf16[2,64,1024]{2,1,0:T(8,128)(2,1)S(1)}, u32[]{:S(2)}, u32[]{:S(2)}) collective-permute-start(bf16[2,64,1024]{2,1,0:T(8,128)(2,1)S(1)} %append.20.a_ref), channel_id=1, source_target_pairs={{0,16},{8,24},{16,0},{24,8},{1,17},{9,25},{17,1},{25,9},{2,18},{10... | collective-permute-start | bytes 786440 | tf_op jit(solution)/shard_map/ppermute | solution.py:26
  290.4 35.0 %collective-permute-start.87 = (bf16[4,64,1024]{2,1,0:T(8,128)(2,1)S(1)}, bf16[4,64,1024]{2,1,0:T(8,128)(2,1)}, u32[]{:S(2)}, u32[]{:S(2)}) collective-permute-start(bf16[4,64,1024]{2,1,0:T(8,128)(2,1)S(1)} %append.23.mine_ref), channel_id=1, source_target_pairs={{0,8},{8,0},{16,24},{24,16},{1,9},{9,1},{17,25},{25,17},{2,10},{10... | collective-permute-start | bytes 1572872 | tf_op jit(solution)/shard_map/ppermute | solution.py:26
  292.5 22.9 %collective-permute-start.76 = (bf16[256,1024]{1,0:T(8,128)(2,1)}, bf16[256,1024]{1,0:T(8,128)(2,1)S(1)}, u32[]{:S(2)}, u32[]{:S(2)}) collective-permute-start(bf16[256,1024]{1,0:T(8,128)(2,1)} %get-tuple-element.342), channel_id=1, source_target_pairs={{0,8},{8,0},{16,24},{24,16},{1,9},{9,1},{17,25},{25,17},{2,10},{10... | collective-permute-start | bytes 1572872 | tf_op jit(solution)/shard_map/ppermute | solution.py:26
  292.6 22.8 %collective-permute-start.78 = (bf16[256,1024]{1,0:T(8,128)(2,1)}, bf16[256,1024]{1,0:T(8,128)(2,1)}, u32[]{:S(2)}, u32[]{:S(2)}) collective-permute-start(bf16[256,1024]{1,0:T(8,128)(2,1)} %far_sum.9), channel_id=1, source_target_pairs={{0,1},{1,0},{2,3},{3,2},{4,5},{5,4},{6,7},{7,6},{8,9},{9,8},{10,11... | collective-permute-start | bytes 1572872 | tf_op jit(solution)/shard_map/ppermute | solution.py:26
  298.6 10.0 %collective-permute-start.80 = (bf16[1,64,1024]{2,1,0:T(8,128)(2,1)S(1)}, bf16[1,64,1024]{2,1,0:T(8,128)(2,1)S(1)}, u32[]{:S(2)}, u32[]{:S(2)}) collective-permute-start(bf16[1,64,1024]{2,1,0:T(8,128)(2,1)S(1)} %get-tuple-element.347), channel_id=1, source_target_pairs={{0,1},{1,0},{2,3},{3,2},{4,5},{5,4},{6,7},{7,6},{8,9},{9,8},{10,11... | collective-permute-start | bytes 393224 | tf_op jit(solution)/shard_map/ppermute | solution.py:26
  299.5 32.4 %collective-permute-start.85 = (bf16[4,64,1024]{2,1,0:T(8,128)(2,1)S(1)}, bf16[4,64,1024]{2,1,0:T(8,128)(2,1)}, u32[]{:S(2)}, u32[]{:S(2)}) collective-permute-start(bf16[4,64,1024]{2,1,0:T(8,128)(2,1)S(1)} %append.21.mine_ref), channel_id=1, source_target_pairs={{0,8},{8,0},{16,24},{24,16},{1,9},{9,1},{17,25},{25,17},{2,10},{10... | collective-permute-start | bytes 1572872 | tf_op jit(solution)/shard_map/ppermute | solution.py:26
  308.7 13.8 %collective-permute-start.81 = (bf16[2,64,1024]{2,1,0:T(8,128)(2,1)S(1)}, bf16[2,64,1024]{2,1,0:T(8,128)(2,1)}, u32[]{:S(2)}, u32[]{:S(2)}) collective-permute-start(bf16[2,64,1024]{2,1,0:T(8,128)(2,1)S(1)} %append.18.a_ref), channel_id=1, source_target_pairs={{0,16},{8,24},{16,0},{24,8},{1,17},{9,25},{17,1},{25,9},{2,18},{10... | collective-permute-start | bytes 786440 | tf_op jit(solution)/shard_map/ppermute | solution.py:26
  319.0 8.9 %collective-permute-start.88 = (f32[176,128]{1,0:T(8,128)S(1)}, f32[176,128]{1,0:T(8,128)S(1)}, u32[]{:S(2)}, u32[]{:S(2)}) collective-permute-start(f32[176,128]{1,0:T(8,128)S(1)} %pad_maximum_fusion.1), channel_id=1, source_target_pairs={{0,4},{1,5},{2,6},{3,7},{4,0},{5,1},{6,2},{7,3},{8,12},{9,13},{10,... | collective-permute-start | bytes 270344 | tf_op jit(solution)/shard_map/ppermute | solution.py:26
  323.5 21.1 %collective-permute-start.82 = (bf16[4,64,1024]{2,1,0:T(8,128)(2,1)S(1)}, bf16[4,64,1024]{2,1,0:T(8,128)(2,1)S(1)}, u32[]{:S(2)}, u32[]{:S(2)}) collective-permute-start(bf16[4,64,1024]{2,1,0:T(8,128)(2,1)S(1)} %append.19.mine_ref), channel_id=1, source_target_pairs={{0,8},{8,0},{16,24},{24,16},{1,9},{9,1},{17,25},{25,17},{2,10},{10... | collective-permute-start | bytes 1572872 | tf_op jit(solution)/shard_map/ppermute | solution.py:26
  (99 other events, 1164.3 us)

commit v3 on v2

--- a/solution.py
+++ b/solution.py
@@ -434,28 +434,31 @@
                     to[pl.ds(row, rows), pl.ds(col, quarter)] = block.astype(f32)
 
 
-def spread(own, near):
-    blocks = {0: append(own, near)}
+def spread_places(pair):
+    blocks = {0: append(*pair)}
     for bit in high_bits("dp"):
         for m in list(blocks):
             blocks[m | (bit // 2)] = swap(blocks[m], "dp", bit)
-    blocks = [blocks[m] for m in range(len(blocks))]
+    return [blocks[m] for m in range(len(blocks))]
+
+
+def spread_cores(blocks):
     while len(blocks) > 1:
         blocks = [append(a, b) for a, b in zip(blocks[0::2], blocks[1::2])]
     return blocks[0], swap(blocks[0], "dp", 1)
 
 
-def spread_weight(kind, pair, idx, shapes, fb=LANES):
+def spread_weight(kind, blocks, idx, shapes, fb=LANES):
     return call(
         functools.partial(final_kernel, kind, fb),
         "final_" + kind,
         [jax.ShapeDtypeStruct(s, f32) for s in shapes],
-        (idx, *spread(*pair)),
-    )
-
-
-def spread_narrow(pair, idx, shape, fb):
-    mine, other = spread(*pair)
+        (idx, *spread_cores(blocks)),
+    )
+
+
+def spread_narrow(blocks, idx, shape, fb):
+    mine, other = spread_cores(blocks)
     teams = [mine[0::2], other[0::2], mine[1::2], other[1::2]]
     teams = jnp.stack(ordered(teams, idx[0]))
     rows = jnp.stack(ordered([teams[:, m] for m in range(teams.shape[1])], idx[1]), axis=1)
@@ -548,9 +551,13 @@
 
 
 def first_context_kernel(dy0_ref, a_ref, gout_ref, init_ref, da_ref, dgout_ref, g0_ref, hs):
-    ns = range(GROUP)
-    a = [a_ref[n] for n in ns]
-    gout = [gout_ref[n] for n in ns]
+    half = a_ref.shape[1] // 2
+    ns = range(a_ref.shape[0] // 2)
+
+    def paired(ref):
+        return [jnp.concatenate([ref[2 * n, :half], ref[2 * n + 1, :half]], axis=0) for n in ns]
+
+    a, gout, init = paired(a_ref), paired(gout_ref), paired(init_ref)
     zero = tuple(jnp.zeros_like(a[0]) for _ in ns)
 
     def ahead(k, h):
@@ -560,7 +567,7 @@
                 hs[k * 8 + t + 1, n] = h[n]
         return h
 
-    h = tuple(init_ref[n] for n in ns)
+    h = tuple(init)
     for n in ns:
         hs[0, n] = h[n]
     lax.fori_loop(0, CTX // 8, ahead, h)
@@ -576,19 +583,20 @@
             mu = tuple(a[n] * mu[n] for n in ns)
         return mu, da, dgout
 
-    mu, da, dgout = lax.fori_loop(0, CTX // 4, back, (zero, zero, zero))
-    for n in ns:
-        g0_ref[n] = mu[n]
-        da_ref[n] = da[n]
-        dgout_ref[n] = dgout[n]
+    results = lax.fori_loop(0, CTX // 4, back, (zero, zero, zero))
+    rest = jnp.zeros_like(a[0][:half])
+    for ref, values in zip((g0_ref, da_ref, dgout_ref), results):
+        for n in ns:
+            ref[2 * n] = jnp.concatenate([values[n][:half], rest], axis=0)
+            ref[2 * n + 1] = jnp.concatenate([values[n][half:], rest], axis=0)
 
 
 def first_context_back(dy0, a, gout, h_init):
     tile = dy0.shape[1:]
-    states = pl.BlockSpec((GROUP,) + tile, lambda g: (g, 0, 0))
+    states = pl.BlockSpec((2 * GROUP,) + tile, lambda g: (g, 0, 0))
     return pl.pallas_call(
         first_context_kernel,
-        grid=(NST // GROUP,),
+        grid=(NST // (2 * GROUP),),
         out_shape=(jax.ShapeDtypeStruct(a.shape, f32),) * 3,
         in_specs=[pl.BlockSpec(dy0.shape, lambda g: (0, 0, 0))] + [states] * 3,
         out_specs=(states,) * 3,
@@ -1041,6 +1049,27 @@
         out[:, pl.ds(at, cols)] = part[...]
 
 
+def small_pack_kernel(flags, a, d_a, d_in, d_out, g_in, g_init, one, two, out):
+    per = d_a.shape[1] // TEAM
+    row = 0
+    for k, ref in enumerate((d_a, d_in, d_out)):
+        for c in range(per):
+            total = 0.0
+            for r in range(TEAM):
+                part = ref[:, r * per + c, :]
+                total = total + (-a[:, r * per + c, :] * part if k == 0 else part)
+            out[row : row + NST, :] = total
+            row += NST
+    for ref in (one, two):
+        for c in range(ref.shape[1] // LANES):
+            out[row : row + 1, :] = ref[:, c * LANES : (c + 1) * LANES]
+            row += 1
+    for s in range(2 * per):
+        first = jnp.where(flags[0] == 1, g_in[:, 2 * per + s, :], g_in[:, s, :])
+        out[row : row + NST, :] = g_init[:, s, :] + jnp.where(flags[1] == 0, first, 0.0)
+        row += NST
+
+
 def small_kernel(spots, p0, p1, p2, p3, gains_ref, rate_ref, in_ref, out_ref, init_ref):
     packs = [p[...] for p in (p0, p1, p2, p3)]
     tiles = packs[0].shape[0] - 3 * NST * 2 - NST * 4
@@ -1054,12 +1083,13 @@
     for r in (1, 2, 3):
         chosen = jnp.where(spots[0] == r, packs[r], chosen)
     side = spots[1] % 2 == 1
-    params = chosen[:one].reshape(3 * NST, 2, LANES)
-    params = jnp.where(side, params[:, 1], params[:, 0])
+
+    def of_side(at):
+        return jnp.where(side, chosen[at + NST : at + 2 * NST], chosen[at : at + NST])
+
     for k, ref in enumerate((rate_ref, in_ref, out_ref)):
-        ref[...] = params[k * NST : (k + 1) * NST]
-    init = chosen[two:].reshape(NST, 4, LANES)
-    window = [jnp.where(side, init[:, 2 * w + 1], init[:, 2 * w]) for w in (0, 1)]
+        ref[...] = of_side(2 * NST * k)
+    window = [of_side(two + 2 * NST * w) for w in (0, 1)]
     init_ref[...] = jnp.where(spots[0] % 2 == 1, window[1], window[0])
 
 
@@ -1103,7 +1133,18 @@
     out[...] = added(p0, one, far).astype(bf16)
 
 
-def context_rows_kernel(flags, came, own, dy_ref, dy_full, dy0_full):
+def first_rows_kernel(flags, own, dy0_full):
+    per = dy0_full.shape[1] // TEAM
+    zero = jnp.zeros((CTX, LANES), f32)
+    for w in range(2):
+        for c in range(per):
+            at = (slice(w * CTX, (w + 1) * CTX), slice(c * LANES, (c + 1) * LANES))
+            dy0 = jnp.where(flags[1] == 0, own[at].astype(f32), zero)
+            dy0_full[:, w * per + c, :] = dy0
+            dy0_full[:, (2 + w) * per + c, :] = dy0
+
+
+def context_rows_kernel(flags, came, dy_ref, dy_full):
     per = dy_ref.shape[1] // 2
     zero = jnp.zeros((CTX, LANES), f32)
     for w in range(2):
@@ -1113,8 +1154,6 @@
             dy_ref[:, w * per + c, :] = dy
             dy_full[:, w * per + c, :] = jnp.where(flags[0] == 1, dy, zero)
             dy_full[:, (2 + w) * per + c, :] = jnp.where(flags[0] == 1, zero, dy)
-            dy0_full[:, w * per + c, :] = jnp.where(flags[1] == 0, own[at].astype(f32), zero)
-            dy0_full[:, (2 + w) * per + c, :] = zero
 
 
 def on_device(
@@ -1198,7 +1237,6 @@
         (half, init, swap_team(near_init, 1), *trade_team(end_cot)),
     )
     end_cot = [end_first, end_second]
-    g_blocks = gather_team(after(cotangent[0], attn_first))
 
     def by_half(a, axis=1):
         n = a.shape[axis] // 2
@@ -1252,7 +1290,9 @@
 
     full_qkv = after(full_qkv, up_third)
     qkv = dot_nn(inputs_low, full_qkv).astype(bf16)
-    context = after(gather_team(context), qkv)
+    context = gather_team(context)
+    g_blocks = gather_team(after(cotangent[0], context[2]))
+    context = after(context, qkv)
     ctx_kv, context = call(
         context_kv_kernel,
         "context_kv",
@@ -1262,7 +1302,8 @@
     attended = attend(half, qkv, ctx_kv)
 
     up_last = up.across(1, up_third)
-    attended = after(attended, (g_blocks[2], down_first, up_last))
+    down.came = after(down.came, ctx_kv)
+    attended = after(attended, (g_blocks[2], down.came, up_last))
     down_second = down.step()
     down_third = down.across(0, up_last)
     attended_parts = call(out_kernel, "out_dot", part_types(rows, dim), (idx, attended, *full_out))
@@ -1325,23 +1366,25 @@
     )
     d_attn = attn_grad(idx, inputs_low, after(d_qkv, d_context), context, d_ctx_kv, d_out)
     sum_attn = reduction(d_attn, place)
-    sum_attn.step()
     d_context = sum_team(d_context, None, d_attn)
     d_context = call(context_sum_kernel, "context_sum", like((2 * CTX, cols), bf16), d_context[:3], 0)
     came = lax.ppermute(d_context, "seq", [(k + 2, k) for k in range(ns - 2)])
+    sum_attn.step(d_context)
     flags = jnp.stack([seq % 2, block]).astype(jnp.int32)
-    dy, dy_full, dy0_full = call(
+    dy0_full = call(first_rows_kernel, "first_rows", like((CTX,) + tile, f32), (flags, d_context))
+    dy, dy_full = call(
         context_rows_kernel,
         "context_rows",
-        (like((CTX,) + half_tile, f32), like((CTX,) + tile, f32), like((CTX,) + tile, f32)),
-        (flags, after(came, (ends, sum_attn.sent)), d_context),
+        (like((CTX,) + half_tile, f32), like((CTX,) + tile, f32)),
+        (flags, after(came, (ends, dy0_full, sum_attn.sent))),
     )
 
     lam_mid = tail_adjoint(dy, a, gout)
     g_second = jnp.exp(-half_rate * (rows - CTX + 1)) * lam_mid + decay * end_cot[1]
+    d_down_pair = sum_down.last()
     d_a, d_gout, g_init = first_context_back(after(dy0_full, lam_mid), a, gout, init_twice)
-    d_down_pair = sum_down.last()
     leaving = chain(decay * (end_cot[0] + g_second), True, (g_init, d_down_pair[1], sum_attn.out if reduction is HalvedReduction else g_init))
+    down_blocks = spread_places(d_down_pair)
     sum_up.step(leaving)
     sum_attn.step(sum_up.sent)
     result = sum_team(result, d_context)
@@ -1350,27 +1393,27 @@
     du, d_gin, d_a, d_gout, g_in = ssm_back(
         u, dy_full, a, gin, gout, state_in, after(lam_end, sum_attn.sent), d_a, d_gout
     )
-    g_first = by_half(g_in)[0]
-    d_init = g_init[:, : tile[0] // 2] + jnp.where(block == 0, g_first, jnp.zeros_like(g_first))
-    d_rate = -a * d_a
 
     sum_up.step(du)
     *d_inputs, d_gain_one = call(
         inputs_grad_kernel,
         "inputs_grad",
         part_types(rows, dim) + (jax.ShapeDtypeStruct((1, dim), f32),),
-        (idx, d_qkv, full_qkv, after(du, (result, sum_up.sent)), inv_one, *x_blocks),
+        (idx, d_qkv, full_qkv, after(du, (result, sum_up.sent, down_blocks)), inv_one, *x_blocks),
         scratch_shapes=[pltpu.VMEM((rows, dim), f32)],
     )
     sum_attn.step(d_gain_one)
     d_inputs = after(d_inputs, sum_attn.sent)
-    *d_inputs, d_inputs_far = sum_team(d_inputs)
-    d_up_pair = after(sum_up.last(), d_inputs_far)
-    d_down = spread_weight("down", d_down_pair, idx, [w_down.shape])[0]
-    if fb % LANES:
-        d_up = spread_narrow(d_up_pair, idx, w_up.shape, fb)
-    else:
-        d_up = spread_weight("up", d_up_pair, idx, [w_up.shape], fb)[0]
+    small_rows = (3 * NST * cols + 2 * dim + 2 * NST * cols) // LANES
+    pack = call(
+        small_pack_kernel,
+        "small_pack",
+        like((small_rows, LANES), f32),
+        (flags, a, d_a, d_gin, d_gout, g_in, g_init, d_gain_one, d_gain_two),
+    )
+    small, first, *others = pack, *high_bits("seq")
+    pack = pack + swap(pack, "seq", first)
+    *d_inputs, d_inputs_far = sum_team(d_inputs, small)
     d_tokens = call(
         tokens_grad_kernel,
         "tokens_grad",
@@ -1379,23 +1422,20 @@
         0,
     )
 
-    d_params = after(jnp.stack([d_rate, d_gin, d_gout]), d_gain_one)
-    d_params = d_params.reshape(3 * NST, TEAM, cols).sum(1)
-    d_gains = jnp.concatenate([d_gain_one[0], d_gain_two[0]])
-    pack = [d_params.reshape(-1, LANES), d_gains.reshape(-1, LANES), d_init.reshape(-1, LANES)]
-    pack = after(jnp.concatenate(pack, axis=0), d_inputs_far)
-    for n, bit in enumerate(high_bits("seq")):
-        if n == 0:
-            pack = after(pack, (sum_attn.step(), d_tokens))
-        if n == 1:
-            pack = after(pack, d_down)
+    up_blocks = spread_places(after(sum_up.last(), d_tokens))
+    d_down = spread_weight("down", down_blocks, idx, [w_down.shape])[0]
+    if fb % LANES:
+        d_up = spread_narrow(up_blocks, idx, w_up.shape, fb)
+    else:
+        d_up = spread_weight("up", up_blocks, idx, [w_up.shape], fb)[0]
+    sum_attn.step((pack, d_tokens))
+    for bit in others:
         pack = pack + swap(pack, "seq", bit)
     one, two = 3 * NST * cols // LANES, 3 * NST * cols // LANES + 2 * dim // LANES
     shared = pack[:two]
-    shared = after(shared, d_up)
     for bit in high_bits("dp"):
         shared = shared + swap(shared, "dp", bit)
-    packs = gather_team(jnp.concatenate([shared, pack[two:]], axis=0))
+    packs = gather_team(after(jnp.concatenate([shared, pack[two:]], axis=0), (d_down, d_up)))
     if shard == LANES:
         spots = jnp.stack([me ^ (seq * shard // cols), seq]).astype(jnp.int32)
         gains, *d_params, state_grad = call(
@@ -1412,14 +1452,16 @@
         member = me ^ (seq * shard // cols)
         inner = seq * shard % cols
         chosen = pick(packs, member)
-        d_params = chosen[:one].reshape(3 * NST, cols)
+        d_params = chosen[:one].reshape(3, cols // LANES, NST, LANES).transpose(0, 2, 1, 3)
+        d_params = d_params.reshape(3 * NST, cols)
         d_params = lax.dynamic_slice_in_dim(d_params, inner, shard, 1).reshape(3, NST, shard)
         d_params = d_params.transpose(0, 2, 1)
-        state_grad = chosen[two:].reshape(NST, 2, cols)
+        state_grad = chosen[two:].reshape(2, cols // LANES, NST, LANES).transpose(2, 0, 1, 3)
+        state_grad = state_grad.reshape(NST, 2, cols)
         state_grad = pick(state_grad, member % 2, 1)
         state_grad = lax.dynamic_slice_in_dim(state_grad, inner, shard, 1).T[None]
 
-    d_wqkv, d_out = spread_weight("attn", sum_attn.last(), idx, [w_qkv.shape, w_out.shape])
+    d_wqkv, d_out = spread_weight("attn", spread_places(after(sum_attn.last(), pack)), idx, [w_qkv.shape, w_out.shape])
     return (
         result[None],
         d_tokens[None],

time: 350 us -> 332 us (0.949)
  waiting for transfers between devices: 85.8 us -> 97.3 us
  other arithmetic: 15.2 us -> 5.33 us
  starting transfers between devices: 114 us -> 107 us
  local copies, waits for them, and re-layouts: 23 us -> 16.3 us
  Pallas kernels: 106 us -> 101 us
    ppermute x84, starting transfers between devices: 92.3 us -> 85 us  [swap(): lax.ppermute(a, axis, [(k, k ^ bit) for k in range(lax.axis_size(axis))])]
    ppermute x84, waiting for transfers between devices: 82 us -> 86.8 us  [swap(): lax.ppermute(a, axis, [(k, k ^ bit) for k in range(lax.axis_size(axis))])]
    ppermute x4, waiting for transfers between devices: 0.35 us -> 4.27 us  [chain(): lax.ppermute(inclusive, 'seq', [(t, f) for f, t in pairs] if back else pa...]
    pallas_call x58 -> x60, Pallas kernels: 52.6 us -> 49.1 us  [call(): pl.pallas_call(kernel, grid=(1,), out_shape=out_shape, in_specs=specs, ou...]
    unnamed x138 -> x136, local copies, waits for them, and re-layouts: 16.5 us -> 13.5 us
  transfers between devices with their start and end apart: 94 -> 94, of which waited for: 28 -> 32; matrix products, arithmetic and copies ran while one was open for 6% -> 3% of each run, Pallas kernels for 25% -> 25%
where the time goes in v3:
time: 332 us; the launch traced here: 331 us
  starting transfers between devices  107 us (32%)
  Pallas kernels  101 us (30%)
  waiting for transfers between devices  97.3 us (29%)
  local copies, waits for them, and re-layouts  16.3 us (5%)
  other arithmetic  5.33 us (2%)
    ppermute x84, waiting for transfers between devices, swap(): lax.ppermute(a, axis, [(k, k ^ bit) for k in range(lax.axis_size(axis))])  86.8 us
    ppermute x84, starting transfers between devices, swap(): lax.ppermute(a, axis, [(k, k ^ bit) for k in range(lax.axis_size(axis))])  85 us
    pallas_call x60, Pallas kernels, call(): pl.pallas_call(kernel, grid=(1,), out_shape=out_shape, in_specs=specs, ou...  49.1 us
    unnamed x136, local copies, waits for them, and re-layouts  13.5 us
    pallas_call x1, Pallas kernels, feed_forward(): pl.pallas_call(mlp_kernel, grid=(units // step,), out_shape=(unit_out, un...  11.6 us
    ppermute x4, starting transfers between devices, chain(): lax.ppermute(inclusive, 'seq', [(t, f) for f, t in pairs] if back else pa...  11.4 us
    pallas_call x1, Pallas kernels, ssm_back(): pl.pallas_call(back_kernel, grid=(NST // GROUP,), out_shape=(jax.ShapeDty...  9.99 us
    pallas_call x1, Pallas kernels, attend_back(): pl.pallas_call(attend_back_kernel, grid_spec=pltpu.PrefetchScalarGridSpec...  7.18 us
  transfers between devices with their start and end apart: 94, of which 32 were waited for; matrix products, arithmetic and copies ran while one was open for 3% of the time, Pallas kernels for 25%

profile of v3, /device:TPU:1, one launch (start us, length us, event | category | flops | bytes accessed | tf_op | source)
XLA Modules:
  0.0 331.3 jit_solution(17827272331581708018)
XLA Ops:
  1.3 3.0 shares.1
  4.5 2.1 collective-permute-start
  7.7 1.6 collective-permute-start.1
  12.5 2.2 collective-permute-start.3
  14.9 2.5 collective-permute-start.5
  17.4 1.6 collective-permute-start.8
  19.1 11.0 %collective-permute-done.4.b_ref = bf16[2,64,1024]{2,1,0:T(8,128)(2,1)S(1)} collective-permute-done((bf16[2,64,1024]{2,1,0:T(8,128)(2,1)S(1)}, bf16[2,64,1024]{2,1,0:T(8,128)(2,1)S(1)}, u32[]{:S(2)}, u32[]{:S(2)}) %collective-permute-start.4) | collective-permute-done | bytes 262176 | tf_op jit(solution)/shard_map/ppermute | solution.py:26
  35.4 2.0 first_norm.1
  39.9 2.6 collective-permute-done.9.refs_1_
  44.0 3.2 collective-permute-start.12
  48.9 3.0 collective-permute-start.18
  54.2 2.2 collective-permute-start.14
  57.4 1.6 collective-permute-done.12.b_ref
  59.0 2.2 collective-permute-start.17
  62.0 5.7 %collective-permute-start.19 = (f32[16,4,128]{2,1,0:T(4,128)S(1)}, f32[16,4,128]{2,1,0:T(4,128)S(1)}, u32[]{:S(2)}, u32[]{:S(2)}) collective-permute-start(f32[16,4,128]{2,1,0:T(4,128)S(1)} %multiply_add_fusion.6), channel_id=1, source_target_pairs={{0,4},{1,5},{2,6},{3,7},{8,12},{9,13},{10,14},{11,15},{16,20},{17,... | collective-permute-start | bytes 98312 | tf_op jit(solution)/shard_map/ppermute | solution.py:1263
  71.6 2.8 ssm_context.1
  75.0 4.0 %collective-permute-start.20 = (bf16[256,256]{1,0:T(8,128)(2,1)}, bf16[256,256]{1,0:T(8,128)(2,1)}, u32[]{:S(2)}, u32[]{:S(2)}) collective-permute-start(bf16[256,256]{1,0:T(8,128)(2,1)} %get-tuple-element.226), channel_id=1, source_target_pairs={{0,2},{1,3},{2,4},{3,5},{4,6},{5,7},{8,10},{9,11},{10,12},{11,13},... | collective-permute-start | bytes 393224 | tf_op jit(solution)/shard_map/ppermute | solution.py:1282
  81.2 1.5 place_weight.3
  82.8 2.9 collective-permute-done.20
  87.4 1.6 collective-permute-start.23
  89.1 1.5 collective-permute-done.24.c2
  90.6 2.3 collective-permute-start.25
  94.0 5.3 %collective-permute-done.27.b_ref = bf16[2,64,1024]{2,1,0:T(8,128)(2,1)S(1)} collective-permute-done((bf16[2,64,1024]{2,1,0:T(8,128)(2,1)S(1)}, bf16[2,64,1024]{2,1,0:T(8,128)(2,1)S(1)}, u32[]{:S(2)}, u32[]{:S(2)}) %collective-permute-start.27) | collective-permute-done | bytes 262176 | tf_op jit(solution)/shard_map/ppermute | solution.py:26
  99.3 1.7 collective-permute-start.29
  102.6 1.8 convolution_convert_fusion.q0.q1.k0.k1.v0.v1
  105.4 5.0 %attend.1.x_ref.att_ref = bf16[1024,256]{1,0:T(8,128)(2,1)S(1)} custom-call(s32[1]{0:T(128)} %bitcast.3.late.half_ref, bf16[1024,768]{1,0:T(8,128)(2,1)S(1)} %convolution_convert_fusion.q0.q1.k0.k1.v0.v1, bf16[1024,768]{1,0:T(8,128)(2,1)S(1)} %convolution_convert_fusion.q0.q1.k0.k1.v0.v1, bf16[1024,768]{1,0:T(8,128)(2,1)S(1)} %convolution_convert_fusion.q0.q1.k0.k1.v0.v1, ...), custom_call_target="tpu_custom_call" | custom-call | tf_op jit(solution)/shard_map/attend/pallas_call | solution.py:778
  110.5 1.9 collective-permute-done.31.w3
  113.9 3.2 collective-permute-start.35
  120.3 8.5 %collective-permute-done.35.refs_1_ = bf16[4,64,1024]{2,1,0:T(8,128)(2,1)S(1)} collective-permute-done((bf16[4,64,1024]{2,1,0:T(8,128)(2,1)S(1)}, bf16[4,64,1024]{2,1,0:T(8,128)(2,1)S(1)}, u32[]{:S(2)}, u32[]{:S(2)}) %collective-permute-start.35) | collective-permute-done | bytes 524320 | tf_op jit(solution)/shard_map/ppermute | solution.py:26
  129.7 3.3 %collective-permute-done.34.far = bf16[256,1024]{1,0:T(8,128)(2,1)S(1)} collective-permute-done((bf16[256,1024]{1,0:T(8,128)(2,1)S(1)}, bf16[256,1024]{1,0:T(8,128)(2,1)S(1)}, u32[]{:S(2)}, u32[]{:S(2)}) %collective-permute-start.34) | collective-permute-done | bytes 524320 | tf_op jit(solution)/shard_map/ppermute | solution.py:26
  136.0 10.2 %collective-permute-done.38.m2.x2 = bf16[256,1024]{1,0:T(8,128)(2,1)S(1)} collective-permute-done((bf16[256,1024]{1,0:T(8,128)(2,1)S(1)}, bf16[256,1024]{1,0:T(8,128)(2,1)S(1)}, u32[]{:S(2)}, u32[]{:S(2)}) %collective-permute-start.38) | collective-permute-done | bytes 524320 | tf_op jit(solution)/shard_map/ppermute | solution.py:26
  146.2 1.7 collective-permute-start.39
  150.9 11.6 %feed_forward.1 = (bf16[1024,1024]{1,0:T(8,128)(2,1)S(1)}, bf16[1024,1024]{1,0:T(8,128)(2,1)S(1)}, f32[256,1024]{1,0:T(8,128)S(1)}, bf16[256,1024]{1,0:T(8,128)(...) custom-call(bf16[256,1024]{1,0:T(8,128)(2,1)S(1)} %get-tuple-element.255.m0.x0, ...), custom_call_target="tpu_custom_call" | custom-call | tf_op jit(solution)/shard_map/feed_forward/pallas_call | solution.py:907
  162.9 3.2 down_grad.1
  168.1 3.5 %up_grad.1 = bf16[1024,1024]{1,0:T(8,128)(2,1)S(1)} custom-call(bf16[256,1024]{1,0:T(8,128)(2,1)S(1)} %get-tuple-element.255.m0.x0, bf16[256,1024]{1,0:T(8,128)(2,1)S(1)} %collective-permute-done.37.m1.x1, bf16[256,1024]{1,0:T(8,128)(2,1)S(1)} %collective-permute-done.38.m2.x2, bf16[256,1024]{1,0:T(8,128)(2,1)S(1)} %collective-permute-done.39.m3.x3, ...), custom_call_target="tpu_custom_call" | custom-call | tf_op jit(solution)/shard_map/up_grad/pallas_call | solution.py:951
  172.4 2.3 down_dot.1
  176.6 3.2 collective-permute-done.46.came_ref
  184.4 1.5 collective-permute-start.51
  185.9 9.0 %collective-permute-done.52.h2 = bf16[256,1024]{1,0:T(8,128)(2,1)S(1)} collective-permute-done((bf16[256,1024]{1,0:T(8,128)(2,1)S(1)}, bf16[256,1024]{1,0:T(8,128)(2,1)S(1)}, u32[]{:S(2)}, u32[]{:S(2)}) %collective-permute-start.52) | collective-permute-done | bytes 524320 | tf_op jit(solution)/shard_map/ppermute | solution.py:26
  194.9 1.8 collective-permute-start.53
  204.4 7.2 %attend_back.1 = (bf16[1024,768]{1,0:T(8,128)(2,1)S(1)}, bf16[256,512]{1,0:T(8,128)(2,1)S(1)}) custom-call(s32[1]{0:T(128)} %bitcast.3.late.half_ref, bf16[1024,768]{1,0:T(8,128)(2,1)S(1)} %convolution_convert_fusion.q0.q1.k0.k1.v0.v1, bf16[1024,768]{1,0:T(8,128)(2,1)S(1)} %convolution_convert_fusion.q0.q1.k0.k1.v0.v1, ...), custom_call_target="tpu_custom_call" | custom-call | tf_op jit(solution)/shard_map/attend_back/pallas_call | solution.py:798
  218.3 5.1 %attn_grad.1 = bf16[1024,1024]{1,0:T(8,128)(2,1)S(1)} custom-call(s32[2]{0:T(128)S(1)} %copy-done.36, bf16[1024,1024]{1,0:T(8,128)(2,1)S(1)} %copy-done.15, bf16[1024,768]{1,0:T(8,128)(2,1)S(1)} %get-tuple-element.303.dq_ref, bf16[256,1024]{1,0:T(8,128)(2,1)S(1)} %get-tuple-element.304.ctx_ref, bf16[256,512]{1,0:T(8,128)(2,1)S(1)} %get-tuple-element.297.d_ref.dctx_ref, ...), custom_call_target="tpu_custom_call" | custom-call | tf_op jit(solution)/shard_map/attn_grad/pallas_call | solution.py:278
  229.8 1.5 collective-permute-done.66.e3
  238.8 3.0 collective-permute-start.72
  243.5 3.5 %first_context.1 = (f32[16,8,128]{2,1,0:T(8,128)}, f32[16,8,128]{2,1,0:T(8,128)}, f32[16,8,128]{2,1,0:T(8,128)}) custom-call(f32[128,8,128]{2,1,0:T(8,128)} %copy-done.16, f32[16,8,128]{2,1,0:T(8,128)} %copy-done.12, f32[16,8,128]{2,1,0:T(8,128)} %copy-done.24, f32[16,8,128]{2,1,0:T(8,128)} %copy-done.35), custom_call_target="tpu_custom_call" | custom-call | tf_op jit(solution)/shard_map/first_context/pallas_call | solution.py:597
  250.9 4.3 %collective-permute-done.70 = f32[16,4,128]{2,1,0:T(4,128)S(1)} collective-permute-done((f32[16,4,128]{2,1,0:T(4,128)S(1)}, f32[16,4,128]{2,1,0:T(4,128)S(1)}, u32[]{:S(2)}, u32[]{:S(2)}) %collective-permute-start.70) | collective-permute-done | bytes 32800 | tf_op jit(solution)/shard_map/ppermute | solution.py:1263
  258.9 2.1 collective-permute-start.76
  264.8 10.0 %ssm_back.1 = (f32[256,8,128]{2,1,0:T(8,128)S(1)}, f32[16,8,128]{2,1,0:T(8,128)S(1)}, f32[16,8,128]{2,1,0:T(8,128)S(1)}, f32[16,8,128]{2,1,0:T(8,128)S(1)}, f32[16,8,128]{2,1,0:T(8,128)S(1)}) custom-call(f32[256,8,128]{2,1,0:T(8,128)S(1)} %get-tuple-element.206.u_ref, f32[128,8,128]{2,1,0:T(8,128)S(1)} %copy-done.33, f32[16,8,128]{2,1,0:T(8,128)S(1)} %copy-done.13, ...), custom_call_target="tpu_custom_call" | custom-call | tf_op jit(solution)/shard_map/ssm_back/pallas_call | solution.py:679
  274.8 1.7 collective-permute-done.73.refs_0_
  276.5 1.9 collective-permute-done.74.b_ref
  278.4 3.8 %inputs_grad.1 = (f32[256,1024]{1,0:T(8,128)S(1)}, bf16[256,1024]{1,0:T(8,128)(2,1)S(1)}, f32[256,1024]{1,0:T(8,128)S(1)}, bf16[256,1024]{1,0:T(8,128)(2,1)S(1)}, f32[1,1024]{1,0:T(1,128)S(1)}) custom-call(s32[2]{0:T(128)S(1)} %copy-done.36, bf16[1024,768]{1,0:T(8,128)(2,1)S(1)} %copy-done.7, bf16[1024,768]{1,0:T(8,128)(2,1)S(1)} %copy-done.3, ...), custom_call_target="tpu_custom_call" | custom-call | tf_op jit(solution)/shard_map/inputs_grad/pallas_call | solution.py:109
  282.5 2.6 collective-permute-start.78
  290.6 1.4 collective-permute-start.81
  292.0 8.0 %collective-permute-done.79.far = bf16[256,1024]{1,0:T(8,128)(2,1)S(1)} collective-permute-done((bf16[256,1024]{1,0:T(8,128)(2,1)S(1)}, bf16[256,1024]{1,0:T(8,128)(2,1)S(1)}, u32[]{:S(2)}, u32[]{:S(2)}) %collective-permute-start.79) | collective-permute-done | bytes 524320 | tf_op jit(solution)/shard_map/ppermute | solution.py:26
  301.3 1.5 collective-permute-done.86.b_ref
  303.0 3.0 collective-permute-done.81
  306.9 3.7 %collective-permute-done.83 = f32[176,128]{1,0:T(8,128)S(1)} collective-permute-done((f32[176,128]{1,0:T(8,128)S(1)}, f32[176,128]{1,0:T(8,128)S(1)}, u32[]{:S(2)}, u32[]{:S(2)}) %collective-permute-start.83) | collective-permute-done | bytes 90144 | tf_op jit(solution)/shard_map/ppermute | solution.py:26
  311.1 1.8 collective-permute-start.88
  314.2 2.0 final_down.1
  317.3 3.0 collective-permute-start.85
  320.4 2.1 final_up.1
  324.0 2.0 collective-permute-done.92.p2
  325.9 1.7 collective-permute-start.93
  327.6 2.0 final_attn.1
  (373 shorter events, 108.6 us)
Async XLA Ops:
  10.6 19.6 %collective-permute-start.6 = (bf16[256,1024]{1,0:T(8,128)(2,1)S(1)}, bf16[256,1024]{1,0:T(8,128)(2,1)S(1)}, u32[]{:S(2)}, u32[]{:S(2)}) collective-permute-start(bf16[256,1024]{1,0:T(8,128)(2,1)S(1)} %bitcast.70), channel_id=1, source_target_pairs={{0,1},{1,0},{2,3},{3,2},{4,5},{5,4},{6,7},{7,6},{8,9},{9,8},{10,11... | collective-permute-start | bytes 1572872 | tf_op jit(solution)/shard_map/ppermute | solution.py:26
  14.7 15.3 %collective-permute-start.4 = (bf16[2,64,1024]{2,1,0:T(8,128)(2,1)S(1)}, bf16[2,64,1024]{2,1,0:T(8,128)(2,1)S(1)}, u32[]{:S(2)}, u32[]{:S(2)}) collective-permute-start(bf16[2,64,1024]{2,1,0:T(8,128)(2,1)S(1)} %append.12.a_ref), channel_id=1, source_target_pairs={{0,4},{1,5},{2,6},{3,7},{4,0},{5,1},{6,2},{7,3},{8,12},{9,13},{10,... | collective-permute-start | bytes 786440 | tf_op jit(solution)/shard_map/ppermute | solution.py:26
  14.9 18.6 %collective-permute-start.5 = (bf16[256,1024]{1,0:T(8,128)(2,1)S(1)}, bf16[256,1024]{1,0:T(8,128)(2,1)S(1)}, u32[]{:S(2)}, u32[]{:S(2)}) collective-permute-start(bf16[256,1024]{1,0:T(8,128)(2,1)S(1)} %bitcast.71), channel_id=1, source_target_pairs={{0,8},{8,0},{16,24},{24,16},{1,9},{9,1},{17,25},{25,17},{2,10},{10... | collective-permute-start | bytes 1572872 | tf_op jit(solution)/shard_map/ppermute | solution.py:26
  17.4 12.7 %collective-permute-start.8 = (bf16[1,64,1024]{2,1,0:T(8,128)(2,1)}, bf16[1,64,1024]{2,1,0:T(8,128)(2,1)S(1)}, u32[]{:S(2)}, u32[]{:S(2)}) collective-permute-start(bf16[1,64,1024]{2,1,0:T(8,128)(2,1)} %bitcast.101), channel_id=1, source_target_pairs={{0,1},{1,0},{2,3},{3,2},{4,5},{5,4},{6,7},{7,6},{8,9},{9,8},{10,11... | collective-permute-start | bytes 393224 | tf_op jit(solution)/shard_map/ppermute | solution.py:26
  30.1 12.4 %collective-permute-start.9 = (bf16[4,64,1024]{2,1,0:T(8,128)(2,1)S(1)}, bf16[4,64,1024]{2,1,0:T(8,128)(2,1)}, u32[]{:S(2)}, u32[]{:S(2)}) collective-permute-start(bf16[4,64,1024]{2,1,0:T(8,128)(2,1)S(1)} %append.13.refs_0_), channel_id=1, source_target_pairs={{0,2},{1,3},{2,0},{3,1},{4,6},{5,7},{6,4},{7,5},{8,10},{9,11},{10,... | collective-permute-start | bytes 1572872 | tf_op jit(solution)/shard_map/ppermute | solution.py:26
  32.2 16.7 %collective-permute-start.10 = (bf16[4,64,1024]{2,1,0:T(8,128)(2,1)S(1)}, bf16[4,64,1024]{2,1,0:T(8,128)(2,1)}, u32[]{:S(2)}, u32[]{:S(2)}) collective-permute-start(bf16[4,64,1024]{2,1,0:T(8,128)(2,1)S(1)} %append.13.refs_0_), channel_id=1, source_target_pairs={{0,16},{8,24},{16,0},{24,8},{1,17},{9,25},{17,1},{25,9},{2,18},{10... | collective-permute-start | bytes 1572872 | tf_op jit(solution)/shard_map/ppermute | solution.py:26
  42.5 18.6 %collective-permute-start.11 = (bf16[4,64,1024]{2,1,0:T(8,128)(2,1)}, bf16[4,64,1024]{2,1,0:T(8,128)(2,1)}, u32[]{:S(2)}, u32[]{:S(2)}) collective-permute-start(bf16[4,64,1024]{2,1,0:T(8,128)(2,1)} %collective-permute-done.9.refs_1_), channel_id=1, source_target_pairs={{0,16},{8,24},{16,0},{24,8},{1,17},{9,25},{17,1},{25,9},{2,18},{10... | collective-permute-start | bytes 1572872 | tf_op jit(solution)/shard_map/ppermute | solution.py:26
  44.0 14.9 %collective-permute-start.12 = (bf16[2,64,1024]{2,1,0:T(8,128)(2,1)}, bf16[2,64,1024]{2,1,0:T(8,128)(2,1)}, u32[]{:S(2)}, u32[]{:S(2)}) collective-permute-start(bf16[2,64,1024]{2,1,0:T(8,128)(2,1)} %append.14.a_ref), channel_id=1, source_target_pairs={{0,4},{1,5},{2,6},{3,7},{4,0},{5,1},{6,2},{7,3},{8,12},{9,13},{10,... | collective-permute-start | bytes 786440 | tf_op jit(solution)/shard_map/ppermute | solution.py:26
  54.2 13.6 %collective-permute-start.14 = (f32[16,256]{1,0:T(8,128)S(1)}, f32[16,256]{1,0:T(8,128)S(1)}, u32[]{:S(2)}, u32[]{:S(2)}) collective-permute-start(f32[16,256]{1,0:T(8,128)S(1)} %get-tuple-element.215), channel_id=1, source_target_pairs={{0,8},{8,0},{16,24},{24,16},{1,9},{9,1},{17,25},{25,17},{2,10},{10... | collective-permute-start | bytes 49160 | tf_op jit(solution)/shard_map/ppermute | solution.py:26
  56.4 11.3 %collective-permute-start.15 = (f32[16,256]{1,0:T(8,128)S(1)}, f32[16,256]{1,0:T(8,128)S(1)}, u32[]{:S(2)}, u32[]{:S(2)}) collective-permute-start(f32[16,256]{1,0:T(8,128)S(1)} %get-tuple-element.217), channel_id=1, source_target_pairs={{0,8},{8,0},{16,24},{24,16},{1,9},{9,1},{17,25},{25,17},{2,10},{10... | collective-permute-start | bytes 49160 | tf_op jit(solution)/shard_map/ppermute | solution.py:26
  56.5 11.3 %collective-permute-start.16 = (f32[16,256]{1,0:T(8,128)S(1)}, f32[16,256]{1,0:T(8,128)S(1)}, u32[]{:S(2)}, u32[]{:S(2)}) collective-permute-start(f32[16,256]{1,0:T(8,128)S(1)} %get-tuple-element.218), channel_id=1, source_target_pairs={{0,1},{1,0},{2,3},{3,2},{4,5},{5,4},{6,7},{7,6},{8,9},{9,8},{10,11... | collective-permute-start | bytes 49160 | tf_op jit(solution)/shard_map/ppermute | solution.py:26
  59.0 8.9 %collective-permute-start.17 = (f32[16,256]{1,0:T(8,128)S(1)}, f32[16,256]{1,0:T(8,128)S(1)}, u32[]{:S(2)}, u32[]{:S(2)}) collective-permute-start(f32[16,256]{1,0:T(8,128)S(1)} %get-tuple-element.219), channel_id=1, source_target_pairs={{0,9},{1,8},{2,11},{3,10},{4,13},{5,12},{6,15},{7,14},{8,1},{9,0},... | collective-permute-start | bytes 49160 | tf_op jit(solution)/shard_map/ppermute | solution.py:36
  62.0 8.8 %collective-permute-start.19 = (f32[16,4,128]{2,1,0:T(4,128)S(1)}, f32[16,4,128]{2,1,0:T(4,128)S(1)}, u32[]{:S(2)}, u32[]{:S(2)}) collective-permute-start(f32[16,4,128]{2,1,0:T(4,128)S(1)} %multiply_add_fusion.6), channel_id=1, source_target_pairs={{0,4},{1,5},{2,6},{3,7},{8,12},{9,13},{10,14},{11,15},{16,20},{17,... | collective-permute-start | bytes 98312 | tf_op jit(solution)/shard_map/ppermute | solution.py:1263
  68.8 10.5 %collective-permute-start.22 = (bf16[1,64,1024]{2,1,0:T(8,128)(2,1)}, bf16[1,64,1024]{2,1,0:T(8,128)(2,1)}, u32[]{:S(2)}, u32[]{:S(2)}) collective-permute-start(bf16[1,64,1024]{2,1,0:T(8,128)(2,1)} %bitcast.100), channel_id=1, source_target_pairs={{0,1},{1,0},{2,3},{3,2},{4,5},{5,4},{6,7},{7,6},{8,9},{9,8},{10,11... | collective-permute-start | bytes 393224 | tf_op jit(solution)/shard_map/ppermute | solution.py:26
  71.4 14.9 %collective-permute-start.21 = (bf16[4,64,1024]{2,1,0:T(8,128)(2,1)S(1)}, bf16[4,64,1024]{2,1,0:T(8,128)(2,1)}, u32[]{:S(2)}, u32[]{:S(2)}) collective-permute-start(bf16[4,64,1024]{2,1,0:T(8,128)(2,1)S(1)} %append.15.refs_0_), channel_id=1, source_target_pairs={{0,2},{1,3},{2,0},{3,1},{4,6},{5,7},{6,4},{7,5},{8,10},{9,11},{10,... | collective-permute-start | bytes 1572872 | tf_op jit(solution)/shard_map/ppermute | solution.py:26
  75.0 10.7 %collective-permute-start.20 = (bf16[256,256]{1,0:T(8,128)(2,1)}, bf16[256,256]{1,0:T(8,128)(2,1)}, u32[]{:S(2)}, u32[]{:S(2)}) collective-permute-start(bf16[256,256]{1,0:T(8,128)(2,1)} %get-tuple-element.226), channel_id=1, source_target_pairs={{0,2},{1,3},{2,4},{3,5},{4,6},{5,7},{8,10},{9,11},{10,12},{11,13},... | collective-permute-start | bytes 393224 | tf_op jit(solution)/shard_map/ppermute | solution.py:1282
  79.0 13.9 %collective-permute-start.13 = (bf16[4,64,1024]{2,1,0:T(8,128)(2,1)S(1)}, bf16[4,64,1024]{2,1,0:T(8,128)(2,1)S(1)}, u32[]{:S(2)}, u32[]{:S(2)}) collective-permute-start(bf16[4,64,1024]{2,1,0:T(8,128)(2,1)S(1)} %append.15.refs_0_), channel_id=1, source_target_pairs={{0,16},{8,24},{16,0},{24,8},{1,17},{9,25},{17,1},{25,9},{2,18},{10... | collective-permute-start | bytes 1572872 | tf_op jit(solution)/shard_map/ppermute | solution.py:26
  85.7 13.6 %collective-permute-start.27 = (bf16[2,64,1024]{2,1,0:T(8,128)(2,1)S(1)}, bf16[2,64,1024]{2,1,0:T(8,128)(2,1)S(1)}, u32[]{:S(2)}, u32[]{:S(2)}) collective-permute-start(bf16[2,64,1024]{2,1,0:T(8,128)(2,1)S(1)} %append.16.a_ref), channel_id=1, source_target_pairs={{0,4},{1,5},{2,6},{3,7},{4,0},{5,1},{6,2},{7,3},{8,12},{9,13},{10,... | collective-permute-start | bytes 786440 | tf_op jit(solution)/shard_map/ppermute | solution.py:26
  87.4 13.5 %collective-permute-start.23 = (bf16[256,256]{1,0:T(8,128)(2,1)S(1)}, bf16[256,256]{1,0:T(8,128)(2,1)S(1)}, u32[]{:S(2)}, u32[]{:S(2)}) collective-permute-start(bf16[256,256]{1,0:T(8,128)(2,1)S(1)} %broadcast_select_fusion.c0), channel_id=1, source_target_pairs={{0,8},{8,0},{16,24},{24,16},{1,9},{9,1},{17,25},{25,17},{2,10},{10... | collective-permute-start | bytes 393224 | tf_op jit(solution)/shard_map/ppermute | solution.py:26
  90.6 10.7 %collective-permute-start.25 = (bf16[256,256]{1,0:T(8,128)(2,1)S(1)}, bf16[256,256]{1,0:T(8,128)(2,1)S(1)}, u32[]{:S(2)}, u32[]{:S(2)}) collective-permute-start(bf16[256,256]{1,0:T(8,128)(2,1)S(1)} %collective-permute-done.24.c2), channel_id=1, source_target_pairs={{0,8},{8,0},{16,24},{24,16},{1,9},{9,1},{17,25},{25,17},{2,10},{10... | collective-permute-start | bytes 393224 | tf_op jit(solution)/shard_map/ppermute | solution.py:26
  92.9 17.5 %collective-permute-start.28 = (bf16[4,64,1024]{2,1,0:T(8,128)(2,1)}, bf16[4,64,1024]{2,1,0:T(8,128)(2,1)S(1)}, u32[]{:S(2)}, u32[]{:S(2)}) collective-permute-start(bf16[4,64,1024]{2,1,0:T(8,128)(2,1)} %collective-permute-done.21.refs_1_), channel_id=1, source_target_pairs={{0,16},{8,24},{16,0},{24,8},{1,17},{9,25},{17,1},{25,9},{2,18},{10... | collective-permute-start | bytes 1572872 | tf_op jit(solution)/shard_map/ppermute | solution.py:26
  93.2 17.3 %collective-permute-start.26 = (bf16[256,1024]{1,0:T(8,128)(2,1)S(1)}, bf16[256,1024]{1,0:T(8,128)(2,1)S(1)}, u32[]{:S(2)}, u32[]{:S(2)}) collective-permute-start(bf16[256,1024]{1,0:T(8,128)(2,1)S(1)} %bitcast.76), channel_id=1, source_target_pairs={{0,1},{1,0},{2,3},{3,2},{4,5},{5,4},{6,7},{7,6},{8,9},{9,8},{10,11... | collective-permute-start | bytes 1572872 | tf_op jit(solution)/shard_map/ppermute | solution.py:26
  99.3 11.2 %collective-permute-start.29 = (bf16[256,256]{1,0:T(8,128)(2,1)S(1)}, bf16[256,256]{1,0:T(8,128)(2,1)S(1)}, u32[]{:S(2)}, u32[]{:S(2)}) collective-permute-start(bf16[256,256]{1,0:T(8,128)(2,1)S(1)} %get-tuple-element.243), channel_id=1, source_target_pairs={{0,8},{8,0},{16,24},{24,16},{1,9},{9,1},{17,25},{25,17},{2,10},{10... | collective-permute-start | bytes 393224 | tf_op jit(solution)/shard_map/ppermute | solution.py:26
  100.9 9.5 %collective-permute-start.30 = (bf16[256,256]{1,0:T(8,128)(2,1)S(1)}, bf16[256,256]{1,0:T(8,128)(2,1)S(1)}, u32[]{:S(2)}, u32[]{:S(2)}) collective-permute-start(bf16[256,256]{1,0:T(8,128)(2,1)S(1)} %get-tuple-element.244), channel_id=1, source_target_pairs={{0,1},{1,0},{2,3},{3,2},{4,5},{5,4},{6,7},{7,6},{8,9},{9,8},{10,11... | collective-permute-start | bytes 393224 | tf_op jit(solution)/shard_map/ppermute | solution.py:26
  101.3 11.1 %collective-permute-start.31 = (bf16[256,256]{1,0:T(8,128)(2,1)S(1)}, bf16[256,256]{1,0:T(8,128)(2,1)S(1)}, u32[]{:S(2)}, u32[]{:S(2)}) collective-permute-start(bf16[256,256]{1,0:T(8,128)(2,1)S(1)} %get-tuple-element.245), channel_id=1, source_target_pairs={{0,9},{1,8},{2,11},{3,10},{4,13},{5,12},{6,15},{7,14},{8,1},{9,0},... | collective-permute-start | bytes 393224 | tf_op jit(solution)/shard_map/ppermute | solution.py:36
  113.9 15.0 %collective-permute-start.35 = (bf16[4,64,1024]{2,1,0:T(8,128)(2,1)S(1)}, bf16[4,64,1024]{2,1,0:T(8,128)(2,1)S(1)}, u32[]{:S(2)}, u32[]{:S(2)}) collective-permute-start(bf16[4,64,1024]{2,1,0:T(8,128)(2,1)S(1)} %append.17.refs_0_), channel_id=1, source_target_pairs={{0,2},{1,3},{2,0},{3,1},{4,6},{5,7},{6,4},{7,5},{8,10},{9,11},{10,... | collective-permute-start | bytes 1572872 | tf_op jit(solution)/shard_map/ppermute | solution.py:26
  117.0 12.7 %collective-permute-start.36 = (bf16[4,64,1024]{2,1,0:T(8,128)(2,1)S(1)}, bf16[4,64,1024]{2,1,0:T(8,128)(2,1)S(1)}, u32[]{:S(2)}, u32[]{:S(2)}) collective-permute-start(bf16[4,64,1024]{2,1,0:T(8,128)(2,1)S(1)} %append.17.refs_0_), channel_id=1, source_target_pairs={{0,16},{8,24},{16,0},{24,8},{1,17},{9,25},{17,1},{25,9},{2,18},{10... | collective-permute-start | bytes 1572872 | tf_op jit(solution)/shard_map/ppermute | solution.py:26
  118.3 11.4 %collective-permute-start.32 = (bf16[256,1024]{1,0:T(8,128)(2,1)S(1)}, bf16[256,1024]{1,0:T(8,128)(2,1)S(1)}, u32[]{:S(2)}, u32[]{:S(2)}) collective-permute-start(bf16[256,1024]{1,0:T(8,128)(2,1)S(1)} %get-tuple-element.247), channel_id=1, source_target_pairs={{0,8},{8,0},{16,24},{24,16},{1,9},{9,1},{17,25},{25,17},{2,10},{10... | collective-permute-start | bytes 1572872 | tf_op jit(solution)/shard_map/ppermute | solution.py:26
  119.4 13.6 %collective-permute-start.34 = (bf16[256,1024]{1,0:T(8,128)(2,1)S(1)}, bf16[256,1024]{1,0:T(8,128)(2,1)S(1)}, u32[]{:S(2)}, u32[]{:S(2)}) collective-permute-start(bf16[256,1024]{1,0:T(8,128)(2,1)S(1)} %far_sum.5), channel_id=1, source_target_pairs={{0,1},{1,0},{2,3},{3,2},{4,5},{5,4},{6,7},{7,6},{8,9},{9,8},{10,11... | collective-permute-start | bytes 1572872 | tf_op jit(solution)/shard_map/ppermute | solution.py:26
  133.4 12.7 %collective-permute-start.38 = (bf16[256,1024]{1,0:T(8,128)(2,1)S(1)}, bf16[256,1024]{1,0:T(8,128)(2,1)S(1)}, u32[]{:S(2)}, u32[]{:S(2)}) collective-permute-start(bf16[256,1024]{1,0:T(8,128)(2,1)S(1)} %get-tuple-element.255.m0.x0), channel_id=1, source_target_pairs={{0,1},{1,0},{2,3},{3,2},{4,5},{5,4},{6,7},{7,6},{8,9},{9,8},{10,11... | collective-permute-start | bytes 1572872 | tf_op jit(solution)/shard_map/ppermute | solution.py:26
  134.4 15.2 %collective-permute-start.42 = (bf16[4,64,1024]{2,1,0:T(8,128)(2,1)S(1)}, bf16[4,64,1024]{2,1,0:T(8,128)(2,1)S(1)}, u32[]{:S(2)}, u32[]{:S(2)}) collective-permute-start(bf16[4,64,1024]{2,1,0:T(8,128)(2,1)S(1)} %collective-permute-done.35.refs_1_), channel_id=1, source_target_pairs={{0,16},{8,24},{16,0},{24,8},{1,17},{9,25},{17,1},{25,9},{2,18},{10... | collective-permute-start | bytes 1572872 | tf_op jit(solution)/shard_map/ppermute | solution.py:26
  134.6 15.7 %collective-permute-start.37 = (bf16[256,1024]{1,0:T(8,128)(2,1)S(1)}, bf16[256,1024]{1,0:T(8,128)(2,1)S(1)}, u32[]{:S(2)}, u32[]{:S(2)}) collective-permute-start(bf16[256,1024]{1,0:T(8,128)(2,1)S(1)} %get-tuple-element.255.m0.x0), channel_id=1, source_target_pairs={{0,8},{8,0},{16,24},{24,16},{1,9},{9,1},{17,25},{25,17},{2,10},{10... | collective-permute-start | bytes 1572872 | tf_op jit(solution)/shard_map/ppermute | solution.py:26
  166.3 13.5 %collective-permute-start.46 = (bf16[4,64,1024]{2,1,0:T(8,128)(2,1)S(1)}, bf16[4,64,1024]{2,1,0:T(8,128)(2,1)S(1)}, u32[]{:S(2)}, u32[]{:S(2)}) collective-permute-start(bf16[4,64,1024]{2,1,0:T(8,128)(2,1)S(1)} %get-tuple-element.262), channel_id=1, source_target_pairs={{0,16},{8,24},{16,0},{24,8},{1,17},{9,25},{17,1},{25,9},{2,18},{10... | collective-permute-start | bytes 1572872 | tf_op jit(solution)/shard_map/ppermute | solution.py:26
  166.6 13.3 %collective-permute-start.49 = (bf16[256,1024]{1,0:T(8,128)(2,1)S(1)}, bf16[256,1024]{1,0:T(8,128)(2,1)S(1)}, u32[]{:S(2)}, u32[]{:S(2)}) collective-permute-start(bf16[256,1024]{1,0:T(8,128)(2,1)S(1)} %get-tuple-element.278), channel_id=1, source_target_pairs={{0,8},{8,0},{16,24},{24,16},{1,9},{9,1},{17,25},{25,17},{2,10},{10... | collective-permute-start | bytes 1572872 | tf_op jit(solution)/shard_map/ppermute | solution.py:26
  167.1 13.6 %collective-permute-start.50 = (bf16[256,1024]{1,0:T(8,128)(2,1)S(1)}, bf16[256,1024]{1,0:T(8,128)(2,1)S(1)}, u32[]{:S(2)}, u32[]{:S(2)}) collective-permute-start(bf16[256,1024]{1,0:T(8,128)(2,1)S(1)} %far_sum.6), channel_id=1, source_target_pairs={{0,1},{1,0},{2,3},{3,2},{4,5},{5,4},{6,7},{7,6},{8,9},{9,8},{10,11... | collective-permute-start | bytes 1572872 | tf_op jit(solution)/shard_map/ppermute | solution.py:26
  182.3 12.6 %collective-permute-start.52 = (bf16[256,1024]{1,0:T(8,128)(2,1)S(1)}, bf16[256,1024]{1,0:T(8,128)(2,1)S(1)}, u32[]{:S(2)}, u32[]{:S(2)}) collective-permute-start(bf16[256,1024]{1,0:T(8,128)(2,1)S(1)} %get-tuple-element.285.h0), channel_id=1, source_target_pairs={{0,1},{1,0},{2,3},{3,2},{4,5},{5,4},{6,7},{7,6},{8,9},{9,8},{10,11... | collective-permute-start | bytes 1572872 | tf_op jit(solution)/shard_map/ppermute | solution.py:26
  183.2 14.7 %collective-permute-start.48 = (bf16[4,64,1024]{2,1,0:T(8,128)(2,1)S(1)}, bf16[4,64,1024]{2,1,0:T(8,128)(2,1)S(1)}, u32[]{:S(2)}, u32[]{:S(2)}) collective-permute-start(bf16[4,64,1024]{2,1,0:T(8,128)(2,1)S(1)} %leave_sum.3), channel_id=1, source_target_pairs={{0,2},{1,3},{2,0},{3,1},{4,6},{5,7},{6,4},{7,5},{8,10},{9,11},{10,... | collective-permute-start | bytes 1572872 | tf_op jit(solution)/shard_map/ppermute | solution.py:26
  183.5 14.4 %collective-permute-start.45 = (bf16[4,64,1024]{2,1,0:T(8,128)(2,1)S(1)}, bf16[4,64,1024]{2,1,0:T(8,128)(2,1)S(1)}, u32[]{:S(2)}, u32[]{:S(2)}) collective-permute-start(bf16[4,64,1024]{2,1,0:T(8,128)(2,1)S(1)} %get-tuple-element.270), channel_id=1, source_target_pairs={{0,16},{8,24},{16,0},{24,8},{1,17},{9,25},{17,1},{25,9},{2,18},{10... | collective-permute-start | bytes 1572872 | tf_op jit(solution)/shard_map/ppermute | solution.py:26
  184.4 15.0 %collective-permute-start.51 = (bf16[256,1024]{1,0:T(8,128)(2,1)S(1)}, bf16[256,1024]{1,0:T(8,128)(2,1)S(1)}, u32[]{:S(2)}, u32[]{:S(2)}) collective-permute-start(bf16[256,1024]{1,0:T(8,128)(2,1)S(1)} %get-tuple-element.285.h0), channel_id=1, source_target_pairs={{0,8},{8,0},{16,24},{24,16},{1,9},{9,1},{17,25},{25,17},{2,10},{10... | collective-permute-start | bytes 1572872 | tf_op jit(solution)/shard_map/ppermute | solution.py:26
  196.7 15.0 %collective-permute-start.54 = (bf16[4,64,1024]{2,1,0:T(8,128)(2,1)S(1)}, bf16[4,64,1024]{2,1,0:T(8,128)(2,1)S(1)}, u32[]{:S(2)}, u32[]{:S(2)}) collective-permute-start(bf16[4,64,1024]{2,1,0:T(8,128)(2,1)S(1)} %get-tuple-element.264), channel_id=1, source_target_pairs={{0,16},{8,24},{16,0},{24,8},{1,17},{9,25},{17,1},{25,9},{2,18},{10... | collective-permute-start | bytes 1572872 | tf_op jit(solution)/shard_map/ppermute | solution.py:26
  198.1 14.6 %collective-permute-start.55 = (bf16[2,64,1024]{2,1,0:T(8,128)(2,1)S(1)}, bf16[2,64,1024]{2,1,0:T(8,128)(2,1)S(1)}, u32[]{:S(2)}, u32[]{:S(2)}) collective-permute-start(bf16[2,64,1024]{2,1,0:T(8,128)(2,1)S(1)} %get-tuple-element.283), channel_id=1, source_target_pairs={{0,4},{1,5},{2,6},{3,7},{4,0},{5,1},{6,2},{7,3},{8,12},{9,13},{10,... | collective-permute-start | bytes 786440 | tf_op jit(solution)/shard_map/ppermute | solution.py:26
  202.1 12.0 %collective-permute-start.56 = (bf16[256,256]{1,0:T(8,128)(2,1)S(1)}, bf16[256,256]{1,0:T(8,128)(2,1)S(1)}, u32[]{:S(2)}, u32[]{:S(2)}) collective-permute-start(bf16[256,256]{1,0:T(8,128)(2,1)S(1)} %get-tuple-element.288), channel_id=1, source_target_pairs={{0,8},{8,0},{16,24},{24,16},{1,9},{9,1},{17,25},{25,17},{2,10},{10... | collective-permute-start | bytes 393224 | tf_op jit(solution)/shard_map/ppermute | solution.py:26
  202.7 11.3 %collective-permute-start.57 = (bf16[256,256]{1,0:T(8,128)(2,1)S(1)}, bf16[256,256]{1,0:T(8,128)(2,1)S(1)}, u32[]{:S(2)}, u32[]{:S(2)}) collective-permute-start(bf16[256,256]{1,0:T(8,128)(2,1)S(1)} %get-tuple-element.289), channel_id=1, source_target_pairs={{0,1},{1,0},{2,3},{3,2},{4,5},{5,4},{6,7},{7,6},{8,9},{9,8},{10,11... | collective-permute-start | bytes 393224 | tf_op jit(solution)/shard_map/ppermute | solution.py:26
  203.4 10.7 %collective-permute-start.58 = (bf16[256,256]{1,0:T(8,128)(2,1)S(1)}, bf16[256,256]{1,0:T(8,128)(2,1)S(1)}, u32[]{:S(2)}, u32[]{:S(2)}) collective-permute-start(bf16[256,256]{1,0:T(8,128)(2,1)S(1)} %get-tuple-element.290), channel_id=1, source_target_pairs={{0,9},{1,8},{2,11},{3,10},{4,13},{5,12},{6,15},{7,14},{8,1},{9,0},... | collective-permute-start | bytes 393224 | tf_op jit(solution)/shard_map/ppermute | solution.py:36
  217.7 24.2 %collective-permute-start.44 = (bf16[256,1024]{1,0:T(8,128)(2,1)S(1)}, bf16[256,1024]{1,0:T(8,128)(2,1)S(1)}, u32[]{:S(2)}, u32[]{:S(2)}) collective-permute-start(bf16[256,1024]{1,0:T(8,128)(2,1)S(1)} %get-tuple-element.269), channel_id=1, source_target_pairs={{0,8},{8,0},{16,24},{24,16},{1,9},{9,1},{17,25},{25,17},{2,10},{10... | collective-permute-start | bytes 1572872 | tf_op jit(solution)/shard_map/ppermute | solution.py:26
  224.4 24.3 %collective-permute-start.69 = (bf16[4,64,1024]{2,1,0:T(8,128)(2,1)}, bf16[4,64,1024]{2,1,0:T(8,128)(2,1)}, u32[]{:S(2)}, u32[]{:S(2)}) collective-permute-start(bf16[4,64,1024]{2,1,0:T(8,128)(2,1)} %get-tuple-element.314), channel_id=1, source_target_pairs={{0,16},{8,24},{16,0},{24,8},{1,17},{9,25},{17,1},{25,9},{2,18},{10... | collective-permute-start | bytes 1572872 | tf_op jit(solution)/shard_map/ppermute | solution.py:26
  225.1 9.6 %collective-permute-start.63 = (bf16[256,256]{1,0:T(8,128)(2,1)S(1)}, bf16[256,256]{1,0:T(8,128)(2,1)S(1)}, u32[]{:S(2)}, u32[]{:S(2)}) collective-permute-start(bf16[256,256]{1,0:T(8,128)(2,1)S(1)} %context_sum.1.own), channel_id=1, source_target_pairs={{2,0},{3,1},{4,2},{5,3},{6,4},{7,5},{10,8},{11,9},{12,10},{13,11},... | collective-permute-start | bytes 393224 | tf_op jit(solution)/shard_map/ppermute | solution.py:1371
  232.5 14.6 %collective-permute-start.68 = (bf16[1,64,1024]{2,1,0:T(8,128)(2,1)}, bf16[1,64,1024]{2,1,0:T(8,128)(2,1)}, u32[]{:S(2)}, u32[]{:S(2)}) collective-permute-start(bf16[1,64,1024]{2,1,0:T(8,128)(2,1)} %get-tuple-element.296), channel_id=1, source_target_pairs={{0,1},{1,0},{2,3},{3,2},{4,5},{5,4},{6,7},{7,6},{8,9},{9,8},{10,11... | collective-permute-start | bytes 393224 | tf_op jit(solution)/shard_map/ppermute | solution.py:26
  237.5 10.4 %collective-permute-start.67 = (f32[16,4,128]{2,1,0:T(4,128)S(1)}, f32[16,4,128]{2,1,0:T(4,128)S(1)}, u32[]{:S(2)}, u32[]{:S(2)}) collective-permute-start(f32[16,4,128]{2,1,0:T(4,128)S(1)} %get-tuple-element.373), channel_id=1, source_target_pairs={{2,0},{3,1},{4,2},{5,3},{6,4},{7,5},{10,8},{11,9},{12,10},{13,11},... | collective-permute-start | bytes 98312 | tf_op jit(solution)/shard_map/ppermute | solution.py:1263
  238.8 17.2 %collective-permute-start.72 = (bf16[4,64,1024]{2,1,0:T(8,128)(2,1)}, bf16[4,64,1024]{2,1,0:T(8,128)(2,1)}, u32[]{:S(2)}, u32[]{:S(2)}) collective-permute-start(bf16[4,64,1024]{2,1,0:T(8,128)(2,1)} %leave_sum.4), channel_id=1, source_target_pairs={{0,2},{1,3},{2,0},{3,1},{4,6},{5,7},{6,4},{7,5},{8,10},{9,11},{10,... | collective-permute-start | bytes 1572872 | tf_op jit(solution)/shard_map/ppermute | solution.py:26
  241.9 14.2 %collective-permute-start.71 = (bf16[4,64,1024]{2,1,0:T(8,128)(2,1)}, bf16[4,64,1024]{2,1,0:T(8,128)(2,1)}, u32[]{:S(2)}, u32[]{:S(2)}) collective-permute-start(bf16[4,64,1024]{2,1,0:T(8,128)(2,1)} %get-tuple-element.323), channel_id=1, source_target_pairs={{0,16},{8,24},{16,0},{24,8},{1,17},{9,25},{17,1},{25,9},{2,18},{10... | collective-permute-start | bytes 1572872 | tf_op jit(solution)/shard_map/ppermute | solution.py:26
  247.1 16.5 %collective-permute-start.43 = (bf16[256,1024]{1,0:T(8,128)(2,1)}, bf16[256,1024]{1,0:T(8,128)(2,1)S(1)}, u32[]{:S(2)}, u32[]{:S(2)}) collective-permute-start(bf16[256,1024]{1,0:T(8,128)(2,1)} %copy-done.59), channel_id=1, source_target_pairs={{0,8},{8,0},{16,24},{24,16},{1,9},{9,1},{17,25},{25,17},{2,10},{10... | collective-permute-start | bytes 1572872 | tf_op jit(solution)/shard_map/ppermute | solution.py:26
  247.9 15.6 %collective-permute-start.62 = (bf16[256,1024]{1,0:T(8,128)(2,1)}, bf16[256,1024]{1,0:T(8,128)(2,1)S(1)}, u32[]{:S(2)}, u32[]{:S(2)}) collective-permute-start(bf16[256,1024]{1,0:T(8,128)(2,1)} %copy-done.34), channel_id=1, source_target_pairs={{0,1},{1,0},{2,3},{3,2},{4,5},{5,4},{6,7},{7,6},{8,9},{9,8},{10,11... | collective-permute-start | bytes 1572872 | tf_op jit(solution)/shard_map/ppermute | solution.py:26
  258.9 23.4 %collective-permute-start.76 = (bf16[4,64,1024]{2,1,0:T(8,128)(2,1)S(1)}, bf16[4,64,1024]{2,1,0:T(8,128)(2,1)S(1)}, u32[]{:S(2)}, u32[]{:S(2)}) collective-permute-start(bf16[4,64,1024]{2,1,0:T(8,128)(2,1)S(1)} %leave_sum.5), channel_id=1, source_target_pairs={{0,2},{1,3},{2,0},{3,1},{4,6},{5,7},{6,4},{7,5},{8,10},{9,11},{10,... | collective-permute-start | bytes 1572872 | tf_op jit(solution)/shard_map/ppermute | solution.py:26
  261.0 21.3 %collective-permute-start.75 = (bf16[4,64,1024]{2,1,0:T(8,128)(2,1)S(1)}, bf16[4,64,1024]{2,1,0:T(8,128)(2,1)S(1)}, u32[]{:S(2)}, u32[]{:S(2)}) collective-permute-start(bf16[4,64,1024]{2,1,0:T(8,128)(2,1)S(1)} %copy-done.61), channel_id=1, source_target_pairs={{0,16},{8,24},{16,0},{24,8},{1,17},{9,25},{17,1},{25,9},{2,18},{10... | collective-permute-start | bytes 1572872 | tf_op jit(solution)/shard_map/ppermute | solution.py:26
  262.2 16.2 %collective-permute-start.74 = (bf16[2,64,1024]{2,1,0:T(8,128)(2,1)S(1)}, bf16[2,64,1024]{2,1,0:T(8,128)(2,1)S(1)}, u32[]{:S(2)}, u32[]{:S(2)}) collective-permute-start(bf16[2,64,1024]{2,1,0:T(8,128)(2,1)S(1)} %append.18.a_ref), channel_id=1, source_target_pairs={{0,16},{8,24},{16,0},{24,8},{1,17},{9,25},{17,1},{25,9},{2,18},{10... | collective-permute-start | bytes 786440 | tf_op jit(solution)/shard_map/ppermute | solution.py:26
  264.7 11.8 %collective-permute-start.73 = (bf16[2,64,1024]{2,1,0:T(8,128)(2,1)S(1)}, bf16[2,64,1024]{2,1,0:T(8,128)(2,1)S(1)}, u32[]{:S(2)}, u32[]{:S(2)}) collective-permute-start(bf16[2,64,1024]{2,1,0:T(8,128)(2,1)S(1)} %get-tuple-element.325), channel_id=1, source_target_pairs={{0,4},{1,5},{2,6},{3,7},{4,0},{5,1},{6,2},{7,3},{8,12},{9,13},{10,... | collective-permute-start | bytes 786440 | tf_op jit(solution)/shard_map/ppermute | solution.py:26
  286.8 13.2 %collective-permute-start.79 = (bf16[256,1024]{1,0:T(8,128)(2,1)S(1)}, bf16[256,1024]{1,0:T(8,128)(2,1)S(1)}, u32[]{:S(2)}, u32[]{:S(2)}) collective-permute-start(bf16[256,1024]{1,0:T(8,128)(2,1)S(1)} %far_sum.9), channel_id=1, source_target_pairs={{0,1},{1,0},{2,3},{3,2},{4,5},{5,4},{6,7},{7,6},{8,9},{9,8},{10,11... | collective-permute-start | bytes 1572872 | tf_op jit(solution)/shard_map/ppermute | solution.py:26
  287.7 18.4 %collective-permute-start.80 = (bf16[2,64,1024]{2,1,0:T(8,128)(2,1)S(1)}, bf16[2,64,1024]{2,1,0:T(8,128)(2,1)S(1)}, u32[]{:S(2)}, u32[]{:S(2)}) collective-permute-start(bf16[2,64,1024]{2,1,0:T(8,128)(2,1)S(1)} %get-tuple-element.343), channel_id=1, source_target_pairs={{0,4},{1,5},{2,6},{3,7},{4,0},{5,1},{6,2},{7,3},{8,12},{9,13},{10,... | collective-permute-start | bytes 786440 | tf_op jit(solution)/shard_map/ppermute | solution.py:26
  288.7 14.1 %collective-permute-start.86 = (bf16[1,64,1024]{2,1,0:T(8,128)(2,1)S(1)}, bf16[1,64,1024]{2,1,0:T(8,128)(2,1)S(1)}, u32[]{:S(2)}, u32[]{:S(2)}) collective-permute-start(bf16[1,64,1024]{2,1,0:T(8,128)(2,1)S(1)} %get-tuple-element.333), channel_id=1, source_target_pairs={{0,1},{1,0},{2,3},{3,2},{4,5},{5,4},{6,7},{7,6},{8,9},{9,8},{10,11... | collective-permute-start | bytes 393224 | tf_op jit(solution)/shard_map/ppermute | solution.py:26
  289.3 24.8 %collective-permute-start.89 = (bf16[4,64,1024]{2,1,0:T(8,128)(2,1)S(1)}, bf16[4,64,1024]{2,1,0:T(8,128)(2,1)S(1)}, u32[]{:S(2)}, u32[]{:S(2)}) collective-permute-start(bf16[4,64,1024]{2,1,0:T(8,128)(2,1)S(1)} %append.23.mine_ref), channel_id=1, source_target_pairs={{0,8},{8,0},{16,24},{24,16},{1,9},{9,1},{17,25},{25,17},{2,10},{10... | collective-permute-start | bytes 1572872 | tf_op jit(solution)/shard_map/ppermute | solution.py:26
  290.6 15.5 %collective-permute-start.81 = (f32[176,128]{1,0:T(8,128)S(1)}, f32[176,128]{1,0:T(8,128)S(1)}, u32[]{:S(2)}, u32[]{:S(2)}) collective-permute-start(f32[176,128]{1,0:T(8,128)S(1)} %small_pack.1), channel_id=1, source_target_pairs={{0,4},{1,5},{2,6},{3,7},{4,0},{5,1},{6,2},{7,3},{8,12},{9,13},{10,... | collective-permute-start | bytes 270344 | tf_op jit(solution)/shard_map/ppermute | solution.py:26
  311.1 9.3 %collective-permute-start.88 = (bf16[4,64,1024]{2,1,0:T(8,128)(2,1)S(1)}, bf16[4,64,1024]{2,1,0:T(8,128)(2,1)S(1)}, u32[]{:S(2)}, u32[]{:S(2)}) collective-permute-start(bf16[4,64,1024]{2,1,0:T(8,128)(2,1)S(1)} %append.22.mine_ref), channel_id=1, source_target_pairs={{0,8},{8,0},{16,24},{24,16},{1,9},{9,1},{17,25},{25,17},{2,10},{10... | collective-permute-start | bytes 1572872 | tf_op jit(solution)/shard_map/ppermute | solution.py:26
  317.3 10.3 %collective-permute-start.85 = (bf16[4,64,1024]{2,1,0:T(8,128)(2,1)S(1)}, bf16[4,64,1024]{2,1,0:T(8,128)(2,1)S(1)}, u32[]{:S(2)}, u32[]{:S(2)}) collective-permute-start(bf16[4,64,1024]{2,1,0:T(8,128)(2,1)S(1)} %append.20.mine_ref), channel_id=1, source_target_pairs={{0,8},{8,0},{16,24},{24,16},{1,9},{9,1},{17,25},{25,17},{2,10},{10... | collective-permute-start | bytes 1572872 | tf_op jit(solution)/shard_map/ppermute | solution.py:26
  (98 other events, 1201.7 us)

commit v4 on v3

--- a/solution.py
+++ b/solution.py
@@ -1388,21 +1388,20 @@
     sum_up.step(leaving)
     sum_attn.step(sum_up.sent)
     result = sum_team(result, d_context)
-    result = call(result_kernel, "result_sum", like((rows, dim), bf16), (hidden, *result[:3]), 0)
     lam_end = by_owner(end_cot[0] + g_second + decay * leaving, end_cot[1] + leaving)
     du, d_gin, d_a, d_gout, g_in = ssm_back(
         u, dy_full, a, gin, gout, state_in, after(lam_end, sum_attn.sent), d_a, d_gout
     )
 
-    sum_up.step(du)
     *d_inputs, d_gain_one = call(
         inputs_grad_kernel,
         "inputs_grad",
         part_types(rows, dim) + (jax.ShapeDtypeStruct((1, dim), f32),),
-        (idx, d_qkv, full_qkv, after(du, (result, sum_up.sent, down_blocks)), inv_one, *x_blocks),
+        (idx, d_qkv, full_qkv, after(du, result[:3]), inv_one, *x_blocks),
         scratch_shapes=[pltpu.VMEM((rows, dim), f32)],
     )
-    sum_attn.step(d_gain_one)
+    sum_up.step((d_gain_one, down_blocks))
+    sum_attn.step(sum_up.sent)
     d_inputs = after(d_inputs, sum_attn.sent)
     small_rows = (3 * NST * cols + 2 * dim + 2 * NST * cols) // LANES
     pack = call(
@@ -1428,7 +1427,9 @@
         d_up = spread_narrow(up_blocks, idx, w_up.shape, fb)
     else:
         d_up = spread_weight("up", up_blocks, idx, [w_up.shape], fb)[0]
-    sum_attn.step((pack, d_tokens))
+    result = after(result[:3], d_gain_one)
+    result = call(result_kernel, "result_sum", like((rows, dim), bf16), (hidden, *result), 0)
+    sum_attn.step((pack, d_tokens, result))
     for bit in others:
         pack = pack + swap(pack, "seq", bit)
     one, two = 3 * NST * cols // LANES, 3 * NST * cols // LANES + 2 * dim // LANES

time: 332 us -> 327 us (0.985)
  waiting for transfers between devices: 97.3 us -> 88.2 us
    ppermute x84, waiting for transfers between devices: 86.8 us -> 81 us  [swap(): lax.ppermute(a, axis, [(k, k ^ bit) for k in range(lax.axis_size(axis))])]
    unnamed x136 -> x142, local copies, waits for them, and re-layouts: 13.5 us -> 14 us
  transfers between devices with their start and end apart: 94 -> 94, of which waited for: 32 -> 29; matrix products, arithmetic and copies ran while one was open for 3% -> 3% of each run, Pallas kernels for 25% -> 25%
where the time goes in v4:
time: 327 us; the launch traced here: 326 us
  starting transfers between devices  110 us (34%)
  Pallas kernels  101 us (31%)
  waiting for transfers between devices  88.2 us (27%)
  local copies, waits for them, and re-layouts  16.8 us (5%)
  other arithmetic  5.32 us (2%)
    ppermute x84, starting transfers between devices, swap(): lax.ppermute(a, axis, [(k, k ^ bit) for k in range(lax.axis_size(axis))])  87.6 us
    ppermute x84, waiting for transfers between devices, swap(): lax.ppermute(a, axis, [(k, k ^ bit) for k in range(lax.axis_size(axis))])  81 us
    pallas_call x60, Pallas kernels, call(): pl.pallas_call(kernel, grid=(1,), out_shape=out_shape, in_specs=specs, ou...  49.2 us
    unnamed x142, local copies, waits for them, and re-layouts  14 us
    pallas_call x1, Pallas kernels, feed_forward(): pl.pallas_call(mlp_kernel, grid=(units // step,), out_shape=(unit_out, un...  11.6 us
    ppermute x4, starting transfers between devices, chain(): lax.ppermute(inclusive, 'seq', [(t, f) for f, t in pairs] if back else pa...  11.4 us
    pallas_call x1, Pallas kernels, ssm_back(): pl.pallas_call(back_kernel, grid=(NST // GROUP,), out_shape=(jax.ShapeDty...  9.99 us
    pallas_call x1, Pallas kernels, attend_back(): pl.pallas_call(attend_back_kernel, grid_spec=pltpu.PrefetchScalarGridSpec...  7.18 us
  transfers between devices with their start and end apart: 94, of which 29 were waited for; matrix products, arithmetic and copies ran while one was open for 3% of the time, Pallas kernels for 25%

profile of v4, /device:TPU:1, one launch (start us, length us, event | category | flops | bytes accessed | tf_op | source)
XLA Modules:
  0.0 325.6 jit_solution(22494757217439432)
XLA Ops:
  1.3 3.0 shares.1
  4.4 2.1 collective-permute-start
  7.7 1.6 collective-permute-start.1
  12.5 2.2 collective-permute-start.3
  14.9 2.5 collective-permute-start.5
  17.4 1.6 collective-permute-start.8
  19.0 11.0 %collective-permute-done.4.b_ref = bf16[2,64,1024]{2,1,0:T(8,128)(2,1)S(1)} collective-permute-done((bf16[2,64,1024]{2,1,0:T(8,128)(2,1)S(1)}, bf16[2,64,1024]{2,1,0:T(8,128)(2,1)S(1)}, u32[]{:S(2)}, u32[]{:S(2)}) %collective-permute-start.4) | collective-permute-done | bytes 262176 | tf_op jit(solution)/shard_map/ppermute | solution.py:26
  35.4 2.0 first_norm.1
  39.9 2.6 collective-permute-done.9.refs_1_
  44.0 3.2 collective-permute-start.12
  48.9 3.0 collective-permute-start.18
  54.2 2.2 collective-permute-start.14
  57.4 1.6 collective-permute-done.12.b_ref
  58.9 2.2 collective-permute-start.17
  62.0 5.7 %collective-permute-start.19 = (f32[16,4,128]{2,1,0:T(4,128)S(1)}, f32[16,4,128]{2,1,0:T(4,128)S(1)}, u32[]{:S(2)}, u32[]{:S(2)}) collective-permute-start(f32[16,4,128]{2,1,0:T(4,128)S(1)} %multiply_add_fusion.6), channel_id=1, source_target_pairs={{0,4},{1,5},{2,6},{3,7},{8,12},{9,13},{10,14},{11,15},{16,20},{17,... | collective-permute-start | bytes 98312 | tf_op jit(solution)/shard_map/ppermute | solution.py:1263
  71.5 2.8 ssm_context.1
  75.0 4.0 %collective-permute-start.20 = (bf16[256,256]{1,0:T(8,128)(2,1)}, bf16[256,256]{1,0:T(8,128)(2,1)}, u32[]{:S(2)}, u32[]{:S(2)}) collective-permute-start(bf16[256,256]{1,0:T(8,128)(2,1)} %get-tuple-element.229), channel_id=1, source_target_pairs={{0,2},{1,3},{2,4},{3,5},{4,6},{5,7},{8,10},{9,11},{10,12},{11,13},... | collective-permute-start | bytes 393224 | tf_op jit(solution)/shard_map/ppermute | solution.py:1282
  81.2 1.5 place_weight.3
  82.8 2.9 collective-permute-done.20
  87.4 1.6 collective-permute-start.23
  89.1 1.5 collective-permute-done.24.c2
  90.6 2.3 collective-permute-start.25
  94.0 5.3 %collective-permute-done.27.b_ref = bf16[2,64,1024]{2,1,0:T(8,128)(2,1)S(1)} collective-permute-done((bf16[2,64,1024]{2,1,0:T(8,128)(2,1)S(1)}, bf16[2,64,1024]{2,1,0:T(8,128)(2,1)S(1)}, u32[]{:S(2)}, u32[]{:S(2)}) %collective-permute-start.27) | collective-permute-done | bytes 262176 | tf_op jit(solution)/shard_map/ppermute | solution.py:26
  99.2 1.7 collective-permute-start.29
  102.6 1.8 convolution_convert_fusion.q0.q1.k0.k1.v0.v1
  105.4 5.0 %attend.1.x_ref.att_ref = bf16[1024,256]{1,0:T(8,128)(2,1)S(1)} custom-call(s32[1]{0:T(128)} %bitcast.3.late.half_ref, bf16[1024,768]{1,0:T(8,128)(2,1)S(1)} %convolution_convert_fusion.q0.q1.k0.k1.v0.v1, bf16[1024,768]{1,0:T(8,128)(2,1)S(1)} %convolution_convert_fusion.q0.q1.k0.k1.v0.v1, bf16[1024,768]{1,0:T(8,128)(2,1)S(1)} %convolution_convert_fusion.q0.q1.k0.k1.v0.v1, ...), custom_call_target="tpu_custom_call" | custom-call | tf_op jit(solution)/shard_map/attend/pallas_call | solution.py:778
  110.5 1.9 collective-permute-done.31.w3
  113.8 3.2 collective-permute-start.35
  120.3 8.5 %collective-permute-done.35.refs_1_ = bf16[4,64,1024]{2,1,0:T(8,128)(2,1)S(1)} collective-permute-done((bf16[4,64,1024]{2,1,0:T(8,128)(2,1)S(1)}, bf16[4,64,1024]{2,1,0:T(8,128)(2,1)S(1)}, u32[]{:S(2)}, u32[]{:S(2)}) %collective-permute-start.35) | collective-permute-done | bytes 524320 | tf_op jit(solution)/shard_map/ppermute | solution.py:26
  129.7 3.3 %collective-permute-done.34.far = bf16[256,1024]{1,0:T(8,128)(2,1)S(1)} collective-permute-done((bf16[256,1024]{1,0:T(8,128)(2,1)S(1)}, bf16[256,1024]{1,0:T(8,128)(2,1)S(1)}, u32[]{:S(2)}, u32[]{:S(2)}) %collective-permute-start.34) | collective-permute-done | bytes 524320 | tf_op jit(solution)/shard_map/ppermute | solution.py:26
  134.6 1.3 collective-permute-start.37
  135.9 10.2 %collective-permute-done.38.m2.x2 = bf16[256,1024]{1,0:T(8,128)(2,1)S(1)} collective-permute-done((bf16[256,1024]{1,0:T(8,128)(2,1)S(1)}, bf16[256,1024]{1,0:T(8,128)(2,1)S(1)}, u32[]{:S(2)}, u32[]{:S(2)}) %collective-permute-start.38) | collective-permute-done | bytes 524320 | tf_op jit(solution)/shard_map/ppermute | solution.py:26
  146.2 1.7 collective-permute-start.39
  150.9 11.6 %feed_forward.1 = (bf16[1024,1024]{1,0:T(8,128)(2,1)S(1)}, bf16[1024,1024]{1,0:T(8,128)(2,1)S(1)}, f32[256,1024]{1,0:T(8,128)S(1)}, bf16[256,1024]{1,0:T(8,128)(...) custom-call(bf16[256,1024]{1,0:T(8,128)(2,1)S(1)} %get-tuple-element.258.m0.x0, ...), custom_call_target="tpu_custom_call" | custom-call | tf_op jit(solution)/shard_map/feed_forward/pallas_call | solution.py:907
  162.9 3.2 down_grad.1
  168.0 3.5 %up_grad.1 = bf16[1024,1024]{1,0:T(8,128)(2,1)S(1)} custom-call(bf16[256,1024]{1,0:T(8,128)(2,1)S(1)} %get-tuple-element.258.m0.x0, bf16[256,1024]{1,0:T(8,128)(2,1)S(1)} %collective-permute-done.37.m1.x1, bf16[256,1024]{1,0:T(8,128)(2,1)S(1)} %collective-permute-done.38.m2.x2, bf16[256,1024]{1,0:T(8,128)(2,1)S(1)} %collective-permute-done.39.m3.x3, ...), custom_call_target="tpu_custom_call" | custom-call | tf_op jit(solution)/shard_map/up_grad/pallas_call | solution.py:951
  172.4 2.9 down_dot.1
  177.1 2.6 collective-permute-done.46.came_ref
  184.4 1.5 collective-permute-start.51
  185.9 8.9 %collective-permute-done.52.h2 = bf16[256,1024]{1,0:T(8,128)(2,1)S(1)} collective-permute-done((bf16[256,1024]{1,0:T(8,128)(2,1)S(1)}, bf16[256,1024]{1,0:T(8,128)(2,1)S(1)}, u32[]{:S(2)}, u32[]{:S(2)}) %collective-permute-start.52) | collective-permute-done | bytes 524320 | tf_op jit(solution)/shard_map/ppermute | solution.py:26
  194.9 1.8 collective-permute-start.53
  198.1 1.3 collective-permute-start.55
  204.4 7.2 %attend_back.1 = (bf16[1024,768]{1,0:T(8,128)(2,1)S(1)}, bf16[256,512]{1,0:T(8,128)(2,1)S(1)}) custom-call(s32[1]{0:T(128)} %bitcast.3.late.half_ref, bf16[1024,768]{1,0:T(8,128)(2,1)S(1)} %convolution_convert_fusion.q0.q1.k0.k1.v0.v1, bf16[1024,768]{1,0:T(8,128)(2,1)S(1)} %convolution_convert_fusion.q0.q1.k0.k1.v0.v1, ...), custom_call_target="tpu_custom_call" | custom-call | tf_op jit(solution)/shard_map/attend_back/pallas_call | solution.py:798
  212.8 1.3 context_grad.1
  216.4 5.1 %attn_grad.1 = bf16[1024,1024]{1,0:T(8,128)(2,1)S(1)} custom-call(s32[2]{0:T(128)S(1)} %copy-done.37, bf16[1024,1024]{1,0:T(8,128)(2,1)S(1)} %copy-done.15, bf16[1024,768]{1,0:T(8,128)(2,1)S(1)} %get-tuple-element.306.dq_ref, bf16[256,1024]{1,0:T(8,128)(2,1)S(1)} %get-tuple-element.307.ctx_ref, bf16[256,512]{1,0:T(8,128)(2,1)S(1)} %get-tuple-element.300.d_ref.dctx_ref, ...), custom_call_target="tpu_custom_call" | custom-call | tf_op jit(solution)/shard_map/attn_grad/pallas_call | solution.py:278
  237.5 3.1 collective-permute-start.72
  242.0 3.5 %first_context.1 = (f32[16,8,128]{2,1,0:T(8,128)}, f32[16,8,128]{2,1,0:T(8,128)}, f32[16,8,128]{2,1,0:T(8,128)}) custom-call(f32[128,8,128]{2,1,0:T(8,128)} %copy-done.16, f32[16,8,128]{2,1,0:T(8,128)} %copy-done.12, f32[16,8,128]{2,1,0:T(8,128)} %copy-done.24, f32[16,8,128]{2,1,0:T(8,128)} %copy-done.36), custom_call_target="tpu_custom_call" | custom-call | tf_op jit(solution)/shard_map/first_context/pallas_call | solution.py:597
  245.5 1.4 collective-permute-start.43
  254.4 1.5 stay_sum.4
  257.3 2.0 collective-permute-start.74
  261.0 10.0 %ssm_back.1 = (f32[256,8,128]{2,1,0:T(8,128)S(1)}, f32[16,8,128]{2,1,0:T(8,128)S(1)}, f32[16,8,128]{2,1,0:T(8,128)S(1)}, f32[16,8,128]{2,1,0:T(8,128)S(1)}, f32[16,8,128]{2,1,0:T(8,128)S(1)}) custom-call(f32[256,8,128]{2,1,0:T(8,128)S(1)} %get-tuple-element.209.u_ref, f32[128,8,128]{2,1,0:T(8,128)S(1)} %copy-done.35, f32[16,8,128]{2,1,0:T(8,128)S(1)} %copy-done.13, ...), custom_call_target="tpu_custom_call" | custom-call | tf_op jit(solution)/shard_map/ssm_back/pallas_call | solution.py:679
  271.1 3.8 %inputs_grad.1 = (f32[256,1024]{1,0:T(8,128)S(1)}, bf16[256,1024]{1,0:T(8,128)(2,1)S(1)}, f32[256,1024]{1,0:T(8,128)S(1)}, bf16[256,1024]{1,0:T(8,128)(2,1)S(1)}, f32[1,1024]{1,0:T(1,128)S(1)}) custom-call(s32[2]{0:T(128)S(1)} %copy-done.37, bf16[1024,768]{1,0:T(8,128)(2,1)S(1)} %copy-done.7, bf16[1024,768]{1,0:T(8,128)(2,1)S(1)} %copy-done.3, ...), custom_call_target="tpu_custom_call" | custom-call | tf_op jit(solution)/shard_map/inputs_grad/pallas_call | solution.py:109
  276.5 3.2 collective-permute-start.78
  286.6 8.0 %collective-permute-done.79.far = bf16[256,1024]{1,0:T(8,128)(2,1)S(1)} collective-permute-done((bf16[256,1024]{1,0:T(8,128)(2,1)S(1)}, bf16[256,1024]{1,0:T(8,128)(2,1)S(1)}, u32[]{:S(2)}, u32[]{:S(2)}) %collective-permute-start.79) | collective-permute-done | bytes 524320 | tf_op jit(solution)/shard_map/ppermute | solution.py:26
  294.5 1.3 tokens_grad.1
  295.9 1.5 collective-permute-done.86.b_ref
  301.4 3.7 %collective-permute-done.83 = f32[176,128]{1,0:T(8,128)S(1)} collective-permute-done((f32[176,128]{1,0:T(8,128)S(1)}, f32[176,128]{1,0:T(8,128)S(1)}, u32[]{:S(2)}, u32[]{:S(2)}) %collective-permute-start.83) | collective-permute-done | bytes 90144 | tf_op jit(solution)/shard_map/ppermute | solution.py:26
  306.0 1.9 collective-permute-start.88
  308.7 2.0 final_down.1
  311.4 3.2 collective-permute-start.85
  314.7 2.1 final_up.1
  318.5 1.7 collective-permute-done.92.p2
  320.2 1.7 collective-permute-start.93
  322.0 2.0 final_attn.1
  (379 shorter events, 107.6 us)
Async XLA Ops:
  10.6 19.6 %collective-permute-start.6 = (bf16[256,1024]{1,0:T(8,128)(2,1)S(1)}, bf16[256,1024]{1,0:T(8,128)(2,1)S(1)}, u32[]{:S(2)}, u32[]{:S(2)}) collective-permute-start(bf16[256,1024]{1,0:T(8,128)(2,1)S(1)} %bitcast.70), channel_id=1, source_target_pairs={{0,1},{1,0},{2,3},{3,2},{4,5},{5,4},{6,7},{7,6},{8,9},{9,8},{10,11... | collective-permute-start | bytes 1572872 | tf_op jit(solution)/shard_map/ppermute | solution.py:26
  14.7 15.3 %collective-permute-start.4 = (bf16[2,64,1024]{2,1,0:T(8,128)(2,1)S(1)}, bf16[2,64,1024]{2,1,0:T(8,128)(2,1)S(1)}, u32[]{:S(2)}, u32[]{:S(2)}) collective-permute-start(bf16[2,64,1024]{2,1,0:T(8,128)(2,1)S(1)} %append.12.a_ref), channel_id=1, source_target_pairs={{0,4},{1,5},{2,6},{3,7},{4,0},{5,1},{6,2},{7,3},{8,12},{9,13},{10,... | collective-permute-start | bytes 786440 | tf_op jit(solution)/shard_map/ppermute | solution.py:26
  14.9 18.6 %collective-permute-start.5 = (bf16[256,1024]{1,0:T(8,128)(2,1)S(1)}, bf16[256,1024]{1,0:T(8,128)(2,1)S(1)}, u32[]{:S(2)}, u32[]{:S(2)}) collective-permute-start(bf16[256,1024]{1,0:T(8,128)(2,1)S(1)} %bitcast.71), channel_id=1, source_target_pairs={{0,8},{8,0},{16,24},{24,16},{1,9},{9,1},{17,25},{25,17},{2,10},{10... | collective-permute-start | bytes 1572872 | tf_op jit(solution)/shard_map/ppermute | solution.py:26
  17.4 12.7 %collective-permute-start.8 = (bf16[1,64,1024]{2,1,0:T(8,128)(2,1)}, bf16[1,64,1024]{2,1,0:T(8,128)(2,1)S(1)}, u32[]{:S(2)}, u32[]{:S(2)}) collective-permute-start(bf16[1,64,1024]{2,1,0:T(8,128)(2,1)} %bitcast.101), channel_id=1, source_target_pairs={{0,1},{1,0},{2,3},{3,2},{4,5},{5,4},{6,7},{7,6},{8,9},{9,8},{10,11... | collective-permute-start | bytes 393224 | tf_op jit(solution)/shard_map/ppermute | solution.py:26
  30.1 12.4 %collective-permute-start.9 = (bf16[4,64,1024]{2,1,0:T(8,128)(2,1)S(1)}, bf16[4,64,1024]{2,1,0:T(8,128)(2,1)}, u32[]{:S(2)}, u32[]{:S(2)}) collective-permute-start(bf16[4,64,1024]{2,1,0:T(8,128)(2,1)S(1)} %append.13.refs_0_), channel_id=1, source_target_pairs={{0,2},{1,3},{2,0},{3,1},{4,6},{5,7},{6,4},{7,5},{8,10},{9,11},{10,... | collective-permute-start | bytes 1572872 | tf_op jit(solution)/shard_map/ppermute | solution.py:26
  32.1 16.7 %collective-permute-start.10 = (bf16[4,64,1024]{2,1,0:T(8,128)(2,1)S(1)}, bf16[4,64,1024]{2,1,0:T(8,128)(2,1)}, u32[]{:S(2)}, u32[]{:S(2)}) collective-permute-start(bf16[4,64,1024]{2,1,0:T(8,128)(2,1)S(1)} %append.13.refs_0_), channel_id=1, source_target_pairs={{0,16},{8,24},{16,0},{24,8},{1,17},{9,25},{17,1},{25,9},{2,18},{10... | collective-permute-start | bytes 1572872 | tf_op jit(solution)/shard_map/ppermute | solution.py:26
  42.5 18.6 %collective-permute-start.11 = (bf16[4,64,1024]{2,1,0:T(8,128)(2,1)}, bf16[4,64,1024]{2,1,0:T(8,128)(2,1)}, u32[]{:S(2)}, u32[]{:S(2)}) collective-permute-start(bf16[4,64,1024]{2,1,0:T(8,128)(2,1)} %collective-permute-done.9.refs_1_), channel_id=1, source_target_pairs={{0,16},{8,24},{16,0},{24,8},{1,17},{9,25},{17,1},{25,9},{2,18},{10... | collective-permute-start | bytes 1572872 | tf_op jit(solution)/shard_map/ppermute | solution.py:26
  44.0 14.9 %collective-permute-start.12 = (bf16[2,64,1024]{2,1,0:T(8,128)(2,1)}, bf16[2,64,1024]{2,1,0:T(8,128)(2,1)}, u32[]{:S(2)}, u32[]{:S(2)}) collective-permute-start(bf16[2,64,1024]{2,1,0:T(8,128)(2,1)} %append.14.a_ref), channel_id=1, source_target_pairs={{0,4},{1,5},{2,6},{3,7},{4,0},{5,1},{6,2},{7,3},{8,12},{9,13},{10,... | collective-permute-start | bytes 786440 | tf_op jit(solution)/shard_map/ppermute | solution.py:26
  54.2 13.6 %collective-permute-start.14 = (f32[16,256]{1,0:T(8,128)S(1)}, f32[16,256]{1,0:T(8,128)S(1)}, u32[]{:S(2)}, u32[]{:S(2)}) collective-permute-start(f32[16,256]{1,0:T(8,128)S(1)} %get-tuple-element.218), channel_id=1, source_target_pairs={{0,8},{8,0},{16,24},{24,16},{1,9},{9,1},{17,25},{25,17},{2,10},{10... | collective-permute-start | bytes 49160 | tf_op jit(solution)/shard_map/ppermute | solution.py:26
  56.4 11.3 %collective-permute-start.15 = (f32[16,256]{1,0:T(8,128)S(1)}, f32[16,256]{1,0:T(8,128)S(1)}, u32[]{:S(2)}, u32[]{:S(2)}) collective-permute-start(f32[16,256]{1,0:T(8,128)S(1)} %get-tuple-element.220), channel_id=1, source_target_pairs={{0,8},{8,0},{16,24},{24,16},{1,9},{9,1},{17,25},{25,17},{2,10},{10... | collective-permute-start | bytes 49160 | tf_op jit(solution)/shard_map/ppermute | solution.py:26
  56.5 11.3 %collective-permute-start.16 = (f32[16,256]{1,0:T(8,128)S(1)}, f32[16,256]{1,0:T(8,128)S(1)}, u32[]{:S(2)}, u32[]{:S(2)}) collective-permute-start(f32[16,256]{1,0:T(8,128)S(1)} %get-tuple-element.221), channel_id=1, source_target_pairs={{0,1},{1,0},{2,3},{3,2},{4,5},{5,4},{6,7},{7,6},{8,9},{9,8},{10,11... | collective-permute-start | bytes 49160 | tf_op jit(solution)/shard_map/ppermute | solution.py:26
  58.9 8.9 %collective-permute-start.17 = (f32[16,256]{1,0:T(8,128)S(1)}, f32[16,256]{1,0:T(8,128)S(1)}, u32[]{:S(2)}, u32[]{:S(2)}) collective-permute-start(f32[16,256]{1,0:T(8,128)S(1)} %get-tuple-element.222), channel_id=1, source_target_pairs={{0,9},{1,8},{2,11},{3,10},{4,13},{5,12},{6,15},{7,14},{8,1},{9,0},... | collective-permute-start | bytes 49160 | tf_op jit(solution)/shard_map/ppermute | solution.py:36
  62.0 8.8 %collective-permute-start.19 = (f32[16,4,128]{2,1,0:T(4,128)S(1)}, f32[16,4,128]{2,1,0:T(4,128)S(1)}, u32[]{:S(2)}, u32[]{:S(2)}) collective-permute-start(f32[16,4,128]{2,1,0:T(4,128)S(1)} %multiply_add_fusion.6), channel_id=1, source_target_pairs={{0,4},{1,5},{2,6},{3,7},{8,12},{9,13},{10,14},{11,15},{16,20},{17,... | collective-permute-start | bytes 98312 | tf_op jit(solution)/shard_map/ppermute | solution.py:1263
  68.7 10.5 %collective-permute-start.22 = (bf16[1,64,1024]{2,1,0:T(8,128)(2,1)}, bf16[1,64,1024]{2,1,0:T(8,128)(2,1)}, u32[]{:S(2)}, u32[]{:S(2)}) collective-permute-start(bf16[1,64,1024]{2,1,0:T(8,128)(2,1)} %bitcast.100), channel_id=1, source_target_pairs={{0,1},{1,0},{2,3},{3,2},{4,5},{5,4},{6,7},{7,6},{8,9},{9,8},{10,11... | collective-permute-start | bytes 393224 | tf_op jit(solution)/shard_map/ppermute | solution.py:26
  71.4 14.9 %collective-permute-start.21 = (bf16[4,64,1024]{2,1,0:T(8,128)(2,1)S(1)}, bf16[4,64,1024]{2,1,0:T(8,128)(2,1)}, u32[]{:S(2)}, u32[]{:S(2)}) collective-permute-start(bf16[4,64,1024]{2,1,0:T(8,128)(2,1)S(1)} %append.15.refs_0_), channel_id=1, source_target_pairs={{0,2},{1,3},{2,0},{3,1},{4,6},{5,7},{6,4},{7,5},{8,10},{9,11},{10,... | collective-permute-start | bytes 1572872 | tf_op jit(solution)/shard_map/ppermute | solution.py:26
  75.0 10.7 %collective-permute-start.20 = (bf16[256,256]{1,0:T(8,128)(2,1)}, bf16[256,256]{1,0:T(8,128)(2,1)}, u32[]{:S(2)}, u32[]{:S(2)}) collective-permute-start(bf16[256,256]{1,0:T(8,128)(2,1)} %get-tuple-element.229), channel_id=1, source_target_pairs={{0,2},{1,3},{2,4},{3,5},{4,6},{5,7},{8,10},{9,11},{10,12},{11,13},... | collective-permute-start | bytes 393224 | tf_op jit(solution)/shard_map/ppermute | solution.py:1282
  79.0 13.9 %collective-permute-start.13 = (bf16[4,64,1024]{2,1,0:T(8,128)(2,1)S(1)}, bf16[4,64,1024]{2,1,0:T(8,128)(2,1)S(1)}, u32[]{:S(2)}, u32[]{:S(2)}) collective-permute-start(bf16[4,64,1024]{2,1,0:T(8,128)(2,1)S(1)} %append.15.refs_0_), channel_id=1, source_target_pairs={{0,16},{8,24},{16,0},{24,8},{1,17},{9,25},{17,1},{25,9},{2,18},{10... | collective-permute-start | bytes 1572872 | tf_op jit(solution)/shard_map/ppermute | solution.py:26
  85.7 13.6 %collective-permute-start.27 = (bf16[2,64,1024]{2,1,0:T(8,128)(2,1)S(1)}, bf16[2,64,1024]{2,1,0:T(8,128)(2,1)S(1)}, u32[]{:S(2)}, u32[]{:S(2)}) collective-permute-start(bf16[2,64,1024]{2,1,0:T(8,128)(2,1)S(1)} %append.16.a_ref), channel_id=1, source_target_pairs={{0,4},{1,5},{2,6},{3,7},{4,0},{5,1},{6,2},{7,3},{8,12},{9,13},{10,... | collective-permute-start | bytes 786440 | tf_op jit(solution)/shard_map/ppermute | solution.py:26
  87.4 13.5 %collective-permute-start.23 = (bf16[256,256]{1,0:T(8,128)(2,1)S(1)}, bf16[256,256]{1,0:T(8,128)(2,1)S(1)}, u32[]{:S(2)}, u32[]{:S(2)}) collective-permute-start(bf16[256,256]{1,0:T(8,128)(2,1)S(1)} %broadcast_select_fusion.c0), channel_id=1, source_target_pairs={{0,8},{8,0},{16,24},{24,16},{1,9},{9,1},{17,25},{25,17},{2,10},{10... | collective-permute-start | bytes 393224 | tf_op jit(solution)/shard_map/ppermute | solution.py:26
  90.6 10.7 %collective-permute-start.25 = (bf16[256,256]{1,0:T(8,128)(2,1)S(1)}, bf16[256,256]{1,0:T(8,128)(2,1)S(1)}, u32[]{:S(2)}, u32[]{:S(2)}) collective-permute-start(bf16[256,256]{1,0:T(8,128)(2,1)S(1)} %collective-permute-done.24.c2), channel_id=1, source_target_pairs={{0,8},{8,0},{16,24},{24,16},{1,9},{9,1},{17,25},{25,17},{2,10},{10... | collective-permute-start | bytes 393224 | tf_op jit(solution)/shard_map/ppermute | solution.py:26
  92.9 17.5 %collective-permute-start.28 = (bf16[4,64,1024]{2,1,0:T(8,128)(2,1)}, bf16[4,64,1024]{2,1,0:T(8,128)(2,1)S(1)}, u32[]{:S(2)}, u32[]{:S(2)}) collective-permute-start(bf16[4,64,1024]{2,1,0:T(8,128)(2,1)} %collective-permute-done.21.refs_1_), channel_id=1, source_target_pairs={{0,16},{8,24},{16,0},{24,8},{1,17},{9,25},{17,1},{25,9},{2,18},{10... | collective-permute-start | bytes 1572872 | tf_op jit(solution)/shard_map/ppermute | solution.py:26
  93.1 17.3 %collective-permute-start.26 = (bf16[256,1024]{1,0:T(8,128)(2,1)S(1)}, bf16[256,1024]{1,0:T(8,128)(2,1)S(1)}, u32[]{:S(2)}, u32[]{:S(2)}) collective-permute-start(bf16[256,1024]{1,0:T(8,128)(2,1)S(1)} %bitcast.76), channel_id=1, source_target_pairs={{0,1},{1,0},{2,3},{3,2},{4,5},{5,4},{6,7},{7,6},{8,9},{9,8},{10,11... | collective-permute-start | bytes 1572872 | tf_op jit(solution)/shard_map/ppermute | solution.py:26
  99.2 11.2 %collective-permute-start.29 = (bf16[256,256]{1,0:T(8,128)(2,1)S(1)}, bf16[256,256]{1,0:T(8,128)(2,1)S(1)}, u32[]{:S(2)}, u32[]{:S(2)}) collective-permute-start(bf16[256,256]{1,0:T(8,128)(2,1)S(1)} %get-tuple-element.246), channel_id=1, source_target_pairs={{0,8},{8,0},{16,24},{24,16},{1,9},{9,1},{17,25},{25,17},{2,10},{10... | collective-permute-start | bytes 393224 | tf_op jit(solution)/shard_map/ppermute | solution.py:26
  100.9 9.5 %collective-permute-start.30 = (bf16[256,256]{1,0:T(8,128)(2,1)S(1)}, bf16[256,256]{1,0:T(8,128)(2,1)S(1)}, u32[]{:S(2)}, u32[]{:S(2)}) collective-permute-start(bf16[256,256]{1,0:T(8,128)(2,1)S(1)} %get-tuple-element.247), channel_id=1, source_target_pairs={{0,1},{1,0},{2,3},{3,2},{4,5},{5,4},{6,7},{7,6},{8,9},{9,8},{10,11... | collective-permute-start | bytes 393224 | tf_op jit(solution)/shard_map/ppermute | solution.py:26
  101.3 11.1 %collective-permute-start.31 = (bf16[256,256]{1,0:T(8,128)(2,1)S(1)}, bf16[256,256]{1,0:T(8,128)(2,1)S(1)}, u32[]{:S(2)}, u32[]{:S(2)}) collective-permute-start(bf16[256,256]{1,0:T(8,128)(2,1)S(1)} %get-tuple-element.248), channel_id=1, source_target_pairs={{0,9},{1,8},{2,11},{3,10},{4,13},{5,12},{6,15},{7,14},{8,1},{9,0},... | collective-permute-start | bytes 393224 | tf_op jit(solution)/shard_map/ppermute | solution.py:36
  113.8 15.0 %collective-permute-start.35 = (bf16[4,64,1024]{2,1,0:T(8,128)(2,1)S(1)}, bf16[4,64,1024]{2,1,0:T(8,128)(2,1)S(1)}, u32[]{:S(2)}, u32[]{:S(2)}) collective-permute-start(bf16[4,64,1024]{2,1,0:T(8,128)(2,1)S(1)} %append.17.refs_0_), channel_id=1, source_target_pairs={{0,2},{1,3},{2,0},{3,1},{4,6},{5,7},{6,4},{7,5},{8,10},{9,11},{10,... | collective-permute-start | bytes 1572872 | tf_op jit(solution)/shard_map/ppermute | solution.py:26
  117.0 12.7 %collective-permute-start.36 = (bf16[4,64,1024]{2,1,0:T(8,128)(2,1)S(1)}, bf16[4,64,1024]{2,1,0:T(8,128)(2,1)S(1)}, u32[]{:S(2)}, u32[]{:S(2)}) collective-permute-start(bf16[4,64,1024]{2,1,0:T(8,128)(2,1)S(1)} %append.17.refs_0_), channel_id=1, source_target_pairs={{0,16},{8,24},{16,0},{24,8},{1,17},{9,25},{17,1},{25,9},{2,18},{10... | collective-permute-start | bytes 1572872 | tf_op jit(solution)/shard_map/ppermute | solution.py:26
  118.2 11.4 %collective-permute-start.32 = (bf16[256,1024]{1,0:T(8,128)(2,1)S(1)}, bf16[256,1024]{1,0:T(8,128)(2,1)S(1)}, u32[]{:S(2)}, u32[]{:S(2)}) collective-permute-start(bf16[256,1024]{1,0:T(8,128)(2,1)S(1)} %get-tuple-element.250), channel_id=1, source_target_pairs={{0,8},{8,0},{16,24},{24,16},{1,9},{9,1},{17,25},{25,17},{2,10},{10... | collective-permute-start | bytes 1572872 | tf_op jit(solution)/shard_map/ppermute | solution.py:26
  119.4 13.6 %collective-permute-start.34 = (bf16[256,1024]{1,0:T(8,128)(2,1)S(1)}, bf16[256,1024]{1,0:T(8,128)(2,1)S(1)}, u32[]{:S(2)}, u32[]{:S(2)}) collective-permute-start(bf16[256,1024]{1,0:T(8,128)(2,1)S(1)} %far_sum.5), channel_id=1, source_target_pairs={{0,1},{1,0},{2,3},{3,2},{4,5},{5,4},{6,7},{7,6},{8,9},{9,8},{10,11... | collective-permute-start | bytes 1572872 | tf_op jit(solution)/shard_map/ppermute | solution.py:26
  133.4 12.7 %collective-permute-start.38 = (bf16[256,1024]{1,0:T(8,128)(2,1)S(1)}, bf16[256,1024]{1,0:T(8,128)(2,1)S(1)}, u32[]{:S(2)}, u32[]{:S(2)}) collective-permute-start(bf16[256,1024]{1,0:T(8,128)(2,1)S(1)} %get-tuple-element.258.m0.x0), channel_id=1, source_target_pairs={{0,1},{1,0},{2,3},{3,2},{4,5},{5,4},{6,7},{7,6},{8,9},{9,8},{10,11... | collective-permute-start | bytes 1572872 | tf_op jit(solution)/shard_map/ppermute | solution.py:26
  134.4 15.2 %collective-permute-start.42 = (bf16[4,64,1024]{2,1,0:T(8,128)(2,1)S(1)}, bf16[4,64,1024]{2,1,0:T(8,128)(2,1)S(1)}, u32[]{:S(2)}, u32[]{:S(2)}) collective-permute-start(bf16[4,64,1024]{2,1,0:T(8,128)(2,1)S(1)} %collective-permute-done.35.refs_1_), channel_id=1, source_target_pairs={{0,16},{8,24},{16,0},{24,8},{1,17},{9,25},{17,1},{25,9},{2,18},{10... | collective-permute-start | bytes 1572872 | tf_op jit(solution)/shard_map/ppermute | solution.py:26
  134.6 15.7 %collective-permute-start.37 = (bf16[256,1024]{1,0:T(8,128)(2,1)S(1)}, bf16[256,1024]{1,0:T(8,128)(2,1)S(1)}, u32[]{:S(2)}, u32[]{:S(2)}) collective-permute-start(bf16[256,1024]{1,0:T(8,128)(2,1)S(1)} %get-tuple-element.258.m0.x0), channel_id=1, source_target_pairs={{0,8},{8,0},{16,24},{24,16},{1,9},{9,1},{17,25},{25,17},{2,10},{10... | collective-permute-start | bytes 1572872 | tf_op jit(solution)/shard_map/ppermute | solution.py:26
  166.3 13.4 %collective-permute-start.46 = (bf16[4,64,1024]{2,1,0:T(8,128)(2,1)S(1)}, bf16[4,64,1024]{2,1,0:T(8,128)(2,1)S(1)}, u32[]{:S(2)}, u32[]{:S(2)}) collective-permute-start(bf16[4,64,1024]{2,1,0:T(8,128)(2,1)S(1)} %get-tuple-element.265), channel_id=1, source_target_pairs={{0,16},{8,24},{16,0},{24,8},{1,17},{9,25},{17,1},{25,9},{2,18},{10... | collective-permute-start | bytes 1572872 | tf_op jit(solution)/shard_map/ppermute | solution.py:26
  166.6 13.3 %collective-permute-start.49 = (bf16[256,1024]{1,0:T(8,128)(2,1)S(1)}, bf16[256,1024]{1,0:T(8,128)(2,1)S(1)}, u32[]{:S(2)}, u32[]{:S(2)}) collective-permute-start(bf16[256,1024]{1,0:T(8,128)(2,1)S(1)} %get-tuple-element.281), channel_id=1, source_target_pairs={{0,8},{8,0},{16,24},{24,16},{1,9},{9,1},{17,25},{25,17},{2,10},{10... | collective-permute-start | bytes 1572872 | tf_op jit(solution)/shard_map/ppermute | solution.py:26
  167.1 13.5 %collective-permute-start.50 = (bf16[256,1024]{1,0:T(8,128)(2,1)S(1)}, bf16[256,1024]{1,0:T(8,128)(2,1)S(1)}, u32[]{:S(2)}, u32[]{:S(2)}) collective-permute-start(bf16[256,1024]{1,0:T(8,128)(2,1)S(1)} %far_sum.6), channel_id=1, source_target_pairs={{0,1},{1,0},{2,3},{3,2},{4,5},{5,4},{6,7},{7,6},{8,9},{9,8},{10,11... | collective-permute-start | bytes 1572872 | tf_op jit(solution)/shard_map/ppermute | solution.py:26
  182.3 12.6 %collective-permute-start.52 = (bf16[256,1024]{1,0:T(8,128)(2,1)S(1)}, bf16[256,1024]{1,0:T(8,128)(2,1)S(1)}, u32[]{:S(2)}, u32[]{:S(2)}) collective-permute-start(bf16[256,1024]{1,0:T(8,128)(2,1)S(1)} %get-tuple-element.288.h0), channel_id=1, source_target_pairs={{0,1},{1,0},{2,3},{3,2},{4,5},{5,4},{6,7},{7,6},{8,9},{9,8},{10,11... | collective-permute-start | bytes 1572872 | tf_op jit(solution)/shard_map/ppermute | solution.py:26
  183.2 14.7 %collective-permute-start.48 = (bf16[4,64,1024]{2,1,0:T(8,128)(2,1)S(1)}, bf16[4,64,1024]{2,1,0:T(8,128)(2,1)S(1)}, u32[]{:S(2)}, u32[]{:S(2)}) collective-permute-start(bf16[4,64,1024]{2,1,0:T(8,128)(2,1)S(1)} %leave_sum.3), channel_id=1, source_target_pairs={{0,2},{1,3},{2,0},{3,1},{4,6},{5,7},{6,4},{7,5},{8,10},{9,11},{10,... | collective-permute-start | bytes 1572872 | tf_op jit(solution)/shard_map/ppermute | solution.py:26
  183.5 14.4 %collective-permute-start.45 = (bf16[4,64,1024]{2,1,0:T(8,128)(2,1)S(1)}, bf16[4,64,1024]{2,1,0:T(8,128)(2,1)S(1)}, u32[]{:S(2)}, u32[]{:S(2)}) collective-permute-start(bf16[4,64,1024]{2,1,0:T(8,128)(2,1)S(1)} %get-tuple-element.273), channel_id=1, source_target_pairs={{0,16},{8,24},{16,0},{24,8},{1,17},{9,25},{17,1},{25,9},{2,18},{10... | collective-permute-start | bytes 1572872 | tf_op jit(solution)/shard_map/ppermute | solution.py:26
  184.4 15.0 %collective-permute-start.51 = (bf16[256,1024]{1,0:T(8,128)(2,1)S(1)}, bf16[256,1024]{1,0:T(8,128)(2,1)S(1)}, u32[]{:S(2)}, u32[]{:S(2)}) collective-permute-start(bf16[256,1024]{1,0:T(8,128)(2,1)S(1)} %get-tuple-element.288.h0), channel_id=1, source_target_pairs={{0,8},{8,0},{16,24},{24,16},{1,9},{9,1},{17,25},{25,17},{2,10},{10... | collective-permute-start | bytes 1572872 | tf_op jit(solution)/shard_map/ppermute | solution.py:26
  196.6 15.0 %collective-permute-start.54 = (bf16[4,64,1024]{2,1,0:T(8,128)(2,1)S(1)}, bf16[4,64,1024]{2,1,0:T(8,128)(2,1)S(1)}, u32[]{:S(2)}, u32[]{:S(2)}) collective-permute-start(bf16[4,64,1024]{2,1,0:T(8,128)(2,1)S(1)} %get-tuple-element.267), channel_id=1, source_target_pairs={{0,16},{8,24},{16,0},{24,8},{1,17},{9,25},{17,1},{25,9},{2,18},{10... | collective-permute-start | bytes 1572872 | tf_op jit(solution)/shard_map/ppermute | solution.py:26
  198.1 14.6 %collective-permute-start.55 = (bf16[2,64,1024]{2,1,0:T(8,128)(2,1)S(1)}, bf16[2,64,1024]{2,1,0:T(8,128)(2,1)S(1)}, u32[]{:S(2)}, u32[]{:S(2)}) collective-permute-start(bf16[2,64,1024]{2,1,0:T(8,128)(2,1)S(1)} %get-tuple-element.286), channel_id=1, source_target_pairs={{0,4},{1,5},{2,6},{3,7},{4,0},{5,1},{6,2},{7,3},{8,12},{9,13},{10,... | collective-permute-start | bytes 786440 | tf_op jit(solution)/shard_map/ppermute | solution.py:26
  202.1 10.7 %collective-permute-start.56 = (bf16[256,256]{1,0:T(8,128)(2,1)S(1)}, bf16[256,256]{1,0:T(8,128)(2,1)S(1)}, u32[]{:S(2)}, u32[]{:S(2)}) collective-permute-start(bf16[256,256]{1,0:T(8,128)(2,1)S(1)} %get-tuple-element.291), channel_id=1, source_target_pairs={{0,8},{8,0},{16,24},{24,16},{1,9},{9,1},{17,25},{25,17},{2,10},{10... | collective-permute-start | bytes 393224 | tf_op jit(solution)/shard_map/ppermute | solution.py:26
  202.7 10.1 %collective-permute-start.57 = (bf16[256,256]{1,0:T(8,128)(2,1)S(1)}, bf16[256,256]{1,0:T(8,128)(2,1)S(1)}, u32[]{:S(2)}, u32[]{:S(2)}) collective-permute-start(bf16[256,256]{1,0:T(8,128)(2,1)S(1)} %get-tuple-element.292), channel_id=1, source_target_pairs={{0,1},{1,0},{2,3},{3,2},{4,5},{5,4},{6,7},{7,6},{8,9},{9,8},{10,11... | collective-permute-start | bytes 393224 | tf_op jit(solution)/shard_map/ppermute | solution.py:26
  203.4 9.4 %collective-permute-start.58 = (bf16[256,256]{1,0:T(8,128)(2,1)S(1)}, bf16[256,256]{1,0:T(8,128)(2,1)S(1)}, u32[]{:S(2)}, u32[]{:S(2)}) collective-permute-start(bf16[256,256]{1,0:T(8,128)(2,1)S(1)} %get-tuple-element.293), channel_id=1, source_target_pairs={{0,9},{1,8},{2,11},{3,10},{4,13},{5,12},{6,15},{7,14},{8,1},{9,0},... | collective-permute-start | bytes 393224 | tf_op jit(solution)/shard_map/ppermute | solution.py:36
  222.5 24.4 %collective-permute-start.69 = (bf16[4,64,1024]{2,1,0:T(8,128)(2,1)}, bf16[4,64,1024]{2,1,0:T(8,128)(2,1)}, u32[]{:S(2)}, u32[]{:S(2)}) collective-permute-start(bf16[4,64,1024]{2,1,0:T(8,128)(2,1)} %get-tuple-element.316), channel_id=1, source_target_pairs={{0,16},{8,24},{16,0},{24,8},{1,17},{9,25},{17,1},{25,9},{2,18},{10... | collective-permute-start | bytes 1572872 | tf_op jit(solution)/shard_map/ppermute | solution.py:26
  223.2 10.2 %collective-permute-start.63 = (bf16[256,256]{1,0:T(8,128)(2,1)S(1)}, bf16[256,256]{1,0:T(8,128)(2,1)S(1)}, u32[]{:S(2)}, u32[]{:S(2)}) collective-permute-start(bf16[256,256]{1,0:T(8,128)(2,1)S(1)} %context_sum.1.own), channel_id=1, source_target_pairs={{2,0},{3,1},{4,2},{5,3},{6,4},{7,5},{10,8},{11,9},{12,10},{13,11},... | collective-permute-start | bytes 393224 | tf_op jit(solution)/shard_map/ppermute | solution.py:1371
  230.9 18.2 %collective-permute-start.44 = (bf16[256,1024]{1,0:T(8,128)(2,1)}, bf16[256,1024]{1,0:T(8,128)(2,1)}, u32[]{:S(2)}, u32[]{:S(2)}) collective-permute-start(bf16[256,1024]{1,0:T(8,128)(2,1)} %get-tuple-element.272), channel_id=1, source_target_pairs={{0,8},{8,0},{16,24},{24,16},{1,9},{9,1},{17,25},{25,17},{2,10},{10... | collective-permute-start | bytes 1572872 | tf_op jit(solution)/shard_map/ppermute | solution.py:26
  230.9 9.7 %collective-permute-start.68 = (bf16[1,64,1024]{2,1,0:T(8,128)(2,1)S(1)}, bf16[1,64,1024]{2,1,0:T(8,128)(2,1)S(1)}, u32[]{:S(2)}, u32[]{:S(2)}) collective-permute-start(bf16[1,64,1024]{2,1,0:T(8,128)(2,1)S(1)} %get-tuple-element.299), channel_id=1, source_target_pairs={{0,1},{1,0},{2,3},{3,2},{4,5},{5,4},{6,7},{7,6},{8,9},{9,8},{10,11... | collective-permute-start | bytes 393224 | tf_op jit(solution)/shard_map/ppermute | solution.py:26
  236.2 9.3 %collective-permute-start.67 = (f32[16,4,128]{2,1,0:T(4,128)S(1)}, f32[16,4,128]{2,1,0:T(4,128)S(1)}, u32[]{:S(2)}, u32[]{:S(2)}) collective-permute-start(f32[16,4,128]{2,1,0:T(4,128)S(1)} %get-tuple-element.379), channel_id=1, source_target_pairs={{2,0},{3,1},{4,2},{5,3},{6,4},{7,5},{10,8},{11,9},{12,10},{13,11},... | collective-permute-start | bytes 98312 | tf_op jit(solution)/shard_map/ppermute | solution.py:1263
  237.5 16.8 %collective-permute-start.72 = (bf16[4,64,1024]{2,1,0:T(8,128)(2,1)}, bf16[4,64,1024]{2,1,0:T(8,128)(2,1)}, u32[]{:S(2)}, u32[]{:S(2)}) collective-permute-start(bf16[4,64,1024]{2,1,0:T(8,128)(2,1)} %leave_sum.4), channel_id=1, source_target_pairs={{0,2},{1,3},{2,0},{3,1},{4,6},{5,7},{6,4},{7,5},{8,10},{9,11},{10,... | collective-permute-start | bytes 1572872 | tf_op jit(solution)/shard_map/ppermute | solution.py:26
  241.2 13.1 %collective-permute-start.71 = (bf16[4,64,1024]{2,1,0:T(8,128)(2,1)}, bf16[4,64,1024]{2,1,0:T(8,128)(2,1)}, u32[]{:S(2)}, u32[]{:S(2)}) collective-permute-start(bf16[4,64,1024]{2,1,0:T(8,128)(2,1)} %get-tuple-element.325), channel_id=1, source_target_pairs={{0,16},{8,24},{16,0},{24,8},{1,17},{9,25},{17,1},{25,9},{2,18},{10... | collective-permute-start | bytes 1572872 | tf_op jit(solution)/shard_map/ppermute | solution.py:26
  245.5 15.4 %collective-permute-start.43 = (bf16[256,1024]{1,0:T(8,128)(2,1)}, bf16[256,1024]{1,0:T(8,128)(2,1)S(1)}, u32[]{:S(2)}, u32[]{:S(2)}) collective-permute-start(bf16[256,1024]{1,0:T(8,128)(2,1)} %copy-done.62), channel_id=1, source_target_pairs={{0,8},{8,0},{16,24},{24,16},{1,9},{9,1},{17,25},{25,17},{2,10},{10... | collective-permute-start | bytes 1572872 | tf_op jit(solution)/shard_map/ppermute | solution.py:26
  251.5 19.5 %collective-permute-start.62 = (bf16[256,1024]{1,0:T(8,128)(2,1)S(1)}, bf16[256,1024]{1,0:T(8,128)(2,1)S(1)}, u32[]{:S(2)}, u32[]{:S(2)}) collective-permute-start(bf16[256,1024]{1,0:T(8,128)(2,1)S(1)} %far_sum.8), channel_id=1, source_target_pairs={{0,1},{1,0},{2,3},{3,2},{4,5},{5,4},{6,7},{7,6},{8,9},{9,8},{10,11... | collective-permute-start | bytes 1572872 | tf_op jit(solution)/shard_map/ppermute | solution.py:26
  257.3 18.9 %collective-permute-start.74 = (bf16[4,64,1024]{2,1,0:T(8,128)(2,1)S(1)}, bf16[4,64,1024]{2,1,0:T(8,128)(2,1)S(1)}, u32[]{:S(2)}, u32[]{:S(2)}) collective-permute-start(bf16[4,64,1024]{2,1,0:T(8,128)(2,1)S(1)} %leave_sum.5), channel_id=1, source_target_pairs={{0,2},{1,3},{2,0},{3,1},{4,6},{5,7},{6,4},{7,5},{8,10},{9,11},{10,... | collective-permute-start | bytes 1572872 | tf_op jit(solution)/shard_map/ppermute | solution.py:26
  259.4 16.9 %collective-permute-start.73 = (bf16[4,64,1024]{2,1,0:T(8,128)(2,1)S(1)}, bf16[4,64,1024]{2,1,0:T(8,128)(2,1)S(1)}, u32[]{:S(2)}, u32[]{:S(2)}) collective-permute-start(bf16[4,64,1024]{2,1,0:T(8,128)(2,1)S(1)} %copy-done.64), channel_id=1, source_target_pairs={{0,16},{8,24},{16,0},{24,8},{1,17},{9,25},{17,1},{25,9},{2,18},{10... | collective-permute-start | bytes 1572872 | tf_op jit(solution)/shard_map/ppermute | solution.py:26
  260.1 16.1 %collective-permute-start.76 = (bf16[2,64,1024]{2,1,0:T(8,128)(2,1)S(1)}, bf16[2,64,1024]{2,1,0:T(8,128)(2,1)S(1)}, u32[]{:S(2)}, u32[]{:S(2)}) collective-permute-start(bf16[2,64,1024]{2,1,0:T(8,128)(2,1)S(1)} %append.18.a_ref), channel_id=1, source_target_pairs={{0,16},{8,24},{16,0},{24,8},{1,17},{9,25},{17,1},{25,9},{2,18},{10... | collective-permute-start | bytes 786440 | tf_op jit(solution)/shard_map/ppermute | solution.py:26
  260.9 15.3 %collective-permute-start.75 = (bf16[2,64,1024]{2,1,0:T(8,128)(2,1)S(1)}, bf16[2,64,1024]{2,1,0:T(8,128)(2,1)S(1)}, u32[]{:S(2)}, u32[]{:S(2)}) collective-permute-start(bf16[2,64,1024]{2,1,0:T(8,128)(2,1)S(1)} %get-tuple-element.327), channel_id=1, source_target_pairs={{0,4},{1,5},{2,6},{3,7},{4,0},{5,1},{6,2},{7,3},{8,12},{9,13},{10,... | collective-permute-start | bytes 786440 | tf_op jit(solution)/shard_map/ppermute | solution.py:26
  281.3 13.2 %collective-permute-start.79 = (bf16[256,1024]{1,0:T(8,128)(2,1)S(1)}, bf16[256,1024]{1,0:T(8,128)(2,1)S(1)}, u32[]{:S(2)}, u32[]{:S(2)}) collective-permute-start(bf16[256,1024]{1,0:T(8,128)(2,1)S(1)} %far_sum.9), channel_id=1, source_target_pairs={{0,1},{1,0},{2,3},{3,2},{4,5},{5,4},{6,7},{7,6},{8,9},{9,8},{10,11... | collective-permute-start | bytes 1572872 | tf_op jit(solution)/shard_map/ppermute | solution.py:26
  282.0 18.4 %collective-permute-start.80 = (bf16[2,64,1024]{2,1,0:T(8,128)(2,1)S(1)}, bf16[2,64,1024]{2,1,0:T(8,128)(2,1)S(1)}, u32[]{:S(2)}, u32[]{:S(2)}) collective-permute-start(bf16[2,64,1024]{2,1,0:T(8,128)(2,1)S(1)} %get-tuple-element.349), channel_id=1, source_target_pairs={{0,4},{1,5},{2,6},{3,7},{4,0},{5,1},{6,2},{7,3},{8,12},{9,13},{10,... | collective-permute-start | bytes 786440 | tf_op jit(solution)/shard_map/ppermute | solution.py:26
  283.0 14.3 %collective-permute-start.86 = (bf16[1,64,1024]{2,1,0:T(8,128)(2,1)S(1)}, bf16[1,64,1024]{2,1,0:T(8,128)(2,1)S(1)}, u32[]{:S(2)}, u32[]{:S(2)}) collective-permute-start(bf16[1,64,1024]{2,1,0:T(8,128)(2,1)S(1)} %get-tuple-element.347), channel_id=1, source_target_pairs={{0,1},{1,0},{2,3},{3,2},{4,5},{5,4},{6,7},{7,6},{8,9},{9,8},{10,11... | collective-permute-start | bytes 393224 | tf_op jit(solution)/shard_map/ppermute | solution.py:26
  283.9 24.8 %collective-permute-start.89 = (bf16[4,64,1024]{2,1,0:T(8,128)(2,1)S(1)}, bf16[4,64,1024]{2,1,0:T(8,128)(2,1)S(1)}, u32[]{:S(2)}, u32[]{:S(2)}) collective-permute-start(bf16[4,64,1024]{2,1,0:T(8,128)(2,1)S(1)} %append.23.mine_ref), channel_id=1, source_target_pairs={{0,8},{8,0},{16,24},{24,16},{1,9},{9,1},{17,25},{25,17},{2,10},{10... | collective-permute-start | bytes 1572872 | tf_op jit(solution)/shard_map/ppermute | solution.py:26
  285.2 15.2 %collective-permute-start.81 = (f32[176,128]{1,0:T(8,128)S(1)}, f32[176,128]{1,0:T(8,128)S(1)}, u32[]{:S(2)}, u32[]{:S(2)}) collective-permute-start(f32[176,128]{1,0:T(8,128)S(1)} %small_pack.1), channel_id=1, source_target_pairs={{0,4},{1,5},{2,6},{3,7},{4,0},{5,1},{6,2},{7,3},{8,12},{9,13},{10,... | collective-permute-start | bytes 270344 | tf_op jit(solution)/shard_map/ppermute | solution.py:26
  306.0 8.7 %collective-permute-start.88 = (bf16[4,64,1024]{2,1,0:T(8,128)(2,1)S(1)}, bf16[4,64,1024]{2,1,0:T(8,128)(2,1)S(1)}, u32[]{:S(2)}, u32[]{:S(2)}) collective-permute-start(bf16[4,64,1024]{2,1,0:T(8,128)(2,1)S(1)} %append.22.mine_ref), channel_id=1, source_target_pairs={{0,8},{8,0},{16,24},{24,16},{1,9},{9,1},{17,25},{25,17},{2,10},{10... | collective-permute-start | bytes 1572872 | tf_op jit(solution)/shard_map/ppermute | solution.py:26
  311.4 10.5 %collective-permute-start.85 = (bf16[4,64,1024]{2,1,0:T(8,128)(2,1)S(1)}, bf16[4,64,1024]{2,1,0:T(8,128)(2,1)S(1)}, u32[]{:S(2)}, u32[]{:S(2)}) collective-permute-start(bf16[4,64,1024]{2,1,0:T(8,128)(2,1)S(1)} %append.20.mine_ref), channel_id=1, source_target_pairs={{0,8},{8,0},{16,24},{24,16},{1,9},{9,1},{17,25},{25,17},{2,10},{10... | collective-permute-start | bytes 1572872 | tf_op jit(solution)/shard_map/ppermute | solution.py:26
  (101 other events, 1233.9 us)
